TPU v7x, 32 devices: a whole 2x2x4 slice. The times are simulated.
32 devices in a mesh: ja: 8 (over z, y), ia: 4 (over x, core).
Axes of the slice: x: 2, y: 2, z: 4, core: 2. Of those that a mesh axis runs over, the one named last changes fastest.
Arguments:
- argo_value: float32 [32768, 150], P(('ja', 'ia')), may hold values from -6 to 6
- argo_owner: int32 [32768, 1], P(('ja', 'ia')), may hold values from 0 to 31; in each aligned block of 1024 rows (0 to 1023, 1024 to 2047, ...) at most 96 rows name the same one
- argo_cell: int32 [32768], P(('ja', 'ia')), may hold values from 0 to 8191
- alt_value: float32 [24576], P(('ja', 'ia')), may hold values from -6 to 6
- alt_owner: int32 [24576, 1], P(('ja', 'ia')), may hold values from 0 to 31; in each aligned block of 768 rows (0 to 767, 768 to 1535, ...) at most 72 rows name the same one
- alt_cell: int32 [24576], P(('ja', 'ia')), may hold values from 0 to 8191
- alt_profile: float32 [150], replicated, may hold values from -3 to 3
- land_mask: int32 [128, 2048], P('ja', 'ia'), may hold values 0 or 1
- coef_east: float32 [128, 2048], P('ja', 'ia'), may hold values from 0.05 to 0.24
- coef_north: float32 [128, 2048], P('ja', 'ia'), may hold values from 0.05 to 0.24
- mirror: int32 [2048], P('ia'), may hold values from 0 to 2047, as said below
- vinv: float32 [128, 2, 75, 75], P('ja'), may hold values from -1 to 1
Outputs:
- gradient: float32 [150, 128, 2048], P(None, 'ja', 'ia')
Inputs may be any that keep to these rules, and one draw needn't show every extreme that they name: `argo_owner`: the rows of one device name one owner at most 96 times, a bound that some block reaches. `alt_owner`: the rows of one device name one owner at most 72 times, a bound that some block reaches. mirror[i] is 2047 - i or 2047 - (i XOR 1), and mirror[mirror[i]] = i.
All inputs are finite; a program needn't handle non-finite values. No bound on the sum of `land_mask` on one device may be relied on, other than what follows from the above.
Results may differ from a plain program's by a relative error of at most 0.0001.
Values sent between devices are 32-bit elements; how exact they have to be, the bound alone decides.
No kernel may reach another device: no remote copies, remote signals or barrier semaphores. Data moves between devices by JAX's collectives and lax.ppermute only.
A program may use at most 128 MiB of HBM per device.

v0:
```python
import math

import jax
import jax.numpy as jnp
from jax import lax
from jax.experimental import pallas as pl
from jax.experimental.pallas import tpu as pltpu
from jax.sharding import PartitionSpec as P

ITERS = 3
LEVELS = 75
PAD = 80
LANES = 128
NEAR, FAR, TOP = 0, 1, 2
BF = jnp.bfloat16
F32 = jnp.float32
MIB = 1024 * 1024


def round_up(value, unit):
    return (value + unit - 1) // unit * unit


def split_two(value):
    high = value.astype(BF)
    low = (value - high.astype(F32)).astype(BF)
    return high, low


def mm(left, right):
    return jnp.dot(left, right, preferred_element_type=F32)


def as_column(row):
    return jnp.broadcast_to(row, (8, row.shape[1])).T[:, 0:1]


def slot_ranks(owner_row, cell_row, devices, col_count, row_count, capacity, spread):
    count = owner_row.shape[1]
    owner = owner_row.astype(F32)
    inside = cell_row // col_count
    order = lax.broadcasted_iota(jnp.int32, (1, count), 1).astype(F32)
    key = (owner * float(row_count) + inside.astype(F32)) * float(count) + order
    key_col = as_column(key)
    device = lax.broadcasted_iota(jnp.int32, (devices, 1), 0)
    mine = device == owner_row
    totals = jnp.sum(jnp.where(mine, 1.0, 0.0), axis=1, keepdims=True)
    rank = -jnp.sum(jnp.where(device < owner_row, totals, 0.0), axis=0, keepdims=True)
    for start in range(0, count, 128):
        before = jnp.where(key_col[start : start + 128] < key, 1.0, 0.0)
        rank = rank + jnp.sum(before, axis=0, keepdims=True)
    if spread:
        total = jnp.sum(jnp.where(mine, totals, 0.0), axis=0, keepdims=True)
        offset = owner * 1024.0
        goal = (inside * capacity // row_count).astype(F32) - rank + offset
        goal_col = as_column(goal)
        shift = offset
        for start in range(0, count, 128):
            within = key_col[start : start + 128] <= key
            reached = jnp.where(within, goal_col[start : start + 128], 0.0)
            shift = jnp.maximum(shift, jnp.max(reached, axis=0, keepdims=True))
        rank = rank + jnp.minimum(shift - offset, float(capacity) - total)
    return rank


def table_kernel(
    devices,
    capacity,
    group,
    row_count,
    col_count,
    value_ref,
    owner_ref,
    cell_ref,
    alt_value_ref,
    alt_cell_ref,
    alt_owner_ref,
    message_ref,
    level_ref,
    side_ref,
    hi_ref,
    lo_ref,
    alt_all_ref,
    rank_hot_ref,
    alt_rank_hot_ref,
):
    index = pl.program_id(0)
    n_obs = owner_ref.shape[1]
    n_alt = alt_owner_ref.shape[1]

    @pl.when(index == 0)
    def _():
        slot = lax.broadcasted_iota(jnp.int32, (capacity, 1), 0).astype(F32)
        alt_cell = alt_cell_ref[...].reshape(1, n_alt)
        rank = slot_ranks(
            owner_ref[...], cell_ref[...], devices, col_count, row_count, capacity, True
        )
        rank_hot_ref[...] = jnp.where(slot == rank, 1.0, 0.0).astype(BF)
        rank = slot_ranks(
            alt_owner_ref[...], alt_cell, devices, col_count, row_count, capacity, False
        )
        alt_rank_hot_ref[...] = jnp.where(slot == rank, 1.0, 0.0).astype(BF)
        level_ref[...] = jnp.zeros(level_ref.shape, F32)
        level_ref[0:75, :] = value_ref[0:75, :]
        level_ref[75:76, :] = cell_ref[...].astype(F32) + 1.0
        level_ref[80:128, :] = value_ref[75:123, :]
        for lane_group in range(4):
            level_ref[128 + 32 * lane_group : 155 + 32 * lane_group, :] = value_ref[123:150, :]
        high, low = split_two(level_ref[...].T)
        hi_ref[...] = high
        lo_ref[...] = low
        side_ref[...] = jnp.zeros(side_ref.shape, F32)
        pair = jnp.concatenate(
            [alt_value_ref[...].reshape(1, n_alt), alt_cell.astype(F32) + 1.0], axis=0
        )
        pair_high = pair.astype(BF).astype(F32)
        side_ref[76:78, :] = pair_high
        side_ref[78:80, :] = pair - pair_high
        alt_all_ref[...] = side_ref[...].T.astype(BF)

    per_step = message_ref.shape[0]
    chosen = []
    chosen_alt = []
    for member in range(per_step):
        device = index * per_step + member
        mask = jnp.where(owner_ref[...] == device, 1.0, 0.0).astype(BF)
        chosen.append(rank_hot_ref[...] * mask)
        mask = jnp.where(alt_owner_ref[...] == device, 1.0, 0.0).astype(BF)
        chosen_alt.append(alt_rank_hot_ref[...] * mask)
    chosen = jnp.concatenate(chosen, axis=0)
    chosen_alt = jnp.concatenate(chosen_alt, axis=0)
    table = mm(chosen, hi_ref[...]) + mm(chosen, lo_ref[...])
    lane = lax.broadcasted_iota(jnp.int32, (1, LANES), 1)
    extra = mm(chosen_alt, alt_all_ref[...])
    extra = jnp.where(lane < 78, extra + pltpu.roll(extra, LANES - 2, 1), 0.0)
    extra = jnp.where(lane >= 76, extra, 0.0)
    first = table[:, :LANES] + extra
    message_ref[:, 0:capacity] = first.reshape(per_step, capacity, LANES)
    rest = table[:, LANES:].reshape(per_step, capacity, LANES)
    total = jnp.zeros((per_step, group, LANES), F32)
    for lane_group in range(4):
        low_slot = lane_group * group
        if low_slot >= capacity:
            continue
        piece = rest[:, low_slot : low_slot + group]
        here = (lane // 32 == lane_group).reshape(1, 1, LANES)
        total = jnp.where(here, piece, total)
    message_ref[:, capacity : capacity + group] = total


def send_tables(devices, capacity, group, row_count, col_count, operands):
    n_obs = operands[1].shape[1]
    n_alt = operands[5].shape[1]
    per_step = max(1, 768 // capacity)

    def kernel(*refs):
        table_kernel(devices, capacity, group, row_count, col_count, *refs)

    def whole(array):
        return pl.BlockSpec(array.shape, lambda s: (0,) * len(array.shape))

    return pl.pallas_call(
        kernel,
        grid=(devices // per_step,),
        in_specs=[whole(x) for x in operands],
        out_specs=pl.BlockSpec((per_step, capacity + group, LANES), lambda s: (s, 0, 0)),
        out_shape=jax.ShapeDtypeStruct((devices, capacity + group, LANES), F32),
        scratch_shapes=[
            pltpu.VMEM((2 * LANES, n_obs), F32),
            pltpu.VMEM((LANES, n_alt), F32),
            pltpu.VMEM((n_obs, 2 * LANES), BF),
            pltpu.VMEM((n_obs, 2 * LANES), BF),
            pltpu.VMEM((n_alt, LANES), BF),
            pltpu.VMEM((capacity, n_obs), BF),
            pltpu.VMEM((capacity, n_alt), BF),
        ],
        compiler_params=pltpu.CompilerParams(vmem_limit_bytes=56 * MIB),
        name="send_tables",
    )(*operands)


def column_lane(which, rows, field, east, row):
    return (4 * which + 2 * field + east) * rows + row


def columns_of(which, state_ref, cols):
    rows = state_ref.shape[0]
    lane = lax.broadcasted_iota(jnp.int32, (1, LANES), 1)
    for row in range(rows):
        for field in range(2):
            part = state_ref[row, field * PAD : (field + 1) * PAD, :]
            at = column_lane(which, rows, field, 0, row)
            cols = jnp.where(lane == at, pltpu.roll(part[:, :LANES], at, 1), cols)
            at = column_lane(which, rows, field, 1, row)
            cols = jnp.where(lane == at, pltpu.roll(part[:, -LANES:], at + 1, 1), cols)
    return cols


def pack_row(row_ref, edge_ref):
    edge_ref[0:LEVELS] = row_ref[0:LEVELS]
    edge_ref[LEVELS : 2 * LEVELS] = row_ref[PAD : PAD + LEVELS]
    edge_ref[2 * LEVELS : 2 * LEVELS + 2] = row_ref[LEVELS : LEVELS + 2]


def unpack_row(edge, row_ref, piece):
    row_ref[0:LEVELS, piece] = edge[0:LEVELS]
    row_ref[PAD : PAD + LEVELS, piece] = edge[LEVELS : 2 * LEVELS]
    for at in (LEVELS, PAD + LEVELS):
        row_ref[at : at + PAD - LEVELS, piece] = jnp.zeros((PAD - LEVELS, edge.shape[1]), F32)


def write_edge(is_upper, state_ref, edge_ref):
    pack_row(state_ref.at[jnp.where(is_upper, state_ref.shape[0] - 1, 0)], edge_ref)


def prepare(capacity, alt_capacity, group, col_count, message_ref, sea_ref, left_ref, hot_ref, rows_ref, bound_ref):
    row_count = sea_ref.shape[0]
    devices = message_ref.shape[0]
    block = min(32, devices)
    members = block * 8
    octets = capacity // 8
    alt_octets = (alt_capacity + 7) // 8
    per_group = group // 8
    shift = col_count.bit_length() - 1
    col_iota = lax.broadcasted_iota(jnp.int32, (1, col_count), 1)
    row_iota = lax.broadcasted_iota(jnp.int32, (row_count, 1), 0)

    def chunk(index, start):
        return message_ref[index * block : (index + 1) * block, start : start + 8, :].reshape(
            members, LANES
        )

    def hot_of(cell):
        return jnp.where(((cell - 1) & (col_count - 1)) == col_iota, 1.0, 0.0).astype(BF)

    def rows_of(cell):
        return lax.shift_right_arithmetic(cell - 1, shift)

    sea = jnp.zeros((row_count, col_count), F32)
    count = 0
    for index in range(devices // block):
        tails = [chunk(index, capacity + 8 * part).T for part in range(per_group)]
        for octet in range(octets):
            table = chunk(index, 8 * octet)
            turned = table.T
            tail = tails[octet % per_group]
            begin = 32 * (octet // per_group)
            levels = jnp.concatenate([turned, tail[begin : begin + 32]], axis=0)
            high, low = split_two(levels)
            left_ref[count, :, 0:members] = high
            left_ref[count, :, members : 2 * members] = low
            hot = hot_of(table[:, 75:76].astype(jnp.int32))
            hot_ref[count] = hot
            rows = rows_of(turned[75:76].astype(jnp.int32))
            rows_ref[count] = jnp.broadcast_to(rows, (8, members))
            bound_ref[2 * count] = jnp.min(jnp.where(rows >= 0, rows, row_count))
            bound_ref[2 * count + 1] = jnp.max(rows)
            count += 1
            if octet >= alt_octets:
                continue
            alt_hot = hot_of(table[:, 77:78].astype(jnp.int32))
            alt_rows = rows_of(turned[77:78].astype(jnp.int32))
            weighted = jnp.where(alt_rows == row_iota, turned[76:77], 0.0)
            high, low = split_two(weighted)
            product = mm(jnp.concatenate([high, low], axis=0), alt_hot)
            sea = sea + product[:row_count] + product[row_count:]
    sea_ref[...] = sea


def chosen_rows(number, here, row, span, left_ref, hot_ref):
    pieces = []
    for offset in range(span):
        mask = jnp.where(here == row + offset, 1.0, 0.0).astype(BF)
        pieces.append(left_ref[number] * jnp.concatenate([mask, mask], axis=1))
    hot = hot_ref[number]
    return mm(jnp.concatenate(pieces, axis=0), jnp.concatenate([hot, hot], axis=0))


def outer_forcing(row, is_upper, profile_ref, coast_refs, sea_ref, left_ref, hot_ref, rows_ref, bound_ref, edge_ref):
    row_count, col_count = sea_ref.shape
    last = row_count - 1
    profile = jnp.broadcast_to(profile_ref[...], (2 * PAD, LANES))
    sea = jnp.where(is_upper, sea_ref[last : last + 1, :], sea_ref[0:1, :])
    for start in range(0, col_count, LANES):
        edge_ref[:, start : start + LANES] = profile * sea[:, start : start + LANES]

    def step(number, carry):
        @pl.when((bound_ref[2 * number] <= row) & (row <= bound_ref[2 * number + 1]))
        def _():
            edge_ref[...] += chosen_rows(number, rows_ref[number][0:1], row, 1, left_ref, hot_ref)

        return carry

    lax.fori_loop(0, left_ref.shape[0], step, 0)
    for kind, coast_ref in enumerate(coast_refs):
        coast = jnp.where(is_upper, coast_ref[last : last + 1, :], coast_ref[0:1, :])
        edge_ref[LEVELS + kind : LEVELS + kind + 1, :] = coast.astype(F32)


def all_forcing(profile_ref, coast_refs, sea_ref, left_ref, hot_ref, rows_ref, bound_ref, state):
    row_count, _, col_count = state.shape
    count = left_ref.shape[0]
    for start in range(0, col_count, LANES):
        profile = jnp.broadcast_to(profile_ref[...], (2 * PAD, LANES))
        for row in range(row_count):
            state[row, :, start : start + LANES] = profile * sea_ref[row : row + 1, start : start + LANES]
    span = 3
    batch = math.gcd(count, 4)

    def step(number, carry):
        chunks = [number * batch + member for member in range(batch)]
        least = [bound_ref[2 * chunk] for chunk in chunks]
        most = [bound_ref[2 * chunk + 1] for chunk in chunks]
        runs = [lax.div(most[i] - least[i] + span, span) for i in range(batch)]
        longest = runs[0]
        for run in runs[1:]:
            longest = jnp.maximum(longest, run)

        def run_step(turn, inner):
            for i, chunk in enumerate(chunks):
                begin = least[i] + turn * span
                base = jnp.minimum(begin, row_count - span)
                here = rows_ref[chunk][0:1]
                here = jnp.where(here >= begin, here, -1)
                product = chosen_rows(chunk, here, base, span, left_ref, hot_ref)
                for offset in range(span):
                    state[base + offset] += product[2 * PAD * offset : 2 * PAD * (offset + 1)]
            return inner

        lax.fori_loop(0, longest, run_step, 0)
        return carry

    lax.fori_loop(0, count // batch, step, 0)
    for kind, coast_ref in enumerate(coast_refs):
        coast = coast_ref[...].astype(F32)
        for row in range(row_count):
            state[row, LEVELS + kind : LEVELS + kind + 1, :] = coast[row : row + 1, :]


def half_shapes(row_count, col_count):
    return (
        jax.ShapeDtypeStruct((row_count // 2, 2 * PAD, col_count), F32),
        jax.ShapeDtypeStruct((2 * LEVELS + 2, col_count), F32),
        jax.ShapeDtypeStruct((PAD, LANES), F32),
    )


def in_place(count):
    return [pl.BlockSpec(memory_space=pltpu.SMEM)] + [pl.BlockSpec(memory_space=pltpu.VMEM)] * count


def first_forcing(capacity, alt_capacity, group, flags, message, profile, coast):
    row_count, col_count = coast[0].shape
    devices = message.shape[0]
    members = min(32, devices) * 8
    chunks = capacity // 8 * (devices // min(32, devices))

    def kernel(flag_ref, message_ref, profile_ref, wet, north, east, edge_ref, *refs):
        *outs, row_ref = refs
        prepare(capacity, alt_capacity, group, col_count, message_ref, *outs)
        is_upper = flag_ref[NEAR] > 0
        row = jnp.where(is_upper, row_count - 1, 0)
        outer_forcing(row, is_upper, profile_ref, (wet, north, east), *outs, row_ref)
        pack_row(row_ref, edge_ref)

    return pl.pallas_call(
        kernel,
        in_specs=in_place(5),
        out_shape=(
            half_shapes(row_count, col_count)[1],
            jax.ShapeDtypeStruct((row_count, col_count), F32),
            jax.ShapeDtypeStruct((chunks, 2 * PAD, 2 * members), BF),
            jax.ShapeDtypeStruct((chunks, members, col_count), BF),
            jax.ShapeDtypeStruct((chunks, 8, members), jnp.int32),
            jax.ShapeDtypeStruct((2 * chunks,), jnp.int32),
        ),
        out_specs=[pl.BlockSpec(memory_space=pltpu.VMEM)] * 5
        + [pl.BlockSpec(memory_space=pltpu.SMEM)],
        scratch_shapes=[pltpu.VMEM((2 * PAD, col_count), F32)],
        compiler_params=pltpu.CompilerParams(vmem_limit_bytes=24 * MIB),
        cost_estimate=pl.CostEstimate(
            flops=6_000_000_000, bytes_accessed=8_000_000, transcendentals=0
        ),
        name="forcing_first",
    )(flags, message, profile, *coast)


def rest_forcing(flags, profile, coast, prepared):
    row_count, col_count = coast[0].shape
    half = row_count // 2

    def kernel(flag_ref, profile_ref, wet, north, east, sea, left, hot, rows, bound, state, edge_ref, cols_ref):
        all_forcing(profile_ref, (wet, north, east), sea, left, hot, rows, bound, state)
        cols = jnp.zeros((PAD, LANES), F32)
        for which in (NEAR, FAR):
            first_row = jnp.where(flag_ref[which] > 0, half, 0)
            cols = columns_of(which, state.at[pl.ds(first_row, half)], cols)
        cols_ref[...] = cols
        write_edge(flag_ref[FAR] > 0, state, edge_ref)

    _, edge, cols = half_shapes(row_count, col_count)
    state = jax.ShapeDtypeStruct((row_count, 2 * PAD, col_count), F32)
    return pl.pallas_call(
        kernel,
        in_specs=in_place(8) + [pl.BlockSpec(memory_space=pltpu.SMEM)],
        out_shape=(state, edge, cols),
        compiler_params=pltpu.CompilerParams(vmem_limit_bytes=20 * MIB),
        cost_estimate=pl.CostEstimate(
            flops=6_000_000_000, bytes_accessed=8_000_000, transcendentals=0
        ),
        name="forcing_rest",
    )(flags, profile, *coast, *prepared)


def fold_row(row_ref, mirror_ref, piece, chunk, chunks, rows):
    index = jnp.broadcast_to(mirror_ref[0:1, piece(chunk)], (rows, LANES))
    return jnp.take_along_axis(row_ref[:, piece(chunks - 1 - chunk)], index, axis=1)


def weight_kernel(which, flag_ref, wet_ref, north_ref, east_ref, edge_in, west_in, east_in, mirror_ref, out_ref, fold_ref):
    row_count, col_count = wet_ref.shape
    rows = row_count // 2
    is_upper = flag_ref[which] > 0
    at = pl.multiple_of(jnp.where(is_upper, rows, 0), 8)
    wet = wet_ref[pl.ds(at, rows), :].astype(F32)
    north = north_ref[pl.ds(at, rows), :]
    east = east_ref[pl.ds(at, rows), :]
    chunks = col_count // LANES
    lane = lax.broadcasted_iota(jnp.int32, (1, col_count), 1)
    start = column_lane(which, rows, 0, 1, 0)
    west_cols = west_in[72:80, :].T[start : start + rows]
    start = column_lane(which, rows, 0, 0, 0)
    east_cols = east_in[72:80, :].T[start : start + rows]
    west_wet = jnp.where(lane == 0, west_cols[:, 3:4], pltpu.roll(wet, 1, 1))
    west_coef = jnp.where(lane == 0, west_cols[:, 5:6], pltpu.roll(east, 1, 1))
    east_wet = jnp.where(
        lane == col_count - 1, east_cols[:, 3:4], pltpu.roll(wet, col_count - 1, 1)
    )
    east_w = east * wet * east_wet
    west_w = west_coef * west_wet * wet

    def piece(c):
        return slice(c * LANES, (c + 1) * LANES)

    spare_ref = edge_in.at[2 * LEVELS - 6 : 2 * LEVELS + 2]
    if which == FAR:
        for c in range(chunks):
            fold_ref[:, piece(c)] = fold_row(spare_ref, mirror_ref, piece, c, chunks, 8)
    spare = spare_ref[...]
    last = rows - 1
    inner_wet = jnp.where(
        is_upper, wet_ref[rows - 1 : rows, :], wet_ref[rows : rows + 1, :]
    ).astype(F32)
    above = jnp.where(is_upper, spare[6:7], inner_wet)
    top_w = north[last:] * wet[last:] * above
    if which == FAR:
        fold = 0.5 * (north[last:] + fold_ref[7:8]) * wet[last:] * fold_ref[6:7]
        top_w = jnp.where(flag_ref[TOP] > 0, fold, top_w)
    below = jnp.where(is_upper, north_ref[rows - 1 : rows, :] * inner_wet, spare[7:8] * spare[6:7])
    between = north[:last] * wet[:last] * wet[1:]
    north_w = jnp.concatenate([between, top_w], axis=0)
    south_w = jnp.concatenate([below * wet[0:1], between], axis=0)
    center = 1.0 - (east_w + west_w + north_w + south_w)
    for kind, weight in enumerate((center, east_w, west_w, north_w, south_w)):
        for row in range(rows):
            out_ref[row, kind : kind + 1, :] = weight[row : row + 1]


def edge_weights(which, flags, coast, received, mirror):
    row_count, col_count = coast[0].shape

    def kernel(*refs):
        weight_kernel(which, *refs)

    return pl.pallas_call(
        kernel,
        in_specs=in_place(7),
        out_shape=jax.ShapeDtypeStruct((row_count // 2, 8, col_count), F32),
        scratch_shapes=[pltpu.VMEM((8, col_count), F32)],
        compiler_params=pltpu.CompilerParams(vmem_limit_bytes=16 * MIB),
        name="edge_weights",
    )(flags, *coast, *received, mirror)


def receive_row(which, flag_ref, edge_in, mirror_ref, row_ref):
    levels, col_count = edge_in.shape
    chunks = col_count // LANES
    is_top = flag_ref[TOP] > 0

    def piece(c):
        return slice(c * LANES, (c + 1) * LANES)

    def plain():
        for c in range(chunks):
            unpack_row(edge_in[:, piece(c)], row_ref, piece(c))

    if which == NEAR:
        plain()
        return

    @pl.when(jnp.logical_not(is_top))
    def _():
        plain()

    @pl.when(is_top)
    def _():
        for c in range(chunks):
            unpack_row(
                fold_row(edge_in, mirror_ref, piece, c, chunks, levels), row_ref, piece(c)
            )


def neighbour_rows(is_upper, inner, outer_ref, south_ref, north_ref):
    @pl.when(is_upper)
    def _():
        south_ref[...] = inner[...]
        north_ref[...] = outer_ref[...]

    @pl.when(jnp.logical_not(is_upper))
    def _():
        south_ref[...] = outer_ref[...]
        north_ref[...] = inner[...]


def mix_row(which, row, rows, field, state_ref, south_ref, north_ref, west_in, east_in, coef_ref, right_ref, slot):
    col_count = state_ref.shape[2]
    chunks = col_count // LANES
    lane = lax.broadcasted_iota(jnp.int32, (1, LANES), 1)
    levels = slice(field * PAD, (field + 1) * PAD)

    def piece(chunk):
        return slice(chunk * LANES, (chunk + 1) * LANES)

    west_lane = column_lane(which, rows, field, 1, row)
    east_lane = column_lane(which, rows, field, 0, row)
    centers = [state_ref[row, levels, piece(c)] for c in range(chunks)]
    to_left = [pltpu.roll(c, LANES - 1, 1) for c in centers]
    to_right = [pltpu.roll(c, 1, 1) for c in centers]
    to_right.append(pltpu.roll(west_in[...], LANES - west_lane, 1))
    to_left.append(pltpu.roll(east_in[...], LANES - 1 - east_lane, 1))
    for c in range(chunks):
        south = south_ref[levels, piece(c)]
        north = north_ref[levels, piece(c)]
        east = jnp.where(lane == LANES - 1, to_left[c + 1], to_left[c])
        west = jnp.where(lane == 0, to_right[c - 1], to_right[c])

        def coef(kind):
            return coef_ref[row, kind : kind + 1, piece(c)]

        mixed = (
            coef(0) * centers[c]
            + coef(1) * east
            + coef(2) * west
            + coef(3) * north
            + coef(4) * south
        )
        high, low = split_two(mixed)
        right_ref[slot, 0:PAD, piece(c)] = high
        right_ref[slot, PAD : 2 * PAD, piece(c)] = low
        right_ref[slot, 2 * PAD : 3 * PAD, piece(c)] = high


def sweep_rows(which, rows, units, state_ref, south_ref, north_ref, west_in, east_in, coef_ref, matrix_ref, right_ref, emit):
    slots = right_ref.shape[0]
    right_ref[:, 3 * PAD :, :] = jnp.zeros((slots,) + (256 - 3 * PAD, right_ref.shape[2]), BF)

    def product(number):
        row, field = units[number]
        emit(number, row, field, mm(matrix_ref[field, row], right_ref[number % slots]))

    for number, (row, field) in enumerate(units):
        south = state_ref.at[row - 1] if row > 0 else south_ref
        north = state_ref.at[row + 1] if row < rows - 1 else north_ref
        mix_row(which, row, rows, field, state_ref, south, north, west_in, east_in, coef_ref, right_ref, number % slots)
        if number > 0:
            product(number - 1)
    product(len(units) - 1)


def diffuse(which, flags, state, other, received, mirror, coef, matrix, *far_cols):
    rows = coef.shape[0]
    col_count = state.shape[2]

    def kernel(flag_ref, state_ref, other_ref, edge_in, west_in, east_in, mirror_ref, coef_ref, matrix_ref, *refs):
        out_ref, edge_ref, cols_ref, south_ref, north_ref, outer_ref, right_ref = refs[-7:]
        is_upper = flag_ref[which] > 0
        if state.shape[0] > rows:
            state_ref = state_ref.at[pl.ds(jnp.where(is_upper, rows, 0), rows)]
            inner = other_ref.at[jnp.where(is_upper, rows - 1, rows)]
        else:
            inner = other_ref.at[jnp.where(is_upper, rows - 1, 0)]
        receive_row(which, flag_ref, edge_in, mirror_ref, outer_ref)
        neighbour_rows(is_upper, inner, outer_ref, south_ref, north_ref)

        def emit(number, row, field, result):
            out_ref[row, field * PAD : (field + 1) * PAD] = result

        units = [(row, field) for row in range(rows) for field in range(2)]
        sweep_rows(which, rows, units, state_ref, south_ref, north_ref, west_in, east_in, coef_ref, matrix_ref, right_ref, emit)
        write_edge(is_upper, out_ref, edge_ref)
        old_cols = refs[0][...] if which == NEAR else jnp.zeros((PAD, LANES), F32)
        cols_ref[...] = columns_of(which, out_ref, old_cols)

    return pl.pallas_call(
        kernel,
        in_specs=in_place(8 + len(far_cols)),
        out_shape=half_shapes(2 * rows, col_count),
        scratch_shapes=[pltpu.VMEM((2 * PAD, col_count), F32)] * 3
        + [pltpu.VMEM((4, 256, col_count), BF)],
        compiler_params=pltpu.CompilerParams(vmem_limit_bytes=16 * MIB),
        cost_estimate=pl.CostEstimate(
            flops=3_000_000_000, bytes_accessed=8_000_000, transcendentals=0
        ),
        name="diffusion_" + ("near", "far")[which],
    )(flags, state, other, *received, mirror, coef, matrix, *far_cols)


def store_block(results, out_ref, stage_ref, sem, at, field):
    rows = stage_ref.shape[2]
    stage_ref[field] = jnp.swapaxes(jnp.stack(results), 0, 1)[:LEVELS]
    copy = pltpu.make_async_copy(
        stage_ref.at[field],
        out_ref.at[pl.ds(field * LEVELS, LEVELS), pl.ds(at, rows), :],
        sem.at[field],
    )
    copy.start()
    return copy


def last_inner(flags, near, far, near_edge, near_sides, far_sides, mirror, near_fixed, far_fixed, mask):
    rows, _, col_count = near.shape

    def kernel(flag_ref, near_ref, far_ref, edge_in, near_west, near_east, far_west, far_east, mirror_ref, near_coef, near_matrix, far_coef, far_matrix, mask_ref, out_ref, done_ref, south_ref, north_ref, outer_ref, right_ref, stage_ref, sem):
        is_upper = flag_ref[NEAR] > 0
        at = pl.multiple_of(jnp.where(is_upper, rows, 0), 8)
        wet = mask_ref[pl.ds(at, rows), :].astype(F32)
        far_at = pl.multiple_of(rows - at, 8)
        far_wet = mask_ref[pl.ds(far_at, rows), :].astype(F32)
        last = rows - 1
        far_inner = far_ref.at[jnp.where(is_upper, last, 0)]
        receive_row(NEAR, flag_ref, edge_in, mirror_ref, outer_ref)
        neighbour_rows(is_upper, far_inner, outer_ref, south_ref, north_ref)
        copies = []
        for field in range(2):
            results = []

            def emit(number, row, field, result):
                results.append(result * wet[row : row + 1])

            units = [(row, field) for row in range(rows)]
            sweep_rows(NEAR, rows, units, near_ref, south_ref, north_ref, near_west, near_east, near_coef, near_matrix, right_ref, emit)
            copies.append(store_block(results, out_ref, stage_ref, sem, at, field))
        edge = jnp.where(is_upper, last, 0)
        near_inner = near_ref.at[jnp.where(is_upper, 0, last)]

        @pl.when(is_upper)
        def _():
            south_ref[...] = far_ref[last - 1]
            north_ref[...] = near_inner[...]

        @pl.when(jnp.logical_not(is_upper))
        def _():
            south_ref[...] = near_inner[...]
            north_ref[...] = far_ref[1]

        def keep(number, row, field, result):
            done_ref[row, field * PAD : (field + 1) * PAD] = result * far_wet[row : row + 1]

        units = [(row, field) for row in range(1, last) for field in range(2)]
        sweep_rows(FAR, rows, units, far_ref, south_ref, north_ref, far_west, far_east, far_coef, far_matrix, right_ref, keep)
        edge_wet = jnp.where(is_upper, far_wet[last:], far_wet[0:1])
        for field in range(2):
            mix_row(FAR, edge, rows, field, far_ref, south_ref, north_ref, far_west, far_east, far_coef, right_ref, field)
        for field in range(2):
            result = mm(far_matrix[field, edge], right_ref[field])
            done_ref[edge, field * PAD : (field + 1) * PAD] = result * edge_wet
        for copy in copies:
            copy.wait()

    return pl.pallas_call(
        kernel,
        in_specs=in_place(13),
        out_specs=[pl.BlockSpec(memory_space=pl.ANY), pl.BlockSpec(memory_space=pltpu.VMEM)],
        out_shape=(
            jax.ShapeDtypeStruct((2 * LEVELS, 2 * rows, col_count), F32),
            jax.ShapeDtypeStruct((rows, 2 * PAD, col_count), F32),
        ),
        scratch_shapes=[pltpu.VMEM((2 * PAD, col_count), F32)] * 3
        + [
            pltpu.VMEM((4, 256, col_count), BF),
            pltpu.VMEM((2, LEVELS, rows, col_count), F32),
            pltpu.SemaphoreType.DMA((2,)),
        ],
        compiler_params=pltpu.CompilerParams(vmem_limit_bytes=20 * MIB),
        cost_estimate=pl.CostEstimate(
            flops=6_000_000_000, bytes_accessed=16_000_000, transcendentals=0
        ),
        name="last_inner",
    )(flags, near, far, near_edge, *near_sides, *far_sides, mirror, *near_fixed, *far_fixed, mask)


def last_outer(flags, far, far_edge, far_sides, mirror, far_fixed, mask, done, target):
    rows, _, col_count = far.shape

    def kernel(flag_ref, far_ref, edge_in, west_in, east_in, mirror_ref, coef_ref, matrix_ref, mask_ref, done_ref, target_ref, out_ref, south_ref, north_ref, outer_ref, right_ref, stage_ref, sem):
        is_upper = flag_ref[FAR] > 0
        at = pl.multiple_of(jnp.where(is_upper, rows, 0), 8)
        wet = mask_ref[pl.ds(at, rows), :].astype(F32)
        last = rows - 1
        row = jnp.where(is_upper, last, 0)
        row_wet = jnp.where(is_upper, wet[last:], wet[0:1])
        receive_row(FAR, flag_ref, edge_in, mirror_ref, outer_ref)
        neighbour_rows(is_upper, far_ref.at[jnp.where(is_upper, last - 1, 1)], outer_ref, south_ref, north_ref)
        right_ref[:, 3 * PAD :, :] = jnp.zeros((2, 256 - 3 * PAD, col_count), BF)
        for field in range(2):
            mix_row(FAR, row, rows, field, far_ref, south_ref, north_ref, west_in, east_in, coef_ref, right_ref, field)
        copies = []
        for field in range(2):
            result = mm(matrix_ref[field, row], right_ref[field]) * row_wet
            done_field = [done_ref[r, field * PAD : (field + 1) * PAD] for r in range(rows)]
            done_field[0] = jnp.where(is_upper, done_field[0], result)
            done_field[last] = jnp.where(is_upper, result, done_field[last])
            copies.append(store_block(done_field, out_ref, stage_ref, sem, at, field))
        for copy in copies:
            copy.wait()

    operands = [flags, far, far_edge, *far_sides, mirror, *far_fixed, mask, done, target]
    return pl.pallas_call(
        kernel,
        in_specs=in_place(9) + [pl.BlockSpec(memory_space=pl.ANY)],
        out_specs=pl.BlockSpec(memory_space=pl.ANY),
        out_shape=jax.ShapeDtypeStruct((2 * LEVELS, 2 * rows, col_count), F32),
        input_output_aliases={len(operands) - 1: 0},
        scratch_shapes=[pltpu.VMEM((2 * PAD, col_count), F32)] * 3
        + [
            pltpu.VMEM((2, 256, col_count), BF),
            pltpu.VMEM((2, LEVELS, rows, col_count), F32),
            pltpu.SemaphoreType.DMA((2,)),
        ],
        compiler_params=pltpu.CompilerParams(vmem_limit_bytes=20 * MIB),
        name="last_outer",
    )(*operands)


def mixing_matrices(vinv):
    turned = jnp.transpose(vinv, (1, 0, 3, 2))
    turned = jnp.pad(turned, ((0, 0), (0, 0), (0, PAD - LEVELS), (0, PAD - LEVELS)))
    high = lax.reduce_precision(turned, 8, 7)
    low = (turned - high).astype(BF)
    high = high.astype(BF)
    rest = jnp.zeros(high.shape[:3] + (256 - 3 * PAD,), BF)
    return jnp.concatenate([high, high, low, rest], axis=3)


def body(
    argo_value,
    argo_owner,
    argo_cell,
    alt_value,
    alt_owner,
    alt_cell,
    alt_profile,
    land_mask,
    coef_east,
    coef_north,
    mirror,
    vinv,
):
    row_count, col_count = land_mask.shape
    count_ja = lax.axis_size("ja")
    count_ia = lax.axis_size("ia")
    devices = count_ja * count_ia
    capacity = round_up(3 * argo_value.shape[0] // devices, 8)
    group = round_up(capacity // 4, 8)
    message = send_tables(
        devices,
        capacity,
        group,
        row_count,
        col_count,
        (
            argo_value.T,
            argo_owner.reshape(1, -1),
            argo_cell.reshape(1, -1),
            alt_value,
            alt_cell,
            alt_owner.reshape(1, -1),
        ),
    )
    message, ja_index = lax.optimization_barrier((message, lax.axis_index("ja")))
    message = lax.all_to_all(message, ("ja", "ia"), split_axis=0, concat_axis=0, tiled=True)

    ia_index = lax.axis_index("ia")
    is_top = (ja_index == count_ja - 1).astype(jnp.int32)
    parity = ja_index % 2
    flags = jnp.stack([1 - parity, parity, is_top]).astype(jnp.int32)
    fold_index = mirror - (count_ia - 1 - ia_index) * col_count
    mirror_lane = jnp.broadcast_to((fold_index % LANES)[None, :], (8, col_count))
    matrices = mixing_matrices(vinv)
    profile = jnp.pad(alt_profile.reshape(2, LEVELS, 1), ((0, 0), (0, PAD - LEVELS), (0, 0)))
    profile = profile.reshape(2 * PAD, 1)
    alt_capacity = max(2, 3 * alt_value.shape[0] // devices)
    coast = (land_mask, coef_north, coef_east)
    rows = row_count // 2
    lower = [matrices[:, :rows], matrices[:, rows:]]
    odd_device = parity == 1
    half_matrices = [
        jnp.where(odd_device, lower[0], lower[1]),
        jnp.where(odd_device, lower[1], lower[0]),
    ]

    ring_east = [(i, (i + 1) % count_ia) for i in range(count_ia)]
    ring_west = [((i + 1) % count_ia, i) for i in range(count_ia)]
    even_swap = []
    odd_swap = []
    for ja in range(count_ja):
        for ia in range(count_ia):
            here = ja * count_ia + ia
            even_swap.append((here, (ja ^ 1) * count_ia + ia))
            if ja == count_ja - 1:
                odd_swap.append((here, ja * count_ia + count_ia - 1 - ia))
            elif ja > 0:
                odd_swap.append((here, (((ja - 1) ^ 1) + 1) * count_ia + ia))
    swaps = (even_swap, odd_swap)

    def swap(which, edge):
        return lax.ppermute(edge, ("ja", "ia"), swaps[which])

    def pass_columns(cols):
        return lax.ppermute(cols, "ia", ring_east), lax.ppermute(cols, "ia", ring_west)

    near_edge, *prepared = first_forcing(
        capacity, alt_capacity, group, flags, message, profile, coast
    )
    near_edge = swap(NEAR, near_edge)
    state, far_edge, cols = rest_forcing(flags, profile, coast, prepared)
    near = far = state
    sides = pass_columns(cols)
    far_edge = swap(FAR, far_edge)
    near_coef = edge_weights(NEAR, flags, coast, (near_edge, *sides), mirror_lane)
    far_coef = edge_weights(FAR, flags, coast, (far_edge, *sides), mirror_lane)
    near_fixed = (mirror_lane, near_coef, half_matrices[NEAR])
    far_fixed = (mirror_lane, far_coef, half_matrices[FAR])
    for sweep in range(ITERS - 1):
        new_near, new_edge, cols = diffuse(
            NEAR, flags, near, far, (near_edge, *sides), *near_fixed, cols
        )
        near_edge = swap(NEAR, new_edge)
        sides = pass_columns(cols)
        far, new_edge, cols = diffuse(FAR, flags, far, near, (far_edge, *sides), *far_fixed)
        far_edge = swap(FAR, new_edge)
        near = new_near
    last_sides = pass_columns(cols)
    output, done = last_inner(
        flags, near, far, near_edge, sides, last_sides, mirror_lane, near_fixed[1:], far_fixed[1:], land_mask
    )
    return last_outer(
        flags, far, far_edge, last_sides, mirror_lane, far_fixed[1:], land_mask, done, output
    )


def solution(mesh):
    in_specs = (
        P(("ja", "ia"), None),
        P(("ja", "ia"), None),
        P(("ja", "ia")),
        P(("ja", "ia")),
        P(("ja", "ia"), None),
        P(("ja", "ia")),
        P(),
        P("ja", "ia"),
        P("ja", "ia"),
        P("ja", "ia"),
        P("ia"),
        P("ja", None, None, None),
    )
    out_specs = P(None, "ja", "ia")
    return jax.shard_map(body, mesh=mesh, in_specs=in_specs, out_specs=out_specs, check_vma=False)
```

profile of v0, /device:TPU:5, one launch (start us, length us, event | category | flops | bytes accessed | tf_op | source)
XLA Modules:
  0.0 124.2 jit_solution(1490928326621726379)
XLA Ops:
  0.0 9.8 %send_tables.1 = f32[32,120,128]{2,1,0:T(8,128)} custom-call(f32[150,1024]{1,0:T(8,128)} %bitcast.11, s32[1,1024]{1,0:T(1,128)} %bitcast.12, s32[1,1024]{1,0:T(1,128)} %bitcast.13, f32[768]{0:T(1024)} %refs_3_.3, s32[768]{0:T(1024)} %refs_4_.1, s32[1,768]{1,0:T(1,128)} %bitcast.14), custom_call_target="tpu_custom_call" | custom-call | tf_op jit(solution)/shard_map/send_tables/pallas_call | solution.py:162
  9.8 0.0 copy-start.4
  9.8 6.4 %all-to-all-start = ((f32[32,120,128]{2,1,0:T(8,128)}), f32[32,120,128]{2,1,0:T(8,128)S(1)}, u32[]{:S(2)}, u32[]{:S(2)}) async-start(f32[32,120,128]{2,1,0:T(8,128)} %send_tables.1), calls=%async_computation | async-start | bytes 3932160 | tf_op jit(solution)/shard_map/all_to_all | solution.py:791
  16.2 0.0 copy-done.4
  16.2 0.1 reshape.19
  16.3 0.1 reshape.22.profile_ref
  16.5 1.7 %copy.17 = f32[16,2,75,75]{2,3,0,1:T(8,128)S(1)} copy(f32[16,2,75,75]{3,1,2,0:T(2,128)} %param.23) | data formatting | bytes 1440000 | tf_op args[11]
  18.2 0.1 pad.13.clone
  18.3 0.1 pad_add_fusion.flag_ref.refs_0_
  18.3 0.2 reduce-precision_convert_fusion
  18.6 0.0 copy-start
  18.6 0.0 copy-start.1
  18.6 0.0 copy-start.2
  18.6 0.9 maximum_maximum_fusion
  19.5 0.1 broadcast_select_fusion
  19.6 41.7 %all-to-all-done.message_ref = f32[32,120,128]{2,1,0:T(8,128)S(1)} async-done(((f32[32,120,128]{2,1,0:T(8,128)}), f32[32,120,128]{2,1,0:T(8,128)S(1)}, u32[]{:S(2)}, u32[]{:S(2)}) %all-to-all-start) | async-done | bytes 1966112 | tf_op jit(solution)/shard_map/all_to_all | solution.py:791
  61.3 0.0 copy-done
  61.3 0.0 copy-done.1
  61.3 0.0 copy-done.2
  61.3 4.6 %forcing_first.1 = (f32[152,512]{1,0:T(8,128)S(1)}, f32[16,512]{1,0:T(8,128)S(1)}, bf16[12,160,512]{2,1,0:T(8,128)(2,1)S(1)}, bf16[12,256,512]{2,1,0:T(8,128)(2,...) custom-call(s32[3]{0:T(128)S(1)} %pad_add_fusion.flag_ref.refs_0_, f32[32,120,128]{2,1,0:T(8,128)S(1)} %all-to-all-done.message_ref, ...), custom_call_target="tpu_custom_call" | custom-call | flops 6000000000 | bytes 8000000 | tf_op jit(solution)/shard_map/forcing_first/pallas_call | solution.py:366
  65.9 0.5 collective-permute-start.1
  66.4 0.0 copy-start.3
  66.4 5.7 %forcing_rest.1 = (f32[16,160,512]{2,1,0:T(8,128)S(1)}, f32[152,512]{1,0:T(8,128)S(1)}, f32[80,128]{1,0:T(8,128)S(1)}) custom-call(s32[3]{0:T(128)S(1)} %pad_add_fusion.flag_ref.refs_0_, f32[160,1]{1,0:T(8,128)S(1)} %reshape.22.profile_ref, s32[16,512]{1,0:T(8,128)S(1)} %copy-done, f32[16,512]{1,0:T(8,128)S(1)} %copy-done.1, f32[16,512]{1,0:T(8,128)S(1)} %copy-done.2, ...), custom_call_target="tpu_custom_call" | custom-call | flops 6000000000 | bytes 8000000 | tf_op jit(solution)/shard_map/forcing_rest/pallas_call | solution.py:403
  72.1 1.2 collective-permute-start.3
  73.3 1.1 collective-permute-start.2
  74.3 0.0 copy-done.3
  74.4 1.9 %collective-permute-start = (f32[152,512]{1,0:T(8,128)S(1)}, f32[152,512]{1,0:T(8,128)S(1)}, u32[]{:S(2)}, u32[]{:S(2)}) collective-permute-start(f32[152,512]{1,0:T(8,128)S(1)} %get-tuple-element.38), channel_id=1, source_target_pairs={{4,8},{5,9},{6,10},{7,11},{8,4},{9,5},{10,6},{11,7},{12,16},{13,17... | collective-permute-start | bytes 933896 | tf_op jit(solution)/shard_map/ppermute | solution.py:827
  76.3 0.0 collective-permute-done.3.refs_6_.east_in
  76.3 0.7 collective-permute-done.2.refs_5_.west_in
  77.0 0.0 collective-permute-done.1.refs_4_.edge_in
  77.0 0.7 edge_weights.2.coef_ref.near_coef
  77.7 3.7 %diffusion_near.2 = (f32[8,160,512]{2,1,0:T(8,128)S(1)}, f32[152,512]{1,0:T(8,128)S(1)}, f32[80,128]{1,0:T(8,128)S(1)}) custom-call(s32[3]{0:T(128)S(1)} %pad_add_fusion.flag_ref.refs_0_, f32[16,160,512]{2,1,0:T(8,128)S(1)} %get-tuple-element.37.state_ref.other_ref, f32[16,160,512]{2,1,0:T(8,128)S(1)} %get-tuple-element.37.state_ref.other_ref, ...), custom_call_target="tpu_custom_call" | custom-call | flops 3000000000 | bytes 8000000 | tf_op jit(solution)/shard_map/diffusion_near/pallas_call | solution.py:604
  81.4 2.8 %collective-permute-start.5 = (f32[80,128]{1,0:T(8,128)S(1)}, f32[80,128]{1,0:T(8,128)S(1)}, u32[]{:S(2)}, u32[]{:S(2)}) collective-permute-start(f32[80,128]{1,0:T(8,128)S(1)} %get-tuple-element.41), channel_id=1, source_target_pairs={{1,0},{2,1},{3,2},{0,3},{5,4},{6,5},{7,6},{4,7},{9,8},{10,9},{11,1... | collective-permute-start | bytes 122888 | tf_op jit(solution)/shard_map/ppermute | solution.py:830
  84.1 0.0 collective-permute-start.4
  84.1 2.4 %collective-permute-start.7 = (f32[152,512]{1,0:T(8,128)S(1)}, f32[152,512]{1,0:T(8,128)S(1)}, u32[]{:S(2)}, u32[]{:S(2)}) collective-permute-start(f32[152,512]{1,0:T(8,128)S(1)} %get-tuple-element.45), channel_id=1, source_target_pairs={{0,4},{1,5},{2,6},{3,7},{4,0},{5,1},{6,2},{7,3},{8,12},{9,13},{10,... | collective-permute-start | bytes 933896 | tf_op jit(solution)/shard_map/ppermute | solution.py:827
  86.5 0.0 collective-permute-done.refs_4_.edge_in
  86.5 0.7 edge_weights.3.coef_ref.far_coef
  87.2 0.0 collective-permute-done.5.east_in
  87.3 0.0 collective-permute-done.4.west_in
  87.3 3.5 %diffusion_far.2 = (f32[8,160,512]{2,1,0:T(8,128)S(1)}, f32[152,512]{1,0:T(8,128)S(1)}, f32[80,128]{1,0:T(8,128)S(1)}) custom-call(s32[3]{0:T(128)S(1)} %pad_add_fusion.flag_ref.refs_0_, f32[16,160,512]{2,1,0:T(8,128)S(1)} %get-tuple-element.37.state_ref.other_ref, f32[16,160,512]{2,1,0:T(8,128)S(1)} %get-tuple-element.37.state_ref.other_ref, ...), custom_call_target="tpu_custom_call" | custom-call | flops 3000000000 | bytes 8000000 | tf_op jit(solution)/shard_map/diffusion_far/pallas_call | solution.py:604
  90.8 2.1 %collective-permute-start.6 = (f32[152,512]{1,0:T(8,128)S(1)}, f32[152,512]{1,0:T(8,128)S(1)}, u32[]{:S(2)}, u32[]{:S(2)}) collective-permute-start(f32[152,512]{1,0:T(8,128)S(1)} %get-tuple-element.44), channel_id=1, source_target_pairs={{4,8},{5,9},{6,10},{7,11},{8,4},{9,5},{10,6},{11,7},{12,16},{13,17... | collective-permute-start | bytes 933896 | tf_op jit(solution)/shard_map/ppermute | solution.py:827
  92.9 0.9 collective-permute-done.7.edge_in
  93.8 3.5 %diffusion_near.3 = (f32[8,160,512]{2,1,0:T(8,128)S(1)}, f32[152,512]{1,0:T(8,128)S(1)}, f32[80,128]{1,0:T(8,128)S(1)}) custom-call(s32[3]{0:T(128)S(1)} %pad_add_fusion.flag_ref.refs_0_, f32[8,160,512]{2,1,0:T(8,128)S(1)} %get-tuple-element.43.state_ref.other_ref, f32[8,160,512]{2,1,0:T(8,128)S(1)} %get-tuple-element.42.other_ref.state_ref, ...), custom_call_target="tpu_custom_call" | custom-call | flops 3000000000 | bytes 8000000 | tf_op jit(solution)/shard_map/diffusion_near/pallas_call | solution.py:604
  97.3 2.2 %collective-permute-start.9 = (f32[80,128]{1,0:T(8,128)S(1)}, f32[80,128]{1,0:T(8,128)S(1)}, u32[]{:S(2)}, u32[]{:S(2)}) collective-permute-start(f32[80,128]{1,0:T(8,128)S(1)} %get-tuple-element.47), channel_id=1, source_target_pairs={{1,0},{2,1},{3,2},{0,3},{5,4},{6,5},{7,6},{4,7},{9,8},{10,9},{11,1... | collective-permute-start | bytes 122888 | tf_op jit(solution)/shard_map/ppermute | solution.py:830
  99.5 0.1 collective-permute-start.8
  99.6 0.7 collective-permute-start.13
  100.3 1.4 %collective-permute-done.6.edge_in = f32[152,512]{1,0:T(8,128)S(1)} collective-permute-done((f32[152,512]{1,0:T(8,128)S(1)}, f32[152,512]{1,0:T(8,128)S(1)}, u32[]{:S(2)}, u32[]{:S(2)}) %collective-permute-start.6) | collective-permute-done | bytes 311328 | tf_op jit(solution)/shard_map/ppermute | solution.py:827
  101.7 0.0 collective-permute-done.9.east_in.near_east
  101.7 0.0 collective-permute-done.8.west_in.near_west
  101.7 3.5 %diffusion_far.3 = (f32[8,160,512]{2,1,0:T(8,128)S(1)}, f32[152,512]{1,0:T(8,128)S(1)}, f32[80,128]{1,0:T(8,128)S(1)}) custom-call(s32[3]{0:T(128)S(1)} %pad_add_fusion.flag_ref.refs_0_, f32[8,160,512]{2,1,0:T(8,128)S(1)} %get-tuple-element.42.other_ref.state_ref, f32[8,160,512]{2,1,0:T(8,128)S(1)} %get-tuple-element.43.state_ref.other_ref, ...), custom_call_target="tpu_custom_call" | custom-call | flops 3000000000 | bytes 8000000 | tf_op jit(solution)/shard_map/diffusion_far/pallas_call | solution.py:604
  105.2 1.8 %collective-permute-start.12 = (f32[80,128]{1,0:T(8,128)S(1)}, f32[80,128]{1,0:T(8,128)S(1)}, u32[]{:S(2)}, u32[]{:S(2)}) collective-permute-start(f32[80,128]{1,0:T(8,128)S(1)} %get-tuple-element.50), channel_id=1, source_target_pairs={{1,0},{2,1},{3,2},{0,3},{5,4},{6,5},{7,6},{4,7},{9,8},{10,9},{11,1... | collective-permute-start | bytes 122888 | tf_op jit(solution)/shard_map/ppermute | solution.py:830
  107.0 2.4 %collective-permute-start.11 = (f32[80,128]{1,0:T(8,128)S(1)}, f32[80,128]{1,0:T(8,128)S(1)}, u32[]{:S(2)}, u32[]{:S(2)}) collective-permute-start(f32[80,128]{1,0:T(8,128)S(1)} %get-tuple-element.50), channel_id=1, source_target_pairs={{0,1},{1,2},{2,3},{3,0},{4,5},{5,6},{6,7},{7,4},{8,9},{9,10},{10,1... | collective-permute-start | bytes 122888 | tf_op jit(solution)/shard_map/ppermute | solution.py:830
  109.3 1.9 %collective-permute-start.10 = (f32[152,512]{1,0:T(8,128)S(1)}, f32[152,512]{1,0:T(8,128)S(1)}, u32[]{:S(2)}, u32[]{:S(2)}) collective-permute-start(f32[152,512]{1,0:T(8,128)S(1)} %get-tuple-element.49), channel_id=1, source_target_pairs={{4,8},{5,9},{6,10},{7,11},{8,4},{9,5},{10,6},{11,7},{12,16},{13,17... | collective-permute-start | bytes 933896 | tf_op jit(solution)/shard_map/ppermute | solution.py:827
  111.3 0.0 collective-permute-done.12.far_east.east_in
  111.3 0.0 collective-permute-done.11.far_west.west_in
  111.3 0.0 collective-permute-done.13.edge_in
  111.3 6.3 %last_inner.1 = (f32[150,16,512]{2,1,0:T(8,128)}, f32[8,160,512]{2,1,0:T(8,128)S(1)}) custom-call(s32[3]{0:T(128)S(1)} %pad_add_fusion.flag_ref.refs_0_, f32[8,160,512]{2,1,0:T(8,128)S(1)} %get-tuple-element.51.near_ref, f32[8,160,512]{2,1,0:T(8,128)S(1)} %get-tuple-element.48.far_ref, f32[152,512]{1,0:T(8,128)S(1)} %collective-permute-done.13.edge_in, ...), custom_call_target="tpu_custom_call" | custom-call | flops 6000000000 | bytes 16000000 | tf_op jit(solution)/shard_map/last_inner/pallas_call | solution.py:680
  117.6 3.8 %collective-permute-done.10.edge_in = f32[152,512]{1,0:T(8,128)S(1)} collective-permute-done((f32[152,512]{1,0:T(8,128)S(1)}, f32[152,512]{1,0:T(8,128)S(1)}, u32[]{:S(2)}, u32[]{:S(2)}) %collective-permute-start.10) | collective-permute-done | bytes 311328 | tf_op jit(solution)/shard_map/ppermute | solution.py:827
  121.4 2.7 %last_outer.1 = f32[150,16,512]{2,1,0:T(8,128)} custom-call(s32[3]{0:T(128)S(1)} %pad_add_fusion.flag_ref.refs_0_, f32[8,160,512]{2,1,0:T(8,128)S(1)} %get-tuple-element.48.far_ref, f32[152,512]{1,0:T(8,128)S(1)} %collective-permute-done.10.edge_in, f32[80,128]{1,0:T(8,128)S(1)} %collective-permute-done.11.far_west.west_in, ...), custom_call_target="tpu_custom_call", output_to_operand_aliasing={{}: (10, {})} | custom-call | tf_op jit(solution)/shard_map/last_outer/pallas_call | solution.py:728
  (4 shorter events, 0.0 us)
Async XLA Ops:
  9.8 6.4 %copy-start.4 = (f32[150]{0:T(256)S(1)}, f32[150]{0:T(256)}, u32[]{:S(2)}) copy-start(f32[150]{0:T(256)} %param.18) | copy-start | bytes 1804
  9.8 51.5 %all-to-all-start = ((f32[32,120,128]{2,1,0:T(8,128)}), f32[32,120,128]{2,1,0:T(8,128)S(1)}, u32[]{:S(2)}, u32[]{:S(2)}) async-start(f32[32,120,128]{2,1,0:T(8,128)} %send_tables.1), calls=%async_computation | async-start | bytes 3932160 | tf_op jit(solution)/shard_map/all_to_all | solution.py:791
  18.6 42.7 %copy-start = (s32[16,512]{1,0:T(8,128)S(1)}, s32[16,512]{1,0:T(8,128)}, u32[]{:S(2)}) copy-start(s32[16,512]{1,0:T(8,128)} %mask_ref.3) | copy-start | bytes 98308
  18.6 42.7 %copy-start.1 = (f32[16,512]{1,0:T(8,128)S(1)}, f32[16,512]{1,0:T(8,128)}, u32[]{:S(2)}) copy-start(f32[16,512]{1,0:T(8,128)} %refs_2_.3) | copy-start | bytes 98308
  18.6 42.7 %copy-start.2 = (f32[16,512]{1,0:T(8,128)S(1)}, f32[16,512]{1,0:T(8,128)}, u32[]{:S(2)}) copy-start(f32[16,512]{1,0:T(8,128)} %refs_3_.5) | copy-start | bytes 98308
  65.9 11.1 %collective-permute-start.1 = (f32[152,512]{1,0:T(8,128)S(1)}, f32[152,512]{1,0:T(8,128)S(1)}, u32[]{:S(2)}, u32[]{:S(2)}) collective-permute-start(f32[152,512]{1,0:T(8,128)S(1)} %get-tuple-element.39), channel_id=1, source_target_pairs={{0,4},{1,5},{2,6},{3,7},{4,0},{5,1},{6,2},{7,3},{8,12},{9,13},{10,... | collective-permute-start | bytes 933896 | tf_op jit(solution)/shard_map/ppermute | solution.py:827
  66.4 8.0 %copy-start.3 = (s32[512]{0:T(512)S(1)}, s32[512]{0:T(512)}, u32[]{:S(2)}) copy-start(s32[512]{0:T(512)} %param.22) | copy-start | bytes 6148
  72.1 4.2 %collective-permute-start.3 = (f32[80,128]{1,0:T(8,128)S(1)}, f32[80,128]{1,0:T(8,128)S(1)}, u32[]{:S(2)}, u32[]{:S(2)}) collective-permute-start(f32[80,128]{1,0:T(8,128)S(1)} %get-tuple-element.40.refs_0_), channel_id=1, source_target_pairs={{1,0},{2,1},{3,2},{0,3},{5,4},{6,5},{7,6},{4,7},{9,8},{10,9},{11,1... | collective-permute-start | bytes 122888 | tf_op jit(solution)/shard_map/ppermute | solution.py:830
  73.3 3.7 %collective-permute-start.2 = (f32[80,128]{1,0:T(8,128)S(1)}, f32[80,128]{1,0:T(8,128)S(1)}, u32[]{:S(2)}, u32[]{:S(2)}) collective-permute-start(f32[80,128]{1,0:T(8,128)S(1)} %get-tuple-element.40.refs_0_), channel_id=1, source_target_pairs={{0,1},{1,2},{2,3},{3,0},{4,5},{5,6},{6,7},{7,4},{8,9},{9,10},{10,1... | collective-permute-start | bytes 122888 | tf_op jit(solution)/shard_map/ppermute | solution.py:830
  74.4 12.2 %collective-permute-start = (f32[152,512]{1,0:T(8,128)S(1)}, f32[152,512]{1,0:T(8,128)S(1)}, u32[]{:S(2)}, u32[]{:S(2)}) collective-permute-start(f32[152,512]{1,0:T(8,128)S(1)} %get-tuple-element.38), channel_id=1, source_target_pairs={{4,8},{5,9},{6,10},{7,11},{8,4},{9,5},{10,6},{11,7},{12,16},{13,17... | collective-permute-start | bytes 933896 | tf_op jit(solution)/shard_map/ppermute | solution.py:827
  81.4 5.9 %collective-permute-start.5 = (f32[80,128]{1,0:T(8,128)S(1)}, f32[80,128]{1,0:T(8,128)S(1)}, u32[]{:S(2)}, u32[]{:S(2)}) collective-permute-start(f32[80,128]{1,0:T(8,128)S(1)} %get-tuple-element.41), channel_id=1, source_target_pairs={{1,0},{2,1},{3,2},{0,3},{5,4},{6,5},{7,6},{4,7},{9,8},{10,9},{11,1... | collective-permute-start | bytes 122888 | tf_op jit(solution)/shard_map/ppermute | solution.py:830
  84.1 3.1 %collective-permute-start.4 = (f32[80,128]{1,0:T(8,128)S(1)}, f32[80,128]{1,0:T(8,128)S(1)}, u32[]{:S(2)}, u32[]{:S(2)}) collective-permute-start(f32[80,128]{1,0:T(8,128)S(1)} %get-tuple-element.41), channel_id=1, source_target_pairs={{0,1},{1,2},{2,3},{3,0},{4,5},{5,6},{6,7},{7,4},{8,9},{9,10},{10,1... | collective-permute-start | bytes 122888 | tf_op jit(solution)/shard_map/ppermute | solution.py:830
  84.1 9.7 %collective-permute-start.7 = (f32[152,512]{1,0:T(8,128)S(1)}, f32[152,512]{1,0:T(8,128)S(1)}, u32[]{:S(2)}, u32[]{:S(2)}) collective-permute-start(f32[152,512]{1,0:T(8,128)S(1)} %get-tuple-element.45), channel_id=1, source_target_pairs={{0,4},{1,5},{2,6},{3,7},{4,0},{5,1},{6,2},{7,3},{8,12},{9,13},{10,... | collective-permute-start | bytes 933896 | tf_op jit(solution)/shard_map/ppermute | solution.py:827
  90.8 10.9 %collective-permute-start.6 = (f32[152,512]{1,0:T(8,128)S(1)}, f32[152,512]{1,0:T(8,128)S(1)}, u32[]{:S(2)}, u32[]{:S(2)}) collective-permute-start(f32[152,512]{1,0:T(8,128)S(1)} %get-tuple-element.44), channel_id=1, source_target_pairs={{4,8},{5,9},{6,10},{7,11},{8,4},{9,5},{10,6},{11,7},{12,16},{13,17... | collective-permute-start | bytes 933896 | tf_op jit(solution)/shard_map/ppermute | solution.py:827
  97.3 4.3 %collective-permute-start.9 = (f32[80,128]{1,0:T(8,128)S(1)}, f32[80,128]{1,0:T(8,128)S(1)}, u32[]{:S(2)}, u32[]{:S(2)}) collective-permute-start(f32[80,128]{1,0:T(8,128)S(1)} %get-tuple-element.47), channel_id=1, source_target_pairs={{1,0},{2,1},{3,2},{0,3},{5,4},{6,5},{7,6},{4,7},{9,8},{10,9},{11,1... | collective-permute-start | bytes 122888 | tf_op jit(solution)/shard_map/ppermute | solution.py:830
  99.5 2.2 %collective-permute-start.8 = (f32[80,128]{1,0:T(8,128)S(1)}, f32[80,128]{1,0:T(8,128)S(1)}, u32[]{:S(2)}, u32[]{:S(2)}) collective-permute-start(f32[80,128]{1,0:T(8,128)S(1)} %get-tuple-element.47), channel_id=1, source_target_pairs={{0,1},{1,2},{2,3},{3,0},{4,5},{5,6},{6,7},{7,4},{8,9},{9,10},{10,1... | collective-permute-start | bytes 122888 | tf_op jit(solution)/shard_map/ppermute | solution.py:830
  99.6 11.7 %collective-permute-start.13 = (f32[152,512]{1,0:T(8,128)S(1)}, f32[152,512]{1,0:T(8,128)S(1)}, u32[]{:S(2)}, u32[]{:S(2)}) collective-permute-start(f32[152,512]{1,0:T(8,128)S(1)} %get-tuple-element.52), channel_id=1, source_target_pairs={{0,4},{1,5},{2,6},{3,7},{4,0},{5,1},{6,2},{7,3},{8,12},{9,13},{10,... | collective-permute-start | bytes 933896 | tf_op jit(solution)/shard_map/ppermute | solution.py:827
  105.2 6.1 %collective-permute-start.12 = (f32[80,128]{1,0:T(8,128)S(1)}, f32[80,128]{1,0:T(8,128)S(1)}, u32[]{:S(2)}, u32[]{:S(2)}) collective-permute-start(f32[80,128]{1,0:T(8,128)S(1)} %get-tuple-element.50), channel_id=1, source_target_pairs={{1,0},{2,1},{3,2},{0,3},{5,4},{6,5},{7,6},{4,7},{9,8},{10,9},{11,1... | collective-permute-start | bytes 122888 | tf_op jit(solution)/shard_map/ppermute | solution.py:830
  107.0 4.3 %collective-permute-start.11 = (f32[80,128]{1,0:T(8,128)S(1)}, f32[80,128]{1,0:T(8,128)S(1)}, u32[]{:S(2)}, u32[]{:S(2)}) collective-permute-start(f32[80,128]{1,0:T(8,128)S(1)} %get-tuple-element.50), channel_id=1, source_target_pairs={{0,1},{1,2},{2,3},{3,0},{4,5},{5,6},{6,7},{7,4},{8,9},{9,10},{10,1... | collective-permute-start | bytes 122888 | tf_op jit(solution)/shard_map/ppermute | solution.py:830
  109.3 12.0 %collective-permute-start.10 = (f32[152,512]{1,0:T(8,128)S(1)}, f32[152,512]{1,0:T(8,128)S(1)}, u32[]{:S(2)}, u32[]{:S(2)}) collective-permute-start(f32[152,512]{1,0:T(8,128)S(1)} %get-tuple-element.49), channel_id=1, source_target_pairs={{4,8},{5,9},{6,10},{7,11},{8,4},{9,5},{10,6},{11,7},{12,16},{13,17... | collective-permute-start | bytes 933896 | tf_op jit(solution)/shard_map/ppermute | solution.py:827
where the time goes:
time: 125 us; the launch traced here: 124 us
  waiting for transfers between devices  48.4 us (39%)
  Pallas kernels  44.6 us (36%)
  starting transfers between devices  27.4 us (22%)
  local copies, waits for them, and re-layouts  2.04 us (2%)
  other arithmetic  1.29 us (1%)
    all_to_all x1, waiting for transfers between devices, body(): lax.all_to_all(message, ('ja', 'ia'), split_axis=0, concat_axis=0, tiled=...  41.7 us
    pallas_call x4, Pallas kernels, diffuse(): pl.pallas_call(kernel, in_specs=in_place(8 + len(far_cols)), out_shape=ha...  14.2 us
    pallas_call x1, Pallas kernels, send_tables(): pl.pallas_call(kernel, grid=(devices // per_step,), in_specs=[whole(x) fo...  9.76 us
    ppermute x6, starting transfers between devices, swap(): return lax.ppermute(edge, ('ja', 'ia'), swaps[which])  9.54 us
    ppermute x4, starting transfers between devices, pass_columns(): lax.ppermute(cols, 'ia', ring_west)  7.94 us
    all_to_all x1, starting transfers between devices, body(): lax.all_to_all(message, ('ja', 'ia'), split_axis=0, concat_axis=0, tiled=...  6.41 us
    pallas_call x1, Pallas kernels, last_inner(): pl.pallas_call(kernel, in_specs=in_place(13), out_specs=[pl.BlockSpec(mem...  6.29 us
    ppermute x6, waiting for transfers between devices, swap(): return lax.ppermute(edge, ('ja', 'ia'), swaps[which])  6.05 us
  transfers between devices with their start and end apart: 15, of which 5 were waited for; matrix products, arithmetic and copies ran while one was open for 3% of the time, Pallas kernels for 22%

commit v1 on v0

--- a/solution.py
+++ b/solution.py
@@ -151,7 +151,7 @@
 def send_tables(devices, capacity, group, row_count, col_count, operands):
     n_obs = operands[1].shape[1]
     n_alt = operands[5].shape[1]
-    per_step = max(1, 768 // capacity)
+    per_step = max(1, 1536 // capacity)
 
     def kernel(*refs):
         table_kernel(devices, capacity, group, row_count, col_count, *refs)
@@ -615,9 +615,12 @@
     )(flags, state, other, *received, mirror, coef, matrix, *far_cols)
 
 
-def store_block(results, out_ref, stage_ref, sem, at, field):
+def output_layout(results):
+    return jnp.swapaxes(jnp.stack(results), 0, 1)[:LEVELS]
+
+
+def store_block(out_ref, stage_ref, sem, at, field):
     rows = stage_ref.shape[2]
-    stage_ref[field] = jnp.swapaxes(jnp.stack(results), 0, 1)[:LEVELS]
     copy = pltpu.make_async_copy(
         stage_ref.at[field],
         out_ref.at[pl.ds(field * LEVELS, LEVELS), pl.ds(at, rows), :],
@@ -630,7 +633,7 @@
 def last_inner(flags, near, far, near_edge, near_sides, far_sides, mirror, near_fixed, far_fixed, mask):
     rows, _, col_count = near.shape
 
-    def kernel(flag_ref, near_ref, far_ref, edge_in, near_west, near_east, far_west, far_east, mirror_ref, near_coef, near_matrix, far_coef, far_matrix, mask_ref, out_ref, done_ref, south_ref, north_ref, outer_ref, right_ref, stage_ref, sem):
+    def kernel(flag_ref, near_ref, far_ref, edge_in, near_west, near_east, far_west, far_east, mirror_ref, near_coef, near_matrix, far_coef, far_matrix, mask_ref, out_ref, done_ref, south_ref, north_ref, outer_ref, right_ref, stage_ref, sem, kept_ref):
         is_upper = flag_ref[NEAR] > 0
         at = pl.multiple_of(jnp.where(is_upper, rows, 0), 8)
         wet = mask_ref[pl.ds(at, rows), :].astype(F32)
@@ -649,7 +652,8 @@
 
             units = [(row, field) for row in range(rows)]
             sweep_rows(NEAR, rows, units, near_ref, south_ref, north_ref, near_west, near_east, near_coef, near_matrix, right_ref, emit)
-            copies.append(store_block(results, out_ref, stage_ref, sem, at, field))
+            stage_ref[field] = output_layout(results)
+            copies.append(store_block(out_ref, stage_ref, sem, at, field))
         edge = jnp.where(is_upper, last, 0)
         near_inner = near_ref.at[jnp.where(is_upper, 0, last)]
 
@@ -664,7 +668,7 @@
             north_ref[...] = far_ref[1]
 
         def keep(number, row, field, result):
-            done_ref[row, field * PAD : (field + 1) * PAD] = result * far_wet[row : row + 1]
+            kept_ref[row, field * PAD : (field + 1) * PAD] = result * far_wet[row : row + 1]
 
         units = [(row, field) for row in range(1, last) for field in range(2)]
         sweep_rows(FAR, rows, units, far_ref, south_ref, north_ref, far_west, far_east, far_coef, far_matrix, right_ref, keep)
@@ -673,7 +677,10 @@
             mix_row(FAR, edge, rows, field, far_ref, south_ref, north_ref, far_west, far_east, far_coef, right_ref, field)
         for field in range(2):
             result = mm(far_matrix[field, edge], right_ref[field])
-            done_ref[edge, field * PAD : (field + 1) * PAD] = result * edge_wet
+            kept_ref[edge, field * PAD : (field + 1) * PAD] = result * edge_wet
+        for field in range(2):
+            levels = slice(field * PAD, (field + 1) * PAD)
+            done_ref[field] = output_layout([kept_ref[row, levels] for row in range(rows)])
         for copy in copies:
             copy.wait()
 
@@ -683,15 +690,16 @@
         out_specs=[pl.BlockSpec(memory_space=pl.ANY), pl.BlockSpec(memory_space=pltpu.VMEM)],
         out_shape=(
             jax.ShapeDtypeStruct((2 * LEVELS, 2 * rows, col_count), F32),
-            jax.ShapeDtypeStruct((rows, 2 * PAD, col_count), F32),
+            jax.ShapeDtypeStruct((2, LEVELS, rows, col_count), F32),
         ),
         scratch_shapes=[pltpu.VMEM((2 * PAD, col_count), F32)] * 3
         + [
             pltpu.VMEM((4, 256, col_count), BF),
             pltpu.VMEM((2, LEVELS, rows, col_count), F32),
             pltpu.SemaphoreType.DMA((2,)),
+            pltpu.VMEM((rows, 2 * PAD, col_count), F32),
         ],
-        compiler_params=pltpu.CompilerParams(vmem_limit_bytes=20 * MIB),
+        compiler_params=pltpu.CompilerParams(vmem_limit_bytes=22 * MIB),
         cost_estimate=pl.CostEstimate(
             flops=6_000_000_000, bytes_accessed=16_000_000, transcendentals=0
         ),
@@ -715,12 +723,14 @@
         for field in range(2):
             mix_row(FAR, row, rows, field, far_ref, south_ref, north_ref, west_in, east_in, coef_ref, right_ref, field)
         copies = []
+        here = lax.broadcasted_iota(jnp.int32, (rows, 1), 0) == row
         for field in range(2):
-            result = mm(matrix_ref[field, row], right_ref[field]) * row_wet
-            done_field = [done_ref[r, field * PAD : (field + 1) * PAD] for r in range(rows)]
-            done_field[0] = jnp.where(is_upper, done_field[0], result)
-            done_field[last] = jnp.where(is_upper, result, done_field[last])
-            copies.append(store_block(done_field, out_ref, stage_ref, sem, at, field))
+            outer_ref[0:PAD] = mm(matrix_ref[field, row], right_ref[field]) * row_wet
+            for level in range(LEVELS):
+                stage_ref[field, level] = jnp.where(
+                    here, outer_ref[level : level + 1, :], done_ref[field, level]
+                )
+            copies.append(store_block(out_ref, stage_ref, sem, at, field))
         for copy in copies:
             copy.wait()
 

time: 125 us -> 124 us (level)
  the two profiles are of different devices: /device:TPU:5 before, /device:TPU:13 now
where the time goes in v1:
time: 124 us
  waiting for transfers between devices  49.2 us (40%)
  Pallas kernels  48.4 us (39%)
  starting transfers between devices  22.4 us (18%)
  local copies, waits for them, and re-layouts  2.04 us (2%)
  other arithmetic  1.29 us (1%)
    all_to_all x1, waiting for transfers between devices, body(): lax.all_to_all(message, ('ja', 'ia'), split_axis=0, concat_axis=0, tiled=...  39.4 us
    pallas_call x4, Pallas kernels, diffuse(): pl.pallas_call(kernel, in_specs=in_place(8 + len(far_cols)), out_shape=ha...  14.2 us
    ppermute x6, waiting for transfers between devices, swap(): return lax.ppermute(edge, ('ja', 'ia'), swaps[which])  9.67 us
    pallas_call x1, Pallas kernels, send_tables(): pl.pallas_call(kernel, grid=(devices // per_step,), in_specs=[whole(x) fo...  9.42 us
    pallas_call x1, Pallas kernels, rest_forcing(): pl.pallas_call(kernel, in_specs=in_place(8) + [pl.BlockSpec(memory_space=...  9.25 us
    ppermute x6, starting transfers between devices, swap(): return lax.ppermute(edge, ('ja', 'ia'), swaps[which])  8.93 us
    pallas_call x1, Pallas kernels, last_inner(): pl.pallas_call(kernel, in_specs=in_place(13), out_specs=[pl.BlockSpec(mem...  6.69 us
    all_to_all x1, starting transfers between devices, body(): lax.all_to_all(message, ('ja', 'ia'), split_axis=0, concat_axis=0, tiled=...  6.31 us
  transfers between devices with their start and end apart: 15, of which 4 were waited for; matrix products, arithmetic and copies ran while one was open for 3% of the time, Pallas kernels for 26%

profile of v1, /device:TPU:13, one launch (start us, length us, event | category | flops | bytes accessed | tf_op | source)
XLA Modules:
  0.0 123.7 jit_solution(4862530309622103401)
XLA Ops:
  0.0 9.4 %send_tables.1 = f32[32,120,128]{2,1,0:T(8,128)} custom-call(f32[150,1024]{1,0:T(8,128)} %bitcast.11, s32[1,1024]{1,0:T(1,128)} %bitcast.12, s32[1,1024]{1,0:T(1,128)} %bitcast.13, f32[768]{0:T(1024)} %refs_3_.3, s32[768]{0:T(1024)} %refs_4_.1, s32[1,768]{1,0:T(1,128)} %bitcast.14), custom_call_target="tpu_custom_call" | custom-call | tf_op jit(solution)/shard_map/send_tables/pallas_call | solution.py:162
  9.4 0.0 copy-start.4
  9.4 6.3 %all-to-all-start = ((f32[32,120,128]{2,1,0:T(8,128)}), f32[32,120,128]{2,1,0:T(8,128)S(1)}, u32[]{:S(2)}, u32[]{:S(2)}) async-start(f32[32,120,128]{2,1,0:T(8,128)} %send_tables.1), calls=%async_computation | async-start | bytes 3932160 | tf_op jit(solution)/shard_map/all_to_all | solution.py:801
  15.7 0.0 copy-done.4
  15.8 0.1 reshape.19
  15.9 0.1 reshape.22.profile_ref
  16.0 1.7 %copy.17 = f32[16,2,75,75]{2,3,0,1:T(8,128)S(1)} copy(f32[16,2,75,75]{3,1,2,0:T(2,128)} %param.23) | data formatting | bytes 1440000 | tf_op args[11]
  17.7 0.1 pad.13.clone
  17.8 0.1 pad_add_fusion.flag_ref.refs_0_
  17.9 0.2 reduce-precision_convert_fusion
  18.1 0.0 copy-start
  18.1 0.0 copy-start.1
  18.1 0.0 copy-start.2
  18.1 0.9 maximum_maximum_fusion
  19.0 0.1 broadcast_select_fusion
  19.1 39.4 %all-to-all-done.message_ref = f32[32,120,128]{2,1,0:T(8,128)S(1)} async-done(((f32[32,120,128]{2,1,0:T(8,128)}), f32[32,120,128]{2,1,0:T(8,128)S(1)}, u32[]{:S(2)}, u32[]{:S(2)}) %all-to-all-start) | async-done | bytes 1966112 | tf_op jit(solution)/shard_map/all_to_all | solution.py:801
  58.6 0.0 copy-done
  58.6 0.0 copy-done.1
  58.6 0.0 copy-done.2
  58.6 4.8 %forcing_first.1 = (f32[152,512]{1,0:T(8,128)S(1)}, f32[16,512]{1,0:T(8,128)S(1)}, bf16[12,160,512]{2,1,0:T(8,128)(2,1)S(1)}, bf16[12,256,512]{2,1,0:T(8,128)(2,...) custom-call(s32[3]{0:T(128)S(1)} %pad_add_fusion.flag_ref.refs_0_, f32[32,120,128]{2,1,0:T(8,128)S(1)} %all-to-all-done.message_ref, ...), custom_call_target="tpu_custom_call" | custom-call | flops 6000000000 | bytes 8000000 | tf_op jit(solution)/shard_map/forcing_first/pallas_call | solution.py:366
  63.4 1.7 %collective-permute-start.1 = (f32[152,512]{1,0:T(8,128)S(1)}, f32[152,512]{1,0:T(8,128)S(1)}, u32[]{:S(2)}, u32[]{:S(2)}) collective-permute-start(f32[152,512]{1,0:T(8,128)S(1)} %get-tuple-element.39), channel_id=1, source_target_pairs={{0,4},{1,5},{2,6},{3,7},{4,0},{5,1},{6,2},{7,3},{8,12},{9,13},{10,... | collective-permute-start | bytes 933896 | tf_op jit(solution)/shard_map/ppermute | solution.py:837
  65.1 0.0 copy-start.3
  65.1 9.2 %forcing_rest.1 = (f32[16,160,512]{2,1,0:T(8,128)S(1)}, f32[152,512]{1,0:T(8,128)S(1)}, f32[80,128]{1,0:T(8,128)S(1)}) custom-call(s32[3]{0:T(128)S(1)} %pad_add_fusion.flag_ref.refs_0_, f32[160,1]{1,0:T(8,128)S(1)} %reshape.22.profile_ref, s32[16,512]{1,0:T(8,128)S(1)} %copy-done, f32[16,512]{1,0:T(8,128)S(1)} %copy-done.1, f32[16,512]{1,0:T(8,128)S(1)} %copy-done.2, ...), custom_call_target="tpu_custom_call" | custom-call | flops 6000000000 | bytes 8000000 | tf_op jit(solution)/shard_map/forcing_rest/pallas_call | solution.py:403
  74.4 0.1 collective-permute-start.3
  74.5 1.7 %collective-permute-start.2 = (f32[80,128]{1,0:T(8,128)S(1)}, f32[80,128]{1,0:T(8,128)S(1)}, u32[]{:S(2)}, u32[]{:S(2)}) collective-permute-start(f32[80,128]{1,0:T(8,128)S(1)} %get-tuple-element.40.refs_0_), channel_id=1, source_target_pairs={{0,1},{1,2},{2,3},{3,0},{4,5},{5,6},{6,7},{7,4},{8,9},{9,10},{10,1... | collective-permute-start | bytes 122888 | tf_op jit(solution)/shard_map/ppermute | solution.py:840
  76.2 0.0 copy-done.3
  76.2 1.9 %collective-permute-start = (f32[152,512]{1,0:T(8,128)S(1)}, f32[152,512]{1,0:T(8,128)S(1)}, u32[]{:S(2)}, u32[]{:S(2)}) collective-permute-start(f32[152,512]{1,0:T(8,128)S(1)} %get-tuple-element.38), channel_id=1, source_target_pairs={{4,8},{5,9},{6,10},{7,11},{8,4},{9,5},{10,6},{11,7},{12,16},{13,17... | collective-permute-start | bytes 933896 | tf_op jit(solution)/shard_map/ppermute | solution.py:837
  78.1 0.0 collective-permute-done.3.refs_6_.east_in
  78.2 0.0 collective-permute-done.2.refs_5_.west_in
  78.2 0.0 collective-permute-done.1.refs_4_.edge_in
  78.2 0.7 edge_weights.2.coef_ref.near_coef
  78.9 3.7 %diffusion_near.2 = (f32[8,160,512]{2,1,0:T(8,128)S(1)}, f32[152,512]{1,0:T(8,128)S(1)}, f32[80,128]{1,0:T(8,128)S(1)}) custom-call(s32[3]{0:T(128)S(1)} %pad_add_fusion.flag_ref.refs_0_, f32[16,160,512]{2,1,0:T(8,128)S(1)} %get-tuple-element.37.state_ref.other_ref, f32[16,160,512]{2,1,0:T(8,128)S(1)} %get-tuple-element.37.state_ref.other_ref, ...), custom_call_target="tpu_custom_call" | custom-call | flops 3000000000 | bytes 8000000 | tf_op jit(solution)/shard_map/diffusion_near/pallas_call | solution.py:604
  82.6 0.4 collective-permute-start.5
  83.0 1.4 %collective-permute-start.4 = (f32[80,128]{1,0:T(8,128)S(1)}, f32[80,128]{1,0:T(8,128)S(1)}, u32[]{:S(2)}, u32[]{:S(2)}) collective-permute-start(f32[80,128]{1,0:T(8,128)S(1)} %get-tuple-element.41), channel_id=1, source_target_pairs={{0,1},{1,2},{2,3},{3,0},{4,5},{5,6},{6,7},{7,4},{8,9},{9,10},{10,1... | collective-permute-start | bytes 122888 | tf_op jit(solution)/shard_map/ppermute | solution.py:840
  84.4 0.1 collective-permute-start.7
  84.5 3.0 %collective-permute-done.refs_4_.edge_in = f32[152,512]{1,0:T(8,128)S(1)} collective-permute-done((f32[152,512]{1,0:T(8,128)S(1)}, f32[152,512]{1,0:T(8,128)S(1)}, u32[]{:S(2)}, u32[]{:S(2)}) %collective-permute-start) | collective-permute-done | bytes 311328 | tf_op jit(solution)/shard_map/ppermute | solution.py:837
  87.5 0.7 edge_weights.3.coef_ref.far_coef
  88.2 0.0 collective-permute-done.5.east_in
  88.2 0.0 collective-permute-done.4.west_in
  88.2 3.5 %diffusion_far.2 = (f32[8,160,512]{2,1,0:T(8,128)S(1)}, f32[152,512]{1,0:T(8,128)S(1)}, f32[80,128]{1,0:T(8,128)S(1)}) custom-call(s32[3]{0:T(128)S(1)} %pad_add_fusion.flag_ref.refs_0_, f32[16,160,512]{2,1,0:T(8,128)S(1)} %get-tuple-element.37.state_ref.other_ref, f32[16,160,512]{2,1,0:T(8,128)S(1)} %get-tuple-element.37.state_ref.other_ref, ...), custom_call_target="tpu_custom_call" | custom-call | flops 3000000000 | bytes 8000000 | tf_op jit(solution)/shard_map/diffusion_far/pallas_call | solution.py:604
  91.7 2.6 %collective-permute-start.6 = (f32[152,512]{1,0:T(8,128)S(1)}, f32[152,512]{1,0:T(8,128)S(1)}, u32[]{:S(2)}, u32[]{:S(2)}) collective-permute-start(f32[152,512]{1,0:T(8,128)S(1)} %get-tuple-element.44), channel_id=1, source_target_pairs={{4,8},{5,9},{6,10},{7,11},{8,4},{9,5},{10,6},{11,7},{12,16},{13,17... | collective-permute-start | bytes 933896 | tf_op jit(solution)/shard_map/ppermute | solution.py:837
  94.3 0.0 collective-permute-done.7.edge_in
  94.3 3.5 %diffusion_near.3 = (f32[8,160,512]{2,1,0:T(8,128)S(1)}, f32[152,512]{1,0:T(8,128)S(1)}, f32[80,128]{1,0:T(8,128)S(1)}) custom-call(s32[3]{0:T(128)S(1)} %pad_add_fusion.flag_ref.refs_0_, f32[8,160,512]{2,1,0:T(8,128)S(1)} %get-tuple-element.43.state_ref.other_ref, f32[8,160,512]{2,1,0:T(8,128)S(1)} %get-tuple-element.42.other_ref.state_ref, ...), custom_call_target="tpu_custom_call" | custom-call | flops 3000000000 | bytes 8000000 | tf_op jit(solution)/shard_map/diffusion_near/pallas_call | solution.py:604
  97.9 0.5 collective-permute-start.9
  98.4 1.3 %collective-permute-start.8 = (f32[80,128]{1,0:T(8,128)S(1)}, f32[80,128]{1,0:T(8,128)S(1)}, u32[]{:S(2)}, u32[]{:S(2)}) collective-permute-start(f32[80,128]{1,0:T(8,128)S(1)} %get-tuple-element.47), channel_id=1, source_target_pairs={{0,1},{1,2},{2,3},{3,0},{4,5},{5,6},{6,7},{7,4},{8,9},{9,10},{10,1... | collective-permute-start | bytes 122888 | tf_op jit(solution)/shard_map/ppermute | solution.py:840
  99.7 0.2 collective-permute-start.13
  99.9 3.6 %collective-permute-done.6.edge_in = f32[152,512]{1,0:T(8,128)S(1)} collective-permute-done((f32[152,512]{1,0:T(8,128)S(1)}, f32[152,512]{1,0:T(8,128)S(1)}, u32[]{:S(2)}, u32[]{:S(2)}) %collective-permute-start.6) | collective-permute-done | bytes 311328 | tf_op jit(solution)/shard_map/ppermute | solution.py:837
  103.6 0.0 collective-permute-done.9.east_in.near_east
  103.6 0.0 collective-permute-done.8.west_in.near_west
  103.6 3.5 %diffusion_far.3 = (f32[8,160,512]{2,1,0:T(8,128)S(1)}, f32[152,512]{1,0:T(8,128)S(1)}, f32[80,128]{1,0:T(8,128)S(1)}) custom-call(s32[3]{0:T(128)S(1)} %pad_add_fusion.flag_ref.refs_0_, f32[8,160,512]{2,1,0:T(8,128)S(1)} %get-tuple-element.42.other_ref.state_ref, f32[8,160,512]{2,1,0:T(8,128)S(1)} %get-tuple-element.43.state_ref.other_ref, ...), custom_call_target="tpu_custom_call" | custom-call | flops 3000000000 | bytes 8000000 | tf_op jit(solution)/shard_map/diffusion_far/pallas_call | solution.py:604
  107.1 0.9 collective-permute-start.12
  108.0 0.9 collective-permute-start.11
  108.9 2.3 %collective-permute-start.10 = (f32[152,512]{1,0:T(8,128)S(1)}, f32[152,512]{1,0:T(8,128)S(1)}, u32[]{:S(2)}, u32[]{:S(2)}) collective-permute-start(f32[152,512]{1,0:T(8,128)S(1)} %get-tuple-element.49), channel_id=1, source_target_pairs={{4,8},{5,9},{6,10},{7,11},{8,4},{9,5},{10,6},{11,7},{12,16},{13,17... | collective-permute-start | bytes 933896 | tf_op jit(solution)/shard_map/ppermute | solution.py:837
  111.2 0.0 collective-permute-done.12.far_east.east_in
  111.2 0.0 collective-permute-done.11.far_west.west_in
  111.2 0.0 collective-permute-done.13.edge_in
  111.3 6.7 %last_inner.1 = (f32[150,16,512]{2,1,0:T(8,128)}, f32[2,75,8,512]{3,2,1,0:T(8,128)S(1)}) custom-call(s32[3]{0:T(128)S(1)} %pad_add_fusion.flag_ref.refs_0_, f32[8,160,512]{2,1,0:T(8,128)S(1)} %get-tuple-element.51.near_ref, f32[8,160,512]{2,1,0:T(8,128)S(1)} %get-tuple-element.48.far_ref, f32[152,512]{1,0:T(8,128)S(1)} %collective-permute-done.13.edge_in, ...), custom_call_target="tpu_custom_call" | custom-call | flops 6000000000 | bytes 16000000 | tf_op jit(solution)/shard_map/last_inner/pallas_call | solution.py:687
  118.0 3.0 %collective-permute-done.10.edge_in = f32[152,512]{1,0:T(8,128)S(1)} collective-permute-done((f32[152,512]{1,0:T(8,128)S(1)}, f32[152,512]{1,0:T(8,128)S(1)}, u32[]{:S(2)}, u32[]{:S(2)}) %collective-permute-start.10) | collective-permute-done | bytes 311328 | tf_op jit(solution)/shard_map/ppermute | solution.py:837
  121.0 2.6 %last_outer.1 = f32[150,16,512]{2,1,0:T(8,128)} custom-call(s32[3]{0:T(128)S(1)} %pad_add_fusion.flag_ref.refs_0_, f32[8,160,512]{2,1,0:T(8,128)S(1)} %get-tuple-element.48.far_ref, f32[152,512]{1,0:T(8,128)S(1)} %collective-permute-done.10.edge_in, f32[80,128]{1,0:T(8,128)S(1)} %collective-permute-done.11.far_west.west_in, ...), custom_call_target="tpu_custom_call", output_to_operand_aliasing={{}: (10, {})} | custom-call | tf_op jit(solution)/shard_map/last_outer/pallas_call | solution.py:738
  (4 shorter events, 0.0 us)
Async XLA Ops:
  9.4 6.3 %copy-start.4 = (f32[150]{0:T(256)S(1)}, f32[150]{0:T(256)}, u32[]{:S(2)}) copy-start(f32[150]{0:T(256)} %param.18) | copy-start | bytes 1804
  9.4 49.1 %all-to-all-start = ((f32[32,120,128]{2,1,0:T(8,128)}), f32[32,120,128]{2,1,0:T(8,128)S(1)}, u32[]{:S(2)}, u32[]{:S(2)}) async-start(f32[32,120,128]{2,1,0:T(8,128)} %send_tables.1), calls=%async_computation | async-start | bytes 3932160 | tf_op jit(solution)/shard_map/all_to_all | solution.py:801
  18.1 40.4 %copy-start = (s32[16,512]{1,0:T(8,128)S(1)}, s32[16,512]{1,0:T(8,128)}, u32[]{:S(2)}) copy-start(s32[16,512]{1,0:T(8,128)} %mask_ref.3) | copy-start | bytes 98308
  18.1 40.4 %copy-start.1 = (f32[16,512]{1,0:T(8,128)S(1)}, f32[16,512]{1,0:T(8,128)}, u32[]{:S(2)}) copy-start(f32[16,512]{1,0:T(8,128)} %refs_2_.3) | copy-start | bytes 98308
  18.1 40.4 %copy-start.2 = (f32[16,512]{1,0:T(8,128)S(1)}, f32[16,512]{1,0:T(8,128)}, u32[]{:S(2)}) copy-start(f32[16,512]{1,0:T(8,128)} %refs_3_.5) | copy-start | bytes 98308
  63.4 14.8 %collective-permute-start.1 = (f32[152,512]{1,0:T(8,128)S(1)}, f32[152,512]{1,0:T(8,128)S(1)}, u32[]{:S(2)}, u32[]{:S(2)}) collective-permute-start(f32[152,512]{1,0:T(8,128)S(1)} %get-tuple-element.39), channel_id=1, source_target_pairs={{0,4},{1,5},{2,6},{3,7},{4,0},{5,1},{6,2},{7,3},{8,12},{9,13},{10,... | collective-permute-start | bytes 933896 | tf_op jit(solution)/shard_map/ppermute | solution.py:837
  65.1 11.1 %copy-start.3 = (s32[512]{0:T(512)S(1)}, s32[512]{0:T(512)}, u32[]{:S(2)}) copy-start(s32[512]{0:T(512)} %param.22) | copy-start | bytes 6148
  74.4 3.8 %collective-permute-start.3 = (f32[80,128]{1,0:T(8,128)S(1)}, f32[80,128]{1,0:T(8,128)S(1)}, u32[]{:S(2)}, u32[]{:S(2)}) collective-permute-start(f32[80,128]{1,0:T(8,128)S(1)} %get-tuple-element.40.refs_0_), channel_id=1, source_target_pairs={{1,0},{2,1},{3,2},{0,3},{5,4},{6,5},{7,6},{4,7},{9,8},{10,9},{11,1... | collective-permute-start | bytes 122888 | tf_op jit(solution)/shard_map/ppermute | solution.py:840
  74.5 3.7 %collective-permute-start.2 = (f32[80,128]{1,0:T(8,128)S(1)}, f32[80,128]{1,0:T(8,128)S(1)}, u32[]{:S(2)}, u32[]{:S(2)}) collective-permute-start(f32[80,128]{1,0:T(8,128)S(1)} %get-tuple-element.40.refs_0_), channel_id=1, source_target_pairs={{0,1},{1,2},{2,3},{3,0},{4,5},{5,6},{6,7},{7,4},{8,9},{9,10},{10,1... | collective-permute-start | bytes 122888 | tf_op jit(solution)/shard_map/ppermute | solution.py:840
  76.2 11.3 %collective-permute-start = (f32[152,512]{1,0:T(8,128)S(1)}, f32[152,512]{1,0:T(8,128)S(1)}, u32[]{:S(2)}, u32[]{:S(2)}) collective-permute-start(f32[152,512]{1,0:T(8,128)S(1)} %get-tuple-element.38), channel_id=1, source_target_pairs={{4,8},{5,9},{6,10},{7,11},{8,4},{9,5},{10,6},{11,7},{12,16},{13,17... | collective-permute-start | bytes 933896 | tf_op jit(solution)/shard_map/ppermute | solution.py:837
  82.6 5.6 %collective-permute-start.5 = (f32[80,128]{1,0:T(8,128)S(1)}, f32[80,128]{1,0:T(8,128)S(1)}, u32[]{:S(2)}, u32[]{:S(2)}) collective-permute-start(f32[80,128]{1,0:T(8,128)S(1)} %get-tuple-element.41), channel_id=1, source_target_pairs={{1,0},{2,1},{3,2},{0,3},{5,4},{6,5},{7,6},{4,7},{9,8},{10,9},{11,1... | collective-permute-start | bytes 122888 | tf_op jit(solution)/shard_map/ppermute | solution.py:840
  83.0 5.2 %collective-permute-start.4 = (f32[80,128]{1,0:T(8,128)S(1)}, f32[80,128]{1,0:T(8,128)S(1)}, u32[]{:S(2)}, u32[]{:S(2)}) collective-permute-start(f32[80,128]{1,0:T(8,128)S(1)} %get-tuple-element.41), channel_id=1, source_target_pairs={{0,1},{1,2},{2,3},{3,0},{4,5},{5,6},{6,7},{7,4},{8,9},{9,10},{10,1... | collective-permute-start | bytes 122888 | tf_op jit(solution)/shard_map/ppermute | solution.py:840
  84.4 10.0 %collective-permute-start.7 = (f32[152,512]{1,0:T(8,128)S(1)}, f32[152,512]{1,0:T(8,128)S(1)}, u32[]{:S(2)}, u32[]{:S(2)}) collective-permute-start(f32[152,512]{1,0:T(8,128)S(1)} %get-tuple-element.45), channel_id=1, source_target_pairs={{0,4},{1,5},{2,6},{3,7},{4,0},{5,1},{6,2},{7,3},{8,12},{9,13},{10,... | collective-permute-start | bytes 933896 | tf_op jit(solution)/shard_map/ppermute | solution.py:837
  91.7 11.8 %collective-permute-start.6 = (f32[152,512]{1,0:T(8,128)S(1)}, f32[152,512]{1,0:T(8,128)S(1)}, u32[]{:S(2)}, u32[]{:S(2)}) collective-permute-start(f32[152,512]{1,0:T(8,128)S(1)} %get-tuple-element.44), channel_id=1, source_target_pairs={{4,8},{5,9},{6,10},{7,11},{8,4},{9,5},{10,6},{11,7},{12,16},{13,17... | collective-permute-start | bytes 933896 | tf_op jit(solution)/shard_map/ppermute | solution.py:837
  97.9 5.7 %collective-permute-start.9 = (f32[80,128]{1,0:T(8,128)S(1)}, f32[80,128]{1,0:T(8,128)S(1)}, u32[]{:S(2)}, u32[]{:S(2)}) collective-permute-start(f32[80,128]{1,0:T(8,128)S(1)} %get-tuple-element.47), channel_id=1, source_target_pairs={{1,0},{2,1},{3,2},{0,3},{5,4},{6,5},{7,6},{4,7},{9,8},{10,9},{11,1... | collective-permute-start | bytes 122888 | tf_op jit(solution)/shard_map/ppermute | solution.py:840
  98.4 5.2 %collective-permute-start.8 = (f32[80,128]{1,0:T(8,128)S(1)}, f32[80,128]{1,0:T(8,128)S(1)}, u32[]{:S(2)}, u32[]{:S(2)}) collective-permute-start(f32[80,128]{1,0:T(8,128)S(1)} %get-tuple-element.47), channel_id=1, source_target_pairs={{0,1},{1,2},{2,3},{3,0},{4,5},{5,6},{6,7},{7,4},{8,9},{9,10},{10,1... | collective-permute-start | bytes 122888 | tf_op jit(solution)/shard_map/ppermute | solution.py:840
  99.7 11.6 %collective-permute-start.13 = (f32[152,512]{1,0:T(8,128)S(1)}, f32[152,512]{1,0:T(8,128)S(1)}, u32[]{:S(2)}, u32[]{:S(2)}) collective-permute-start(f32[152,512]{1,0:T(8,128)S(1)} %get-tuple-element.52), channel_id=1, source_target_pairs={{0,4},{1,5},{2,6},{3,7},{4,0},{5,1},{6,2},{7,3},{8,12},{9,13},{10,... | collective-permute-start | bytes 933896 | tf_op jit(solution)/shard_map/ppermute | solution.py:837
  107.1 4.1 %collective-permute-start.12 = (f32[80,128]{1,0:T(8,128)S(1)}, f32[80,128]{1,0:T(8,128)S(1)}, u32[]{:S(2)}, u32[]{:S(2)}) collective-permute-start(f32[80,128]{1,0:T(8,128)S(1)} %get-tuple-element.50), channel_id=1, source_target_pairs={{1,0},{2,1},{3,2},{0,3},{5,4},{6,5},{7,6},{4,7},{9,8},{10,9},{11,1... | collective-permute-start | bytes 122888 | tf_op jit(solution)/shard_map/ppermute | solution.py:840
  108.0 3.3 %collective-permute-start.11 = (f32[80,128]{1,0:T(8,128)S(1)}, f32[80,128]{1,0:T(8,128)S(1)}, u32[]{:S(2)}, u32[]{:S(2)}) collective-permute-start(f32[80,128]{1,0:T(8,128)S(1)} %get-tuple-element.50), channel_id=1, source_target_pairs={{0,1},{1,2},{2,3},{3,0},{4,5},{5,6},{6,7},{7,4},{8,9},{9,10},{10,1... | collective-permute-start | bytes 122888 | tf_op jit(solution)/shard_map/ppermute | solution.py:840
  108.9 12.1 %collective-permute-start.10 = (f32[152,512]{1,0:T(8,128)S(1)}, f32[152,512]{1,0:T(8,128)S(1)}, u32[]{:S(2)}, u32[]{:S(2)}) collective-permute-start(f32[152,512]{1,0:T(8,128)S(1)} %get-tuple-element.49), channel_id=1, source_target_pairs={{4,8},{5,9},{6,10},{7,11},{8,4},{9,5},{10,6},{11,7},{12,16},{13,17... | collective-permute-start | bytes 933896 | tf_op jit(solution)/shard_map/ppermute | solution.py:837

commit v2 on v1

--- a/solution.py
+++ b/solution.py
@@ -109,14 +109,15 @@
         high, low = split_two(level_ref[...].T)
         hi_ref[...] = high
         lo_ref[...] = low
-        side_ref[...] = jnp.zeros(side_ref.shape, F32)
         pair = jnp.concatenate(
             [alt_value_ref[...].reshape(1, n_alt), alt_cell.astype(F32) + 1.0], axis=0
         )
         pair_high = pair.astype(BF).astype(F32)
-        side_ref[76:78, :] = pair_high
-        side_ref[78:80, :] = pair - pair_high
-        alt_all_ref[...] = side_ref[...].T.astype(BF)
+        side_ref[...] = jnp.zeros(side_ref.shape, F32)
+        side_ref[:, 0:8] = jnp.concatenate(
+            [pair_high, pair - pair_high, jnp.zeros((4, n_alt), F32)], axis=0
+        ).T
+        alt_all_ref[...] = pltpu.roll(side_ref[...], 76, 1).astype(BF)
 
     per_step = message_ref.shape[0]
     chosen = []
@@ -167,7 +168,7 @@
         out_shape=jax.ShapeDtypeStruct((devices, capacity + group, LANES), F32),
         scratch_shapes=[
             pltpu.VMEM((2 * LANES, n_obs), F32),
-            pltpu.VMEM((LANES, n_alt), F32),
+            pltpu.VMEM((n_alt, LANES), F32),
             pltpu.VMEM((n_obs, 2 * LANES), BF),
             pltpu.VMEM((n_obs, 2 * LANES), BF),
             pltpu.VMEM((n_alt, LANES), BF),
@@ -304,19 +305,17 @@
         profile = jnp.broadcast_to(profile_ref[...], (2 * PAD, LANES))
         for row in range(row_count):
             state[row, :, start : start + LANES] = profile * sea_ref[row : row + 1, start : start + LANES]
-    span = 3
     batch = math.gcd(count, 4)
+    narrow, wide = 3, 6
 
     def step(number, carry):
         chunks = [number * batch + member for member in range(batch)]
         least = [bound_ref[2 * chunk] for chunk in chunks]
-        most = [bound_ref[2 * chunk + 1] for chunk in chunks]
-        runs = [lax.div(most[i] - least[i] + span, span) for i in range(batch)]
-        longest = runs[0]
-        for run in runs[1:]:
-            longest = jnp.maximum(longest, run)
-
-        def run_step(turn, inner):
+        extent = bound_ref[2 * chunks[0] + 1] - least[0]
+        for i in range(1, batch):
+            extent = jnp.maximum(extent, bound_ref[2 * chunks[i] + 1] - least[i])
+
+        def add_runs(span, turn, inner):
             for i, chunk in enumerate(chunks):
                 begin = least[i] + turn * span
                 base = jnp.minimum(begin, row_count - span)
@@ -327,7 +326,10 @@
                     state[base + offset] += product[2 * PAD * offset : 2 * PAD * (offset + 1)]
             return inner
 
-        lax.fori_loop(0, longest, run_step, 0)
+        once = (extent >= 0) & (extent < narrow)
+        lax.fori_loop(0, once.astype(jnp.int32), lambda t, c: add_runs(narrow, t, c), 0)
+        turns = jnp.where(extent < narrow, 0, lax.div(extent + wide, wide))
+        lax.fori_loop(0, turns, lambda t, c: add_runs(wide, t, c), 0)
         return carry
 
     lax.fori_loop(0, count // batch, step, 0)

time: 124 us -> 124 us (level)
  starting transfers between devices: 22.4 us -> 31.3 us
  waiting for transfers between devices: 49.2 us -> 44.1 us
  Pallas kernels: 48.4 us -> 44.7 us
    ppermute x4, starting transfers between devices: 1.88 us -> 10.6 us  [pass_columns(): lax.ppermute(cols, 'ia', ring_west)]
    ppermute x6, waiting for transfers between devices: 9.67 us -> 3.43 us  [swap(): return lax.ppermute(edge, ('ja', 'ia'), swaps[which])]
    pallas_call x1, Pallas kernels: 9.25 us -> 5.69 us  [rest_forcing(): pl.pallas_call(kernel, in_specs=in_place(8) + [pl.BlockSpec(memory_space=...]
    ppermute x6, starting transfers between devices: 8.93 us -> 11.4 us  [swap(): return lax.ppermute(edge, ('ja', 'ia'), swaps[which])]
    ppermute x4, starting transfers between devices: 5.3 us -> 2.96 us  [pass_columns(): lax.ppermute(cols, 'ia', ring_east)]
  transfers between devices with their start and end apart: 15 -> 15, of which waited for: 4 -> 4; matrix products, arithmetic and copies ran while one was open for 3% -> 3% of each run, Pallas kernels for 26% -> 23%
where the time goes in v2:
time: 124 us
  Pallas kernels  44.7 us (36%)
  waiting for transfers between devices  44.1 us (36%)
  starting transfers between devices  31.3 us (25%)
  local copies, waits for them, and re-layouts  2.04 us (2%)
  other arithmetic  1.29 us (1%)
    all_to_all x1, waiting for transfers between devices, body(): lax.all_to_all(message, ('ja', 'ia'), split_axis=0, concat_axis=0, tiled=...  39.4 us
    pallas_call x4, Pallas kernels, diffuse(): pl.pallas_call(kernel, in_specs=in_place(8 + len(far_cols)), out_shape=ha...  14.2 us
    ppermute x6, starting transfers between devices, swap(): return lax.ppermute(edge, ('ja', 'ia'), swaps[which])  11.4 us
    ppermute x4, starting transfers between devices, pass_columns(): lax.ppermute(cols, 'ia', ring_west)  10.6 us
    pallas_call x1, Pallas kernels, send_tables(): pl.pallas_call(kernel, grid=(devices // per_step,), in_specs=[whole(x) fo...  9.45 us
    pallas_call x1, Pallas kernels, last_inner(): pl.pallas_call(kernel, in_specs=in_place(13), out_specs=[pl.BlockSpec(mem...  6.73 us
    all_to_all x1, starting transfers between devices, body(): lax.all_to_all(message, ('ja', 'ia'), split_axis=0, concat_axis=0, tiled=...  6.31 us
    pallas_call x1, Pallas kernels, rest_forcing(): pl.pallas_call(kernel, in_specs=in_place(8) + [pl.BlockSpec(memory_space=...  5.69 us
  transfers between devices with their start and end apart: 15, of which 4 were waited for; matrix products, arithmetic and copies ran while one was open for 3% of the time, Pallas kernels for 23%

profile of v2, /device:TPU:13, one launch (start us, length us, event | category | flops | bytes accessed | tf_op | source)
XLA Modules:
  0.0 123.8 jit_solution(14921754474179905116)
XLA Ops:
  0.0 9.5 %send_tables.1 = f32[32,120,128]{2,1,0:T(8,128)} custom-call(f32[150,1024]{1,0:T(8,128)} %bitcast.11, s32[1,1024]{1,0:T(1,128)} %bitcast.12, s32[1,1024]{1,0:T(1,128)} %bitcast.13, f32[768]{0:T(1024)} %refs_3_.3, s32[768]{0:T(1024)} %refs_4_.1, s32[1,768]{1,0:T(1,128)} %bitcast.14), custom_call_target="tpu_custom_call" | custom-call | tf_op jit(solution)/shard_map/send_tables/pallas_call | solution.py:163
  9.5 0.0 copy-start.4
  9.5 6.3 %all-to-all-start = ((f32[32,120,128]{2,1,0:T(8,128)}), f32[32,120,128]{2,1,0:T(8,128)S(1)}, u32[]{:S(2)}, u32[]{:S(2)}) async-start(f32[32,120,128]{2,1,0:T(8,128)} %send_tables.1), calls=%async_computation | async-start | bytes 3932160 | tf_op jit(solution)/shard_map/all_to_all | solution.py:803
  15.8 0.0 copy-done.4
  15.8 0.1 reshape.19
  15.9 0.1 reshape.22.profile_ref
  16.0 1.7 %copy.17 = f32[16,2,75,75]{2,3,0,1:T(8,128)S(1)} copy(f32[16,2,75,75]{3,1,2,0:T(2,128)} %param.23) | data formatting | bytes 1440000 | tf_op args[11]
  17.8 0.1 pad.13.clone
  17.8 0.1 pad_add_fusion.flag_ref.refs_0_
  17.9 0.2 reduce-precision_convert_fusion
  18.1 0.0 copy-start
  18.2 0.0 copy-start.1
  18.2 0.0 copy-start.2
  18.2 0.9 maximum_maximum_fusion
  19.1 0.1 broadcast_select_fusion
  19.2 39.4 %all-to-all-done.message_ref = f32[32,120,128]{2,1,0:T(8,128)S(1)} async-done(((f32[32,120,128]{2,1,0:T(8,128)}), f32[32,120,128]{2,1,0:T(8,128)S(1)}, u32[]{:S(2)}, u32[]{:S(2)}) %all-to-all-start) | async-done | bytes 1966112 | tf_op jit(solution)/shard_map/all_to_all | solution.py:803
  58.6 0.0 copy-done
  58.6 0.0 copy-done.1
  58.6 0.0 copy-done.2
  58.6 4.6 %forcing_first.1 = (f32[152,512]{1,0:T(8,128)S(1)}, f32[16,512]{1,0:T(8,128)S(1)}, bf16[12,160,512]{2,1,0:T(8,128)(2,1)S(1)}, bf16[12,256,512]{2,1,0:T(8,128)(2,...) custom-call(s32[3]{0:T(128)S(1)} %pad_add_fusion.flag_ref.refs_0_, f32[32,120,128]{2,1,0:T(8,128)S(1)} %all-to-all-done.message_ref, ...), custom_call_target="tpu_custom_call" | custom-call | flops 6000000000 | bytes 8000000 | tf_op jit(solution)/shard_map/forcing_first/pallas_call | solution.py:368
  63.2 2.0 %collective-permute-start.1 = (f32[152,512]{1,0:T(8,128)S(1)}, f32[152,512]{1,0:T(8,128)S(1)}, u32[]{:S(2)}, u32[]{:S(2)}) collective-permute-start(f32[152,512]{1,0:T(8,128)S(1)} %get-tuple-element.39), channel_id=1, source_target_pairs={{0,4},{1,5},{2,6},{3,7},{4,0},{5,1},{6,2},{7,3},{8,12},{9,13},{10,... | collective-permute-start | bytes 933896 | tf_op jit(solution)/shard_map/ppermute | solution.py:839
  65.2 0.0 copy-start.3
  65.2 5.7 %forcing_rest.1 = (f32[16,160,512]{2,1,0:T(8,128)S(1)}, f32[152,512]{1,0:T(8,128)S(1)}, f32[80,128]{1,0:T(8,128)S(1)}) custom-call(s32[3]{0:T(128)S(1)} %pad_add_fusion.flag_ref.refs_0_, f32[160,1]{1,0:T(8,128)S(1)} %reshape.22.profile_ref, s32[16,512]{1,0:T(8,128)S(1)} %copy-done, f32[16,512]{1,0:T(8,128)S(1)} %copy-done.1, f32[16,512]{1,0:T(8,128)S(1)} %copy-done.2, ...), custom_call_target="tpu_custom_call" | custom-call | flops 6000000000 | bytes 8000000 | tf_op jit(solution)/shard_map/forcing_rest/pallas_call | solution.py:405
  70.9 3.2 %collective-permute-start.3 = (f32[80,128]{1,0:T(8,128)S(1)}, f32[80,128]{1,0:T(8,128)S(1)}, u32[]{:S(2)}, u32[]{:S(2)}) collective-permute-start(f32[80,128]{1,0:T(8,128)S(1)} %get-tuple-element.40.refs_0_), channel_id=1, source_target_pairs={{1,0},{2,1},{3,2},{0,3},{5,4},{6,5},{7,6},{4,7},{9,8},{10,9},{11,1... | collective-permute-start | bytes 122888 | tf_op jit(solution)/shard_map/ppermute | solution.py:842
  74.1 0.0 collective-permute-start.2
  74.1 0.0 copy-done.3
  74.1 1.9 %collective-permute-start = (f32[152,512]{1,0:T(8,128)S(1)}, f32[152,512]{1,0:T(8,128)S(1)}, u32[]{:S(2)}, u32[]{:S(2)}) collective-permute-start(f32[152,512]{1,0:T(8,128)S(1)} %get-tuple-element.38), channel_id=1, source_target_pairs={{4,8},{5,9},{6,10},{7,11},{8,4},{9,5},{10,6},{11,7},{12,16},{13,17... | collective-permute-start | bytes 933896 | tf_op jit(solution)/shard_map/ppermute | solution.py:839
  76.0 0.0 collective-permute-done.3.refs_6_.east_in
  76.0 0.3 collective-permute-done.2.refs_5_.west_in
  76.4 0.0 collective-permute-done.1.refs_4_.edge_in
  76.4 0.7 edge_weights.2.coef_ref.near_coef
  77.1 3.5 %diffusion_near.2 = (f32[8,160,512]{2,1,0:T(8,128)S(1)}, f32[152,512]{1,0:T(8,128)S(1)}, f32[80,128]{1,0:T(8,128)S(1)}) custom-call(s32[3]{0:T(128)S(1)} %pad_add_fusion.flag_ref.refs_0_, f32[16,160,512]{2,1,0:T(8,128)S(1)} %get-tuple-element.37.state_ref.other_ref, f32[16,160,512]{2,1,0:T(8,128)S(1)} %get-tuple-element.37.state_ref.other_ref, ...), custom_call_target="tpu_custom_call" | custom-call | flops 3000000000 | bytes 8000000 | tf_op jit(solution)/shard_map/diffusion_near/pallas_call | solution.py:606
  80.6 2.8 %collective-permute-start.5 = (f32[80,128]{1,0:T(8,128)S(1)}, f32[80,128]{1,0:T(8,128)S(1)}, u32[]{:S(2)}, u32[]{:S(2)}) collective-permute-start(f32[80,128]{1,0:T(8,128)S(1)} %get-tuple-element.41), channel_id=1, source_target_pairs={{1,0},{2,1},{3,2},{0,3},{5,4},{6,5},{7,6},{4,7},{9,8},{10,9},{11,1... | collective-permute-start | bytes 122888 | tf_op jit(solution)/shard_map/ppermute | solution.py:842
  83.3 0.0 collective-permute-start.4
  83.3 1.7 %collective-permute-start.7 = (f32[152,512]{1,0:T(8,128)S(1)}, f32[152,512]{1,0:T(8,128)S(1)}, u32[]{:S(2)}, u32[]{:S(2)}) collective-permute-start(f32[152,512]{1,0:T(8,128)S(1)} %get-tuple-element.45), channel_id=1, source_target_pairs={{0,4},{1,5},{2,6},{3,7},{4,0},{5,1},{6,2},{7,3},{8,12},{9,13},{10,... | collective-permute-start | bytes 933896 | tf_op jit(solution)/shard_map/ppermute | solution.py:839
  85.0 0.0 collective-permute-done.refs_4_.edge_in
  85.0 0.7 edge_weights.3.coef_ref.far_coef
  85.7 0.0 collective-permute-done.5.east_in
  85.7 0.0 collective-permute-done.4.west_in
  85.7 3.7 %diffusion_far.2 = (f32[8,160,512]{2,1,0:T(8,128)S(1)}, f32[152,512]{1,0:T(8,128)S(1)}, f32[80,128]{1,0:T(8,128)S(1)}) custom-call(s32[3]{0:T(128)S(1)} %pad_add_fusion.flag_ref.refs_0_, f32[16,160,512]{2,1,0:T(8,128)S(1)} %get-tuple-element.37.state_ref.other_ref, f32[16,160,512]{2,1,0:T(8,128)S(1)} %get-tuple-element.37.state_ref.other_ref, ...), custom_call_target="tpu_custom_call" | custom-call | flops 3000000000 | bytes 8000000 | tf_op jit(solution)/shard_map/diffusion_far/pallas_call | solution.py:606
  89.5 2.9 %collective-permute-start.6 = (f32[152,512]{1,0:T(8,128)S(1)}, f32[152,512]{1,0:T(8,128)S(1)}, u32[]{:S(2)}, u32[]{:S(2)}) collective-permute-start(f32[152,512]{1,0:T(8,128)S(1)} %get-tuple-element.44), channel_id=1, source_target_pairs={{4,8},{5,9},{6,10},{7,11},{8,4},{9,5},{10,6},{11,7},{12,16},{13,17... | collective-permute-start | bytes 933896 | tf_op jit(solution)/shard_map/ppermute | solution.py:839
  92.3 0.0 collective-permute-done.7.edge_in
  92.3 3.5 %diffusion_near.3 = (f32[8,160,512]{2,1,0:T(8,128)S(1)}, f32[152,512]{1,0:T(8,128)S(1)}, f32[80,128]{1,0:T(8,128)S(1)}) custom-call(s32[3]{0:T(128)S(1)} %pad_add_fusion.flag_ref.refs_0_, f32[8,160,512]{2,1,0:T(8,128)S(1)} %get-tuple-element.43.state_ref.other_ref, f32[8,160,512]{2,1,0:T(8,128)S(1)} %get-tuple-element.42.other_ref.state_ref, ...), custom_call_target="tpu_custom_call" | custom-call | flops 3000000000 | bytes 8000000 | tf_op jit(solution)/shard_map/diffusion_near/pallas_call | solution.py:606
  95.9 3.0 %collective-permute-start.9 = (f32[80,128]{1,0:T(8,128)S(1)}, f32[80,128]{1,0:T(8,128)S(1)}, u32[]{:S(2)}, u32[]{:S(2)}) collective-permute-start(f32[80,128]{1,0:T(8,128)S(1)} %get-tuple-element.47), channel_id=1, source_target_pairs={{1,0},{2,1},{3,2},{0,3},{5,4},{6,5},{7,6},{4,7},{9,8},{10,9},{11,1... | collective-permute-start | bytes 122888 | tf_op jit(solution)/shard_map/ppermute | solution.py:842
  98.9 0.1 collective-permute-start.8
  99.0 1.0 collective-permute-start.13
  100.0 0.0 collective-permute-done.6.edge_in
  100.0 0.9 collective-permute-done.9.east_in.near_east
  100.9 0.0 collective-permute-done.8.west_in.near_west
  100.9 3.5 %diffusion_far.3 = (f32[8,160,512]{2,1,0:T(8,128)S(1)}, f32[152,512]{1,0:T(8,128)S(1)}, f32[80,128]{1,0:T(8,128)S(1)}) custom-call(s32[3]{0:T(128)S(1)} %pad_add_fusion.flag_ref.refs_0_, f32[8,160,512]{2,1,0:T(8,128)S(1)} %get-tuple-element.42.other_ref.state_ref, f32[8,160,512]{2,1,0:T(8,128)S(1)} %get-tuple-element.43.state_ref.other_ref, ...), custom_call_target="tpu_custom_call" | custom-call | flops 3000000000 | bytes 8000000 | tf_op jit(solution)/shard_map/diffusion_far/pallas_call | solution.py:606
  104.4 1.6 %collective-permute-start.12 = (f32[80,128]{1,0:T(8,128)S(1)}, f32[80,128]{1,0:T(8,128)S(1)}, u32[]{:S(2)}, u32[]{:S(2)}) collective-permute-start(f32[80,128]{1,0:T(8,128)S(1)} %get-tuple-element.50), channel_id=1, source_target_pairs={{1,0},{2,1},{3,2},{0,3},{5,4},{6,5},{7,6},{4,7},{9,8},{10,9},{11,1... | collective-permute-start | bytes 122888 | tf_op jit(solution)/shard_map/ppermute | solution.py:842
  106.1 2.9 %collective-permute-start.11 = (f32[80,128]{1,0:T(8,128)S(1)}, f32[80,128]{1,0:T(8,128)S(1)}, u32[]{:S(2)}, u32[]{:S(2)}) collective-permute-start(f32[80,128]{1,0:T(8,128)S(1)} %get-tuple-element.50), channel_id=1, source_target_pairs={{0,1},{1,2},{2,3},{3,0},{4,5},{5,6},{6,7},{7,4},{8,9},{9,10},{10,1... | collective-permute-start | bytes 122888 | tf_op jit(solution)/shard_map/ppermute | solution.py:842
  108.9 1.9 %collective-permute-start.10 = (f32[152,512]{1,0:T(8,128)S(1)}, f32[152,512]{1,0:T(8,128)S(1)}, u32[]{:S(2)}, u32[]{:S(2)}) collective-permute-start(f32[152,512]{1,0:T(8,128)S(1)} %get-tuple-element.49), channel_id=1, source_target_pairs={{4,8},{5,9},{6,10},{7,11},{8,4},{9,5},{10,6},{11,7},{12,16},{13,17... | collective-permute-start | bytes 933896 | tf_op jit(solution)/shard_map/ppermute | solution.py:839
  110.9 0.0 collective-permute-done.12.far_east.east_in
  110.9 0.0 collective-permute-done.11.far_west.west_in
  110.9 0.0 collective-permute-done.13.edge_in
  110.9 6.7 %last_inner.1 = (f32[150,16,512]{2,1,0:T(8,128)}, f32[2,75,8,512]{3,2,1,0:T(8,128)S(1)}) custom-call(s32[3]{0:T(128)S(1)} %pad_add_fusion.flag_ref.refs_0_, f32[8,160,512]{2,1,0:T(8,128)S(1)} %get-tuple-element.51.near_ref, f32[8,160,512]{2,1,0:T(8,128)S(1)} %get-tuple-element.48.far_ref, f32[152,512]{1,0:T(8,128)S(1)} %collective-permute-done.13.edge_in, ...), custom_call_target="tpu_custom_call" | custom-call | flops 6000000000 | bytes 16000000 | tf_op jit(solution)/shard_map/last_inner/pallas_call | solution.py:689
  117.6 3.4 %collective-permute-done.10.edge_in = f32[152,512]{1,0:T(8,128)S(1)} collective-permute-done((f32[152,512]{1,0:T(8,128)S(1)}, f32[152,512]{1,0:T(8,128)S(1)}, u32[]{:S(2)}, u32[]{:S(2)}) %collective-permute-start.10) | collective-permute-done | bytes 311328 | tf_op jit(solution)/shard_map/ppermute | solution.py:839
  121.0 2.6 %last_outer.1 = f32[150,16,512]{2,1,0:T(8,128)} custom-call(s32[3]{0:T(128)S(1)} %pad_add_fusion.flag_ref.refs_0_, f32[8,160,512]{2,1,0:T(8,128)S(1)} %get-tuple-element.48.far_ref, f32[152,512]{1,0:T(8,128)S(1)} %collective-permute-done.10.edge_in, f32[80,128]{1,0:T(8,128)S(1)} %collective-permute-done.11.far_west.west_in, ...), custom_call_target="tpu_custom_call", output_to_operand_aliasing={{}: (10, {})} | custom-call | tf_op jit(solution)/shard_map/last_outer/pallas_call | solution.py:740
  (4 shorter events, 0.0 us)
Async XLA Ops:
  9.5 6.3 %copy-start.4 = (f32[150]{0:T(256)S(1)}, f32[150]{0:T(256)}, u32[]{:S(2)}) copy-start(f32[150]{0:T(256)} %param.18) | copy-start | bytes 1804
  9.5 49.1 %all-to-all-start = ((f32[32,120,128]{2,1,0:T(8,128)}), f32[32,120,128]{2,1,0:T(8,128)S(1)}, u32[]{:S(2)}, u32[]{:S(2)}) async-start(f32[32,120,128]{2,1,0:T(8,128)} %send_tables.1), calls=%async_computation | async-start | bytes 3932160 | tf_op jit(solution)/shard_map/all_to_all | solution.py:803
  18.1 40.4 %copy-start = (s32[16,512]{1,0:T(8,128)S(1)}, s32[16,512]{1,0:T(8,128)}, u32[]{:S(2)}) copy-start(s32[16,512]{1,0:T(8,128)} %mask_ref.3) | copy-start | bytes 98308
  18.2 40.4 %copy-start.1 = (f32[16,512]{1,0:T(8,128)S(1)}, f32[16,512]{1,0:T(8,128)}, u32[]{:S(2)}) copy-start(f32[16,512]{1,0:T(8,128)} %refs_2_.3) | copy-start | bytes 98308
  18.2 40.4 %copy-start.2 = (f32[16,512]{1,0:T(8,128)S(1)}, f32[16,512]{1,0:T(8,128)}, u32[]{:S(2)}) copy-start(f32[16,512]{1,0:T(8,128)} %refs_3_.5) | copy-start | bytes 98308
  63.2 13.2 %collective-permute-start.1 = (f32[152,512]{1,0:T(8,128)S(1)}, f32[152,512]{1,0:T(8,128)S(1)}, u32[]{:S(2)}, u32[]{:S(2)}) collective-permute-start(f32[152,512]{1,0:T(8,128)S(1)} %get-tuple-element.39), channel_id=1, source_target_pairs={{0,4},{1,5},{2,6},{3,7},{4,0},{5,1},{6,2},{7,3},{8,12},{9,13},{10,... | collective-permute-start | bytes 933896 | tf_op jit(solution)/shard_map/ppermute | solution.py:839
  65.2 8.9 %copy-start.3 = (s32[512]{0:T(512)S(1)}, s32[512]{0:T(512)}, u32[]{:S(2)}) copy-start(s32[512]{0:T(512)} %param.22) | copy-start | bytes 6148
  70.9 5.1 %collective-permute-start.3 = (f32[80,128]{1,0:T(8,128)S(1)}, f32[80,128]{1,0:T(8,128)S(1)}, u32[]{:S(2)}, u32[]{:S(2)}) collective-permute-start(f32[80,128]{1,0:T(8,128)S(1)} %get-tuple-element.40.refs_0_), channel_id=1, source_target_pairs={{1,0},{2,1},{3,2},{0,3},{5,4},{6,5},{7,6},{4,7},{9,8},{10,9},{11,1... | collective-permute-start | bytes 122888 | tf_op jit(solution)/shard_map/ppermute | solution.py:842
  74.1 2.3 %collective-permute-start.2 = (f32[80,128]{1,0:T(8,128)S(1)}, f32[80,128]{1,0:T(8,128)S(1)}, u32[]{:S(2)}, u32[]{:S(2)}) collective-permute-start(f32[80,128]{1,0:T(8,128)S(1)} %get-tuple-element.40.refs_0_), channel_id=1, source_target_pairs={{0,1},{1,2},{2,3},{3,0},{4,5},{5,6},{6,7},{7,4},{8,9},{9,10},{10,1... | collective-permute-start | bytes 122888 | tf_op jit(solution)/shard_map/ppermute | solution.py:842
  74.1 10.9 %collective-permute-start = (f32[152,512]{1,0:T(8,128)S(1)}, f32[152,512]{1,0:T(8,128)S(1)}, u32[]{:S(2)}, u32[]{:S(2)}) collective-permute-start(f32[152,512]{1,0:T(8,128)S(1)} %get-tuple-element.38), channel_id=1, source_target_pairs={{4,8},{5,9},{6,10},{7,11},{8,4},{9,5},{10,6},{11,7},{12,16},{13,17... | collective-permute-start | bytes 933896 | tf_op jit(solution)/shard_map/ppermute | solution.py:839
  80.6 5.2 %collective-permute-start.5 = (f32[80,128]{1,0:T(8,128)S(1)}, f32[80,128]{1,0:T(8,128)S(1)}, u32[]{:S(2)}, u32[]{:S(2)}) collective-permute-start(f32[80,128]{1,0:T(8,128)S(1)} %get-tuple-element.41), channel_id=1, source_target_pairs={{1,0},{2,1},{3,2},{0,3},{5,4},{6,5},{7,6},{4,7},{9,8},{10,9},{11,1... | collective-permute-start | bytes 122888 | tf_op jit(solution)/shard_map/ppermute | solution.py:842
  83.3 2.4 %collective-permute-start.4 = (f32[80,128]{1,0:T(8,128)S(1)}, f32[80,128]{1,0:T(8,128)S(1)}, u32[]{:S(2)}, u32[]{:S(2)}) collective-permute-start(f32[80,128]{1,0:T(8,128)S(1)} %get-tuple-element.41), channel_id=1, source_target_pairs={{0,1},{1,2},{2,3},{3,0},{4,5},{5,6},{6,7},{7,4},{8,9},{9,10},{10,1... | collective-permute-start | bytes 122888 | tf_op jit(solution)/shard_map/ppermute | solution.py:842
  83.3 9.0 %collective-permute-start.7 = (f32[152,512]{1,0:T(8,128)S(1)}, f32[152,512]{1,0:T(8,128)S(1)}, u32[]{:S(2)}, u32[]{:S(2)}) collective-permute-start(f32[152,512]{1,0:T(8,128)S(1)} %get-tuple-element.45), channel_id=1, source_target_pairs={{0,4},{1,5},{2,6},{3,7},{4,0},{5,1},{6,2},{7,3},{8,12},{9,13},{10,... | collective-permute-start | bytes 933896 | tf_op jit(solution)/shard_map/ppermute | solution.py:839
  89.5 10.6 %collective-permute-start.6 = (f32[152,512]{1,0:T(8,128)S(1)}, f32[152,512]{1,0:T(8,128)S(1)}, u32[]{:S(2)}, u32[]{:S(2)}) collective-permute-start(f32[152,512]{1,0:T(8,128)S(1)} %get-tuple-element.44), channel_id=1, source_target_pairs={{4,8},{5,9},{6,10},{7,11},{8,4},{9,5},{10,6},{11,7},{12,16},{13,17... | collective-permute-start | bytes 933896 | tf_op jit(solution)/shard_map/ppermute | solution.py:839
  95.9 5.0 %collective-permute-start.9 = (f32[80,128]{1,0:T(8,128)S(1)}, f32[80,128]{1,0:T(8,128)S(1)}, u32[]{:S(2)}, u32[]{:S(2)}) collective-permute-start(f32[80,128]{1,0:T(8,128)S(1)} %get-tuple-element.47), channel_id=1, source_target_pairs={{1,0},{2,1},{3,2},{0,3},{5,4},{6,5},{7,6},{4,7},{9,8},{10,9},{11,1... | collective-permute-start | bytes 122888 | tf_op jit(solution)/shard_map/ppermute | solution.py:842
  98.9 2.0 %collective-permute-start.8 = (f32[80,128]{1,0:T(8,128)S(1)}, f32[80,128]{1,0:T(8,128)S(1)}, u32[]{:S(2)}, u32[]{:S(2)}) collective-permute-start(f32[80,128]{1,0:T(8,128)S(1)} %get-tuple-element.47), channel_id=1, source_target_pairs={{0,1},{1,2},{2,3},{3,0},{4,5},{5,6},{6,7},{7,4},{8,9},{9,10},{10,1... | collective-permute-start | bytes 122888 | tf_op jit(solution)/shard_map/ppermute | solution.py:842
  99.0 11.9 %collective-permute-start.13 = (f32[152,512]{1,0:T(8,128)S(1)}, f32[152,512]{1,0:T(8,128)S(1)}, u32[]{:S(2)}, u32[]{:S(2)}) collective-permute-start(f32[152,512]{1,0:T(8,128)S(1)} %get-tuple-element.52), channel_id=1, source_target_pairs={{0,4},{1,5},{2,6},{3,7},{4,0},{5,1},{6,2},{7,3},{8,12},{9,13},{10,... | collective-permute-start | bytes 933896 | tf_op jit(solution)/shard_map/ppermute | solution.py:839
  104.4 6.4 %collective-permute-start.12 = (f32[80,128]{1,0:T(8,128)S(1)}, f32[80,128]{1,0:T(8,128)S(1)}, u32[]{:S(2)}, u32[]{:S(2)}) collective-permute-start(f32[80,128]{1,0:T(8,128)S(1)} %get-tuple-element.50), channel_id=1, source_target_pairs={{1,0},{2,1},{3,2},{0,3},{5,4},{6,5},{7,6},{4,7},{9,8},{10,9},{11,1... | collective-permute-start | bytes 122888 | tf_op jit(solution)/shard_map/ppermute | solution.py:842
  106.1 4.8 %collective-permute-start.11 = (f32[80,128]{1,0:T(8,128)S(1)}, f32[80,128]{1,0:T(8,128)S(1)}, u32[]{:S(2)}, u32[]{:S(2)}) collective-permute-start(f32[80,128]{1,0:T(8,128)S(1)} %get-tuple-element.50), channel_id=1, source_target_pairs={{0,1},{1,2},{2,3},{3,0},{4,5},{5,6},{6,7},{7,4},{8,9},{9,10},{10,1... | collective-permute-start | bytes 122888 | tf_op jit(solution)/shard_map/ppermute | solution.py:842
  108.9 12.1 %collective-permute-start.10 = (f32[152,512]{1,0:T(8,128)S(1)}, f32[152,512]{1,0:T(8,128)S(1)}, u32[]{:S(2)}, u32[]{:S(2)}) collective-permute-start(f32[152,512]{1,0:T(8,128)S(1)} %get-tuple-element.49), channel_id=1, source_target_pairs={{4,8},{5,9},{6,10},{7,11},{8,4},{9,5},{10,6},{11,7},{12,16},{13,17... | collective-permute-start | bytes 933896 | tf_op jit(solution)/shard_map/ppermute | solution.py:839

commit v3 on v2

--- a/solution.py
+++ b/solution.py
@@ -315,9 +315,9 @@
         for i in range(1, batch):
             extent = jnp.maximum(extent, bound_ref[2 * chunks[i] + 1] - least[i])
 
-        def add_runs(span, turn, inner):
+        def add_runs(span, offset_rows, inner):
             for i, chunk in enumerate(chunks):
-                begin = least[i] + turn * span
+                begin = least[i] + offset_rows
                 base = jnp.minimum(begin, row_count - span)
                 here = rows_ref[chunk][0:1]
                 here = jnp.where(here >= begin, here, -1)
@@ -326,10 +326,13 @@
                     state[base + offset] += product[2 * PAD * offset : 2 * PAD * (offset + 1)]
             return inner
 
-        once = (extent >= 0) & (extent < narrow)
-        lax.fori_loop(0, once.astype(jnp.int32), lambda t, c: add_runs(narrow, t, c), 0)
-        turns = jnp.where(extent < narrow, 0, lax.div(extent + wide, wide))
-        lax.fori_loop(0, turns, lambda t, c: add_runs(wide, t, c), 0)
+        wanted = jnp.maximum(extent + 1, 0)
+        full = lax.div(wanted, wide)
+        rest = wanted - wide * full
+        wide_turns = full + (rest > narrow).astype(jnp.int32)
+        narrow_turns = ((rest > 0) & (rest <= narrow)).astype(jnp.int32)
+        lax.fori_loop(0, wide_turns, lambda t, c: add_runs(wide, t * wide, c), 0)
+        lax.fori_loop(0, narrow_turns, lambda t, c: add_runs(narrow, full * wide, c), 0)
         return carry
 
     lax.fori_loop(0, count // batch, step, 0)

time: 124 us -> 126 us (1.016)
  starting transfers between devices: 31.3 us -> 33.2 us
    ppermute x6, waiting for transfers between devices: 3.43 us -> 0.92 us  [swap(): return lax.ppermute(edge, ('ja', 'ia'), swaps[which])]
    ppermute x4, waiting for transfers between devices: 0.89 us -> 2.61 us  [pass_columns(): lax.ppermute(cols, 'ia', ring_west)]
    ppermute x4, starting transfers between devices: 2.96 us -> 4.56 us  [pass_columns(): lax.ppermute(cols, 'ia', ring_east)]
  transfers between devices with their start and end apart: 15 -> 15, of which waited for: 4 -> 5; matrix products, arithmetic and copies ran while one was open for 3% -> 3% of each run, Pallas kernels for 23% -> 22%
where the time goes in v3:
time: 126 us; the launch traced here: 125 us
  Pallas kernels  44.7 us (35%)
  waiting for transfers between devices  43.4 us (34%)
  starting transfers between devices  33.2 us (26%)
  local copies, waits for them, and re-layouts  2.04 us (2%)
  other arithmetic  1.29 us (1%)
    all_to_all x1, waiting for transfers between devices, body(): lax.all_to_all(message, ('ja', 'ia'), split_axis=0, concat_axis=0, tiled=...  39.4 us
    pallas_call x4, Pallas kernels, diffuse(): pl.pallas_call(kernel, in_specs=in_place(8 + len(far_cols)), out_shape=ha...  14.2 us
    ppermute x6, starting transfers between devices, swap(): return lax.ppermute(edge, ('ja', 'ia'), swaps[which])  11.3 us
    ppermute x4, starting transfers between devices, pass_columns(): lax.ppermute(cols, 'ia', ring_west)  11 us
    pallas_call x1, Pallas kernels, send_tables(): pl.pallas_call(kernel, grid=(devices // per_step,), in_specs=[whole(x) fo...  9.45 us
    pallas_call x1, Pallas kernels, last_inner(): pl.pallas_call(kernel, in_specs=in_place(13), out_specs=[pl.BlockSpec(mem...  6.73 us
    all_to_all x1, starting transfers between devices, body(): lax.all_to_all(message, ('ja', 'ia'), split_axis=0, concat_axis=0, tiled=...  6.31 us
    pallas_call x1, Pallas kernels, rest_forcing(): pl.pallas_call(kernel, in_specs=in_place(8) + [pl.BlockSpec(memory_space=...  5.7 us
  transfers between devices with their start and end apart: 15, of which 5 were waited for; matrix products, arithmetic and copies ran while one was open for 3% of the time, Pallas kernels for 22%

profile of v3, /device:TPU:13, one launch (start us, length us, event | category | flops | bytes accessed | tf_op | source)
XLA Modules:
  0.0 125.1 jit_solution(5895084732250787049)
XLA Ops:
  0.0 9.5 %send_tables.1 = f32[32,120,128]{2,1,0:T(8,128)} custom-call(f32[150,1024]{1,0:T(8,128)} %bitcast.11, s32[1,1024]{1,0:T(1,128)} %bitcast.12, s32[1,1024]{1,0:T(1,128)} %bitcast.13, f32[768]{0:T(1024)} %refs_3_.3, s32[768]{0:T(1024)} %refs_4_.1, s32[1,768]{1,0:T(1,128)} %bitcast.14), custom_call_target="tpu_custom_call" | custom-call | tf_op jit(solution)/shard_map/send_tables/pallas_call | solution.py:163
  9.5 0.0 copy-start.4
  9.5 6.3 %all-to-all-start = ((f32[32,120,128]{2,1,0:T(8,128)}), f32[32,120,128]{2,1,0:T(8,128)S(1)}, u32[]{:S(2)}, u32[]{:S(2)}) async-start(f32[32,120,128]{2,1,0:T(8,128)} %send_tables.1), calls=%async_computation | async-start | bytes 3932160 | tf_op jit(solution)/shard_map/all_to_all | solution.py:806
  15.8 0.0 copy-done.4
  15.8 0.1 reshape.19
  15.9 0.1 reshape.22.profile_ref
  16.0 1.7 %copy.17 = f32[16,2,75,75]{2,3,0,1:T(8,128)S(1)} copy(f32[16,2,75,75]{3,1,2,0:T(2,128)} %param.23) | data formatting | bytes 1440000 | tf_op args[11]
  17.8 0.1 pad.13.clone
  17.8 0.1 pad_add_fusion.flag_ref.refs_0_
  17.9 0.2 reduce-precision_convert_fusion
  18.1 0.0 copy-start
  18.2 0.0 copy-start.1
  18.2 0.0 copy-start.2
  18.2 0.9 maximum_maximum_fusion
  19.1 0.1 broadcast_select_fusion
  19.2 39.4 %all-to-all-done.message_ref = f32[32,120,128]{2,1,0:T(8,128)S(1)} async-done(((f32[32,120,128]{2,1,0:T(8,128)}), f32[32,120,128]{2,1,0:T(8,128)S(1)}, u32[]{:S(2)}, u32[]{:S(2)}) %all-to-all-start) | async-done | bytes 1966112 | tf_op jit(solution)/shard_map/all_to_all | solution.py:806
  58.6 0.0 copy-done
  58.6 0.0 copy-done.1
  58.6 0.0 copy-done.2
  58.6 4.6 %forcing_first.1 = (f32[152,512]{1,0:T(8,128)S(1)}, f32[16,512]{1,0:T(8,128)S(1)}, bf16[12,160,512]{2,1,0:T(8,128)(2,1)S(1)}, bf16[12,256,512]{2,1,0:T(8,128)(2,...) custom-call(s32[3]{0:T(128)S(1)} %pad_add_fusion.flag_ref.refs_0_, f32[32,120,128]{2,1,0:T(8,128)S(1)} %all-to-all-done.message_ref, ...), custom_call_target="tpu_custom_call" | custom-call | flops 6000000000 | bytes 8000000 | tf_op jit(solution)/shard_map/forcing_first/pallas_call | solution.py:371
  63.2 2.0 %collective-permute-start.1 = (f32[152,512]{1,0:T(8,128)S(1)}, f32[152,512]{1,0:T(8,128)S(1)}, u32[]{:S(2)}, u32[]{:S(2)}) collective-permute-start(f32[152,512]{1,0:T(8,128)S(1)} %get-tuple-element.39), channel_id=1, source_target_pairs={{0,4},{1,5},{2,6},{3,7},{4,0},{5,1},{6,2},{7,3},{8,12},{9,13},{10,... | collective-permute-start | bytes 933896 | tf_op jit(solution)/shard_map/ppermute | solution.py:842
  65.2 0.0 copy-start.3
  65.2 5.7 %forcing_rest.1 = (f32[16,160,512]{2,1,0:T(8,128)S(1)}, f32[152,512]{1,0:T(8,128)S(1)}, f32[80,128]{1,0:T(8,128)S(1)}) custom-call(s32[3]{0:T(128)S(1)} %pad_add_fusion.flag_ref.refs_0_, f32[160,1]{1,0:T(8,128)S(1)} %reshape.22.profile_ref, s32[16,512]{1,0:T(8,128)S(1)} %copy-done, f32[16,512]{1,0:T(8,128)S(1)} %copy-done.1, f32[16,512]{1,0:T(8,128)S(1)} %copy-done.2, ...), custom_call_target="tpu_custom_call" | custom-call | flops 6000000000 | bytes 8000000 | tf_op jit(solution)/shard_map/forcing_rest/pallas_call | solution.py:408
  70.9 0.1 collective-permute-start.3
  71.0 1.7 %collective-permute-start.2 = (f32[80,128]{1,0:T(8,128)S(1)}, f32[80,128]{1,0:T(8,128)S(1)}, u32[]{:S(2)}, u32[]{:S(2)}) collective-permute-start(f32[80,128]{1,0:T(8,128)S(1)} %get-tuple-element.40.refs_0_), channel_id=1, source_target_pairs={{0,1},{1,2},{2,3},{3,0},{4,5},{5,6},{6,7},{7,4},{8,9},{9,10},{10,1... | collective-permute-start | bytes 122888 | tf_op jit(solution)/shard_map/ppermute | solution.py:845
  72.7 0.0 copy-done.3
  72.7 2.9 %collective-permute-start = (f32[152,512]{1,0:T(8,128)S(1)}, f32[152,512]{1,0:T(8,128)S(1)}, u32[]{:S(2)}, u32[]{:S(2)}) collective-permute-start(f32[152,512]{1,0:T(8,128)S(1)} %get-tuple-element.38), channel_id=1, source_target_pairs={{4,8},{5,9},{6,10},{7,11},{8,4},{9,5},{10,6},{11,7},{12,16},{13,17... | collective-permute-start | bytes 933896 | tf_op jit(solution)/shard_map/ppermute | solution.py:842
  75.6 0.0 collective-permute-done.3.refs_6_.east_in
  75.6 0.0 collective-permute-done.2.refs_5_.west_in
  75.6 0.0 collective-permute-done.1.refs_4_.edge_in
  75.7 0.7 edge_weights.2.coef_ref.near_coef
  76.4 3.5 %diffusion_near.2 = (f32[8,160,512]{2,1,0:T(8,128)S(1)}, f32[152,512]{1,0:T(8,128)S(1)}, f32[80,128]{1,0:T(8,128)S(1)}) custom-call(s32[3]{0:T(128)S(1)} %pad_add_fusion.flag_ref.refs_0_, f32[16,160,512]{2,1,0:T(8,128)S(1)} %get-tuple-element.37.state_ref.other_ref, f32[16,160,512]{2,1,0:T(8,128)S(1)} %get-tuple-element.37.state_ref.other_ref, ...), custom_call_target="tpu_custom_call" | custom-call | flops 3000000000 | bytes 8000000 | tf_op jit(solution)/shard_map/diffusion_near/pallas_call | solution.py:609
  79.9 6.1 %collective-permute-start.5 = (f32[80,128]{1,0:T(8,128)S(1)}, f32[80,128]{1,0:T(8,128)S(1)}, u32[]{:S(2)}, u32[]{:S(2)}) collective-permute-start(f32[80,128]{1,0:T(8,128)S(1)} %get-tuple-element.41), channel_id=1, source_target_pairs={{1,0},{2,1},{3,2},{0,3},{5,4},{6,5},{7,6},{4,7},{9,8},{10,9},{11,1... | collective-permute-start | bytes 122888 | tf_op jit(solution)/shard_map/ppermute | solution.py:845
  86.0 0.1 collective-permute-start.4
  86.1 0.0 collective-permute-start.7
  86.1 0.0 collective-permute-done.refs_4_.edge_in
  86.1 0.7 edge_weights.3.coef_ref.far_coef
  86.8 0.9 collective-permute-done.5.east_in
  87.7 0.4 collective-permute-done.4.west_in
  88.2 3.7 %diffusion_far.2 = (f32[8,160,512]{2,1,0:T(8,128)S(1)}, f32[152,512]{1,0:T(8,128)S(1)}, f32[80,128]{1,0:T(8,128)S(1)}) custom-call(s32[3]{0:T(128)S(1)} %pad_add_fusion.flag_ref.refs_0_, f32[16,160,512]{2,1,0:T(8,128)S(1)} %get-tuple-element.37.state_ref.other_ref, f32[16,160,512]{2,1,0:T(8,128)S(1)} %get-tuple-element.37.state_ref.other_ref, ...), custom_call_target="tpu_custom_call" | custom-call | flops 3000000000 | bytes 8000000 | tf_op jit(solution)/shard_map/diffusion_far/pallas_call | solution.py:609
  91.9 2.1 %collective-permute-start.6 = (f32[152,512]{1,0:T(8,128)S(1)}, f32[152,512]{1,0:T(8,128)S(1)}, u32[]{:S(2)}, u32[]{:S(2)}) collective-permute-start(f32[152,512]{1,0:T(8,128)S(1)} %get-tuple-element.44), channel_id=1, source_target_pairs={{4,8},{5,9},{6,10},{7,11},{8,4},{9,5},{10,6},{11,7},{12,16},{13,17... | collective-permute-start | bytes 933896 | tf_op jit(solution)/shard_map/ppermute | solution.py:842
  94.0 0.0 collective-permute-done.7.edge_in
  94.0 3.5 %diffusion_near.3 = (f32[8,160,512]{2,1,0:T(8,128)S(1)}, f32[152,512]{1,0:T(8,128)S(1)}, f32[80,128]{1,0:T(8,128)S(1)}) custom-call(s32[3]{0:T(128)S(1)} %pad_add_fusion.flag_ref.refs_0_, f32[8,160,512]{2,1,0:T(8,128)S(1)} %get-tuple-element.43.state_ref.other_ref, f32[8,160,512]{2,1,0:T(8,128)S(1)} %get-tuple-element.42.other_ref.state_ref, ...), custom_call_target="tpu_custom_call" | custom-call | flops 3000000000 | bytes 8000000 | tf_op jit(solution)/shard_map/diffusion_near/pallas_call | solution.py:609
  97.6 2.8 %collective-permute-start.9 = (f32[80,128]{1,0:T(8,128)S(1)}, f32[80,128]{1,0:T(8,128)S(1)}, u32[]{:S(2)}, u32[]{:S(2)}) collective-permute-start(f32[80,128]{1,0:T(8,128)S(1)} %get-tuple-element.47), channel_id=1, source_target_pairs={{1,0},{2,1},{3,2},{0,3},{5,4},{6,5},{7,6},{4,7},{9,8},{10,9},{11,1... | collective-permute-start | bytes 122888 | tf_op jit(solution)/shard_map/ppermute | solution.py:845
  100.4 1.9 %collective-permute-start.8 = (f32[80,128]{1,0:T(8,128)S(1)}, f32[80,128]{1,0:T(8,128)S(1)}, u32[]{:S(2)}, u32[]{:S(2)}) collective-permute-start(f32[80,128]{1,0:T(8,128)S(1)} %get-tuple-element.47), channel_id=1, source_target_pairs={{0,1},{1,2},{2,3},{3,0},{4,5},{5,6},{6,7},{7,4},{8,9},{9,10},{10,1... | collective-permute-start | bytes 122888 | tf_op jit(solution)/shard_map/ppermute | solution.py:845
  102.3 0.0 collective-permute-start.13
  102.3 0.0 collective-permute-done.6.edge_in
  102.3 1.7 %collective-permute-done.9.east_in.near_east = f32[80,128]{1,0:T(8,128)S(1)} collective-permute-done((f32[80,128]{1,0:T(8,128)S(1)}, f32[80,128]{1,0:T(8,128)S(1)}, u32[]{:S(2)}, u32[]{:S(2)}) %collective-permute-start.9) | collective-permute-done | bytes 40992 | tf_op jit(solution)/shard_map/ppermute | solution.py:845
  104.1 0.0 collective-permute-done.8.west_in.near_west
  104.1 3.5 %diffusion_far.3 = (f32[8,160,512]{2,1,0:T(8,128)S(1)}, f32[152,512]{1,0:T(8,128)S(1)}, f32[80,128]{1,0:T(8,128)S(1)}) custom-call(s32[3]{0:T(128)S(1)} %pad_add_fusion.flag_ref.refs_0_, f32[8,160,512]{2,1,0:T(8,128)S(1)} %get-tuple-element.42.other_ref.state_ref, f32[8,160,512]{2,1,0:T(8,128)S(1)} %get-tuple-element.43.state_ref.other_ref, ...), custom_call_target="tpu_custom_call" | custom-call | flops 3000000000 | bytes 8000000 | tf_op jit(solution)/shard_map/diffusion_far/pallas_call | solution.py:609
  107.6 1.9 %collective-permute-start.12 = (f32[80,128]{1,0:T(8,128)S(1)}, f32[80,128]{1,0:T(8,128)S(1)}, u32[]{:S(2)}, u32[]{:S(2)}) collective-permute-start(f32[80,128]{1,0:T(8,128)S(1)} %get-tuple-element.50), channel_id=1, source_target_pairs={{1,0},{2,1},{3,2},{0,3},{5,4},{6,5},{7,6},{4,7},{9,8},{10,9},{11,1... | collective-permute-start | bytes 122888 | tf_op jit(solution)/shard_map/ppermute | solution.py:845
  109.5 0.9 collective-permute-start.11
  110.3 4.3 %collective-permute-start.10 = (f32[152,512]{1,0:T(8,128)S(1)}, f32[152,512]{1,0:T(8,128)S(1)}, u32[]{:S(2)}, u32[]{:S(2)}) collective-permute-start(f32[152,512]{1,0:T(8,128)S(1)} %get-tuple-element.49), channel_id=1, source_target_pairs={{4,8},{5,9},{6,10},{7,11},{8,4},{9,5},{10,6},{11,7},{12,16},{13,17... | collective-permute-start | bytes 933896 | tf_op jit(solution)/shard_map/ppermute | solution.py:842
  114.7 0.0 collective-permute-done.12.far_east.east_in
  114.7 0.0 collective-permute-done.11.far_west.west_in
  114.7 0.0 collective-permute-done.13.edge_in
  114.7 6.7 %last_inner.1 = (f32[150,16,512]{2,1,0:T(8,128)}, f32[2,75,8,512]{3,2,1,0:T(8,128)S(1)}) custom-call(s32[3]{0:T(128)S(1)} %pad_add_fusion.flag_ref.refs_0_, f32[8,160,512]{2,1,0:T(8,128)S(1)} %get-tuple-element.51.near_ref, f32[8,160,512]{2,1,0:T(8,128)S(1)} %get-tuple-element.48.far_ref, f32[152,512]{1,0:T(8,128)S(1)} %collective-permute-done.13.edge_in, ...), custom_call_target="tpu_custom_call" | custom-call | flops 6000000000 | bytes 16000000 | tf_op jit(solution)/shard_map/last_inner/pallas_call | solution.py:692
  121.4 0.9 collective-permute-done.10.edge_in
  122.3 2.6 %last_outer.1 = f32[150,16,512]{2,1,0:T(8,128)} custom-call(s32[3]{0:T(128)S(1)} %pad_add_fusion.flag_ref.refs_0_, f32[8,160,512]{2,1,0:T(8,128)S(1)} %get-tuple-element.48.far_ref, f32[152,512]{1,0:T(8,128)S(1)} %collective-permute-done.10.edge_in, f32[80,128]{1,0:T(8,128)S(1)} %collective-permute-done.11.far_west.west_in, ...), custom_call_target="tpu_custom_call", output_to_operand_aliasing={{}: (10, {})} | custom-call | tf_op jit(solution)/shard_map/last_outer/pallas_call | solution.py:743
  (4 shorter events, 0.0 us)
Async XLA Ops:
  9.5 6.3 %copy-start.4 = (f32[150]{0:T(256)S(1)}, f32[150]{0:T(256)}, u32[]{:S(2)}) copy-start(f32[150]{0:T(256)} %param.18) | copy-start | bytes 1804
  9.5 49.1 %all-to-all-start = ((f32[32,120,128]{2,1,0:T(8,128)}), f32[32,120,128]{2,1,0:T(8,128)S(1)}, u32[]{:S(2)}, u32[]{:S(2)}) async-start(f32[32,120,128]{2,1,0:T(8,128)} %send_tables.1), calls=%async_computation | async-start | bytes 3932160 | tf_op jit(solution)/shard_map/all_to_all | solution.py:806
  18.1 40.4 %copy-start = (s32[16,512]{1,0:T(8,128)S(1)}, s32[16,512]{1,0:T(8,128)}, u32[]{:S(2)}) copy-start(s32[16,512]{1,0:T(8,128)} %mask_ref.3) | copy-start | bytes 98308
  18.2 40.4 %copy-start.1 = (f32[16,512]{1,0:T(8,128)S(1)}, f32[16,512]{1,0:T(8,128)}, u32[]{:S(2)}) copy-start(f32[16,512]{1,0:T(8,128)} %refs_2_.3) | copy-start | bytes 98308
  18.2 40.4 %copy-start.2 = (f32[16,512]{1,0:T(8,128)S(1)}, f32[16,512]{1,0:T(8,128)}, u32[]{:S(2)}) copy-start(f32[16,512]{1,0:T(8,128)} %refs_3_.5) | copy-start | bytes 98308
  63.2 12.4 %collective-permute-start.1 = (f32[152,512]{1,0:T(8,128)S(1)}, f32[152,512]{1,0:T(8,128)S(1)}, u32[]{:S(2)}, u32[]{:S(2)}) collective-permute-start(f32[152,512]{1,0:T(8,128)S(1)} %get-tuple-element.39), channel_id=1, source_target_pairs={{0,4},{1,5},{2,6},{3,7},{4,0},{5,1},{6,2},{7,3},{8,12},{9,13},{10,... | collective-permute-start | bytes 933896 | tf_op jit(solution)/shard_map/ppermute | solution.py:842
  65.2 7.5 %copy-start.3 = (s32[512]{0:T(512)S(1)}, s32[512]{0:T(512)}, u32[]{:S(2)}) copy-start(s32[512]{0:T(512)} %param.22) | copy-start | bytes 6148
  70.9 4.7 %collective-permute-start.3 = (f32[80,128]{1,0:T(8,128)S(1)}, f32[80,128]{1,0:T(8,128)S(1)}, u32[]{:S(2)}, u32[]{:S(2)}) collective-permute-start(f32[80,128]{1,0:T(8,128)S(1)} %get-tuple-element.40.refs_0_), channel_id=1, source_target_pairs={{1,0},{2,1},{3,2},{0,3},{5,4},{6,5},{7,6},{4,7},{9,8},{10,9},{11,1... | collective-permute-start | bytes 122888 | tf_op jit(solution)/shard_map/ppermute | solution.py:845
  71.0 4.6 %collective-permute-start.2 = (f32[80,128]{1,0:T(8,128)S(1)}, f32[80,128]{1,0:T(8,128)S(1)}, u32[]{:S(2)}, u32[]{:S(2)}) collective-permute-start(f32[80,128]{1,0:T(8,128)S(1)} %get-tuple-element.40.refs_0_), channel_id=1, source_target_pairs={{0,1},{1,2},{2,3},{3,0},{4,5},{5,6},{6,7},{7,4},{8,9},{9,10},{10,1... | collective-permute-start | bytes 122888 | tf_op jit(solution)/shard_map/ppermute | solution.py:845
  72.7 13.4 %collective-permute-start = (f32[152,512]{1,0:T(8,128)S(1)}, f32[152,512]{1,0:T(8,128)S(1)}, u32[]{:S(2)}, u32[]{:S(2)}) collective-permute-start(f32[152,512]{1,0:T(8,128)S(1)} %get-tuple-element.38), channel_id=1, source_target_pairs={{4,8},{5,9},{6,10},{7,11},{8,4},{9,5},{10,6},{11,7},{12,16},{13,17... | collective-permute-start | bytes 933896 | tf_op jit(solution)/shard_map/ppermute | solution.py:842
  79.9 7.9 %collective-permute-start.5 = (f32[80,128]{1,0:T(8,128)S(1)}, f32[80,128]{1,0:T(8,128)S(1)}, u32[]{:S(2)}, u32[]{:S(2)}) collective-permute-start(f32[80,128]{1,0:T(8,128)S(1)} %get-tuple-element.41), channel_id=1, source_target_pairs={{1,0},{2,1},{3,2},{0,3},{5,4},{6,5},{7,6},{4,7},{9,8},{10,9},{11,1... | collective-permute-start | bytes 122888 | tf_op jit(solution)/shard_map/ppermute | solution.py:845
  86.0 2.2 %collective-permute-start.4 = (f32[80,128]{1,0:T(8,128)S(1)}, f32[80,128]{1,0:T(8,128)S(1)}, u32[]{:S(2)}, u32[]{:S(2)}) collective-permute-start(f32[80,128]{1,0:T(8,128)S(1)} %get-tuple-element.41), channel_id=1, source_target_pairs={{0,1},{1,2},{2,3},{3,0},{4,5},{5,6},{6,7},{7,4},{8,9},{9,10},{10,1... | collective-permute-start | bytes 122888 | tf_op jit(solution)/shard_map/ppermute | solution.py:845
  86.1 7.9 %collective-permute-start.7 = (f32[152,512]{1,0:T(8,128)S(1)}, f32[152,512]{1,0:T(8,128)S(1)}, u32[]{:S(2)}, u32[]{:S(2)}) collective-permute-start(f32[152,512]{1,0:T(8,128)S(1)} %get-tuple-element.45), channel_id=1, source_target_pairs={{0,4},{1,5},{2,6},{3,7},{4,0},{5,1},{6,2},{7,3},{8,12},{9,13},{10,... | collective-permute-start | bytes 933896 | tf_op jit(solution)/shard_map/ppermute | solution.py:842
  91.9 10.5 %collective-permute-start.6 = (f32[152,512]{1,0:T(8,128)S(1)}, f32[152,512]{1,0:T(8,128)S(1)}, u32[]{:S(2)}, u32[]{:S(2)}) collective-permute-start(f32[152,512]{1,0:T(8,128)S(1)} %get-tuple-element.44), channel_id=1, source_target_pairs={{4,8},{5,9},{6,10},{7,11},{8,4},{9,5},{10,6},{11,7},{12,16},{13,17... | collective-permute-start | bytes 933896 | tf_op jit(solution)/shard_map/ppermute | solution.py:842
  97.6 6.5 %collective-permute-start.9 = (f32[80,128]{1,0:T(8,128)S(1)}, f32[80,128]{1,0:T(8,128)S(1)}, u32[]{:S(2)}, u32[]{:S(2)}) collective-permute-start(f32[80,128]{1,0:T(8,128)S(1)} %get-tuple-element.47), channel_id=1, source_target_pairs={{1,0},{2,1},{3,2},{0,3},{5,4},{6,5},{7,6},{4,7},{9,8},{10,9},{11,1... | collective-permute-start | bytes 122888 | tf_op jit(solution)/shard_map/ppermute | solution.py:845
  100.4 3.6 %collective-permute-start.8 = (f32[80,128]{1,0:T(8,128)S(1)}, f32[80,128]{1,0:T(8,128)S(1)}, u32[]{:S(2)}, u32[]{:S(2)}) collective-permute-start(f32[80,128]{1,0:T(8,128)S(1)} %get-tuple-element.47), channel_id=1, source_target_pairs={{0,1},{1,2},{2,3},{3,0},{4,5},{5,6},{6,7},{7,4},{8,9},{9,10},{10,1... | collective-permute-start | bytes 122888 | tf_op jit(solution)/shard_map/ppermute | solution.py:845
  102.3 12.4 %collective-permute-start.13 = (f32[152,512]{1,0:T(8,128)S(1)}, f32[152,512]{1,0:T(8,128)S(1)}, u32[]{:S(2)}, u32[]{:S(2)}) collective-permute-start(f32[152,512]{1,0:T(8,128)S(1)} %get-tuple-element.52), channel_id=1, source_target_pairs={{0,4},{1,5},{2,6},{3,7},{4,0},{5,1},{6,2},{7,3},{8,12},{9,13},{10,... | collective-permute-start | bytes 933896 | tf_op jit(solution)/shard_map/ppermute | solution.py:842
  107.6 7.1 %collective-permute-start.12 = (f32[80,128]{1,0:T(8,128)S(1)}, f32[80,128]{1,0:T(8,128)S(1)}, u32[]{:S(2)}, u32[]{:S(2)}) collective-permute-start(f32[80,128]{1,0:T(8,128)S(1)} %get-tuple-element.50), channel_id=1, source_target_pairs={{1,0},{2,1},{3,2},{0,3},{5,4},{6,5},{7,6},{4,7},{9,8},{10,9},{11,1... | collective-permute-start | bytes 122888 | tf_op jit(solution)/shard_map/ppermute | solution.py:845
  109.5 5.2 %collective-permute-start.11 = (f32[80,128]{1,0:T(8,128)S(1)}, f32[80,128]{1,0:T(8,128)S(1)}, u32[]{:S(2)}, u32[]{:S(2)}) collective-permute-start(f32[80,128]{1,0:T(8,128)S(1)} %get-tuple-element.50), channel_id=1, source_target_pairs={{0,1},{1,2},{2,3},{3,0},{4,5},{5,6},{6,7},{7,4},{8,9},{9,10},{10,1... | collective-permute-start | bytes 122888 | tf_op jit(solution)/shard_map/ppermute | solution.py:845
  110.3 12.0 %collective-permute-start.10 = (f32[152,512]{1,0:T(8,128)S(1)}, f32[152,512]{1,0:T(8,128)S(1)}, u32[]{:S(2)}, u32[]{:S(2)}) collective-permute-start(f32[152,512]{1,0:T(8,128)S(1)} %get-tuple-element.49), channel_id=1, source_target_pairs={{4,8},{5,9},{6,10},{7,11},{8,4},{9,5},{10,6},{11,7},{12,16},{13,17... | collective-permute-start | bytes 933896 | tf_op jit(solution)/shard_map/ppermute | solution.py:842

commit v4 on v3

--- a/solution.py
+++ b/solution.py
@@ -35,7 +35,7 @@
     return jnp.broadcast_to(row, (8, row.shape[1])).T[:, 0:1]
 
 
-def slot_ranks(owner_row, cell_row, devices, col_count, row_count, capacity, spread):
+def slot_ranks(owner_row, cell_row, devices, col_count, row_count, capacity):
     count = owner_row.shape[1]
     owner = owner_row.astype(F32)
     inside = cell_row // col_count
@@ -49,23 +49,23 @@
     for start in range(0, count, 128):
         before = jnp.where(key_col[start : start + 128] < key, 1.0, 0.0)
         rank = rank + jnp.sum(before, axis=0, keepdims=True)
-    if spread:
-        total = jnp.sum(jnp.where(mine, totals, 0.0), axis=0, keepdims=True)
-        offset = owner * 1024.0
-        goal = (inside * capacity // row_count).astype(F32) - rank + offset
-        goal_col = as_column(goal)
-        shift = offset
-        for start in range(0, count, 128):
-            within = key_col[start : start + 128] <= key
-            reached = jnp.where(within, goal_col[start : start + 128], 0.0)
-            shift = jnp.maximum(shift, jnp.max(reached, axis=0, keepdims=True))
-        rank = rank + jnp.minimum(shift - offset, float(capacity) - total)
+    total = jnp.sum(jnp.where(mine, totals, 0.0), axis=0, keepdims=True)
+    offset = owner * 1024.0
+    goal = (inside * capacity // row_count).astype(F32) - rank + offset
+    goal_col = as_column(goal)
+    shift = offset
+    for start in range(0, count, 128):
+        within = key_col[start : start + 128] <= key
+        reached = jnp.where(within, goal_col[start : start + 128], 0.0)
+        shift = jnp.maximum(shift, jnp.max(reached, axis=0, keepdims=True))
+    rank = rank + jnp.minimum(shift - offset, float(capacity) - total)
     return rank
 
 
 def table_kernel(
     devices,
     capacity,
+    alt_capacity,
     group,
     row_count,
     col_count,
@@ -93,11 +93,11 @@
         slot = lax.broadcasted_iota(jnp.int32, (capacity, 1), 0).astype(F32)
         alt_cell = alt_cell_ref[...].reshape(1, n_alt)
         rank = slot_ranks(
-            owner_ref[...], cell_ref[...], devices, col_count, row_count, capacity, True
+            owner_ref[...], cell_ref[...], devices, col_count, row_count, capacity
         )
         rank_hot_ref[...] = jnp.where(slot == rank, 1.0, 0.0).astype(BF)
         rank = slot_ranks(
-            alt_owner_ref[...], alt_cell, devices, col_count, row_count, capacity, False
+            alt_owner_ref[...], alt_cell, devices, col_count, row_count, alt_capacity
         )
         alt_rank_hot_ref[...] = jnp.where(slot == rank, 1.0, 0.0).astype(BF)
         level_ref[...] = jnp.zeros(level_ref.shape, F32)
@@ -149,13 +149,13 @@
     message_ref[:, capacity : capacity + group] = total
 
 
-def send_tables(devices, capacity, group, row_count, col_count, operands):
+def send_tables(devices, capacity, alt_capacity, group, row_count, col_count, operands):
     n_obs = operands[1].shape[1]
     n_alt = operands[5].shape[1]
     per_step = max(1, 1536 // capacity)
 
     def kernel(*refs):
-        table_kernel(devices, capacity, group, row_count, col_count, *refs)
+        table_kernel(devices, capacity, alt_capacity, group, row_count, col_count, *refs)
 
     def whole(array):
         return pl.BlockSpec(array.shape, lambda s: (0,) * len(array.shape))
@@ -214,35 +214,39 @@
     pack_row(state_ref.at[jnp.where(is_upper, state_ref.shape[0] - 1, 0)], edge_ref)
 
 
-def prepare(capacity, alt_capacity, group, col_count, message_ref, sea_ref, left_ref, hot_ref, rows_ref, bound_ref):
-    row_count = sea_ref.shape[0]
+def one_hot_columns(cell, col_count):
+    col_iota = lax.broadcasted_iota(jnp.int32, (1, col_count), 1)
+    cell = cell.astype(jnp.int32) - 1
+    return jnp.where((cell & (col_count - 1)) == col_iota, 1.0, 0.0).astype(BF)
+
+
+def grid_rows(cell, col_count):
+    return lax.shift_right_arithmetic(cell.astype(jnp.int32) - 1, col_count.bit_length() - 1)
+
+
+def slot_chunk(message_ref, index, start):
+    block = min(32, message_ref.shape[0])
+    return message_ref[index * block : (index + 1) * block, start : start + 8, :].reshape(
+        block * 8, LANES
+    )
+
+
+def prepare(capacity, group, row_count, col_count, message_ref, left_ref, hot_ref, rows_ref, bound_ref, alt_ref, alt_bound_ref):
     devices = message_ref.shape[0]
-    block = min(32, devices)
-    members = block * 8
-    octets = capacity // 8
-    alt_octets = (alt_capacity + 7) // 8
+    members = min(32, devices) * 8
     per_group = group // 8
-    shift = col_count.bit_length() - 1
-    col_iota = lax.broadcasted_iota(jnp.int32, (1, col_count), 1)
-    row_iota = lax.broadcasted_iota(jnp.int32, (row_count, 1), 0)
-
-    def chunk(index, start):
-        return message_ref[index * block : (index + 1) * block, start : start + 8, :].reshape(
-            members, LANES
-        )
-
-    def hot_of(cell):
-        return jnp.where(((cell - 1) & (col_count - 1)) == col_iota, 1.0, 0.0).astype(BF)
-
-    def rows_of(cell):
-        return lax.shift_right_arithmetic(cell - 1, shift)
-
-    sea = jnp.zeros((row_count, col_count), F32)
+
+    def bounds(ref, number, rows):
+        ref[2 * number] = jnp.min(jnp.where(rows >= 0, rows, row_count))
+        ref[2 * number + 1] = jnp.max(rows)
+
     count = 0
-    for index in range(devices // block):
-        tails = [chunk(index, capacity + 8 * part).T for part in range(per_group)]
-        for octet in range(octets):
-            table = chunk(index, 8 * octet)
+    for index in range(devices * 8 // members):
+        tails = [
+            slot_chunk(message_ref, index, capacity + 8 * part).T for part in range(per_group)
+        ]
+        for octet in range(capacity // 8):
+            table = slot_chunk(message_ref, index, 8 * octet)
             turned = table.T
             tail = tails[octet % per_group]
             begin = 32 * (octet // per_group)
@@ -250,21 +254,52 @@
             high, low = split_two(levels)
             left_ref[count, :, 0:members] = high
             left_ref[count, :, members : 2 * members] = low
-            hot = hot_of(table[:, 75:76].astype(jnp.int32))
-            hot_ref[count] = hot
-            rows = rows_of(turned[75:76].astype(jnp.int32))
+            hot_ref[count] = one_hot_columns(table[:, 75:76], col_count)
+            rows = grid_rows(turned[75:76], col_count)
             rows_ref[count] = jnp.broadcast_to(rows, (8, members))
-            bound_ref[2 * count] = jnp.min(jnp.where(rows >= 0, rows, row_count))
-            bound_ref[2 * count + 1] = jnp.max(rows)
+            bounds(bound_ref, count, rows)
+            alt_ref[count] = turned[72:80]
+            bounds(alt_bound_ref, count, grid_rows(turned[77:78], col_count))
             count += 1
-            if octet >= alt_octets:
-                continue
-            alt_hot = hot_of(table[:, 77:78].astype(jnp.int32))
-            alt_rows = rows_of(turned[77:78].astype(jnp.int32))
-            weighted = jnp.where(alt_rows == row_iota, turned[76:77], 0.0)
-            high, low = split_two(weighted)
-            product = mm(jnp.concatenate([high, low], axis=0), alt_hot)
-            sea = sea + product[:row_count] + product[row_count:]
+
+
+def alt_chunks(capacity, alt_capacity, devices):
+    octets = capacity // 8
+    blocks = devices // min(32, devices)
+    used = (alt_capacity + 7) // 8
+    return [(b * octets + o, b, o) for b in range(blocks) for o in range(used)]
+
+
+def alt_product(chunk, message_ref, alt_ref, rows_wanted, col_count):
+    number, index, octet = chunk
+    table = slot_chunk(message_ref, index, 8 * octet)
+    alt_hot = one_hot_columns(table[:, 77:78], col_count)
+    rows = grid_rows(alt_ref[number, 5:6], col_count)
+    weighted = jnp.where(rows == rows_wanted, alt_ref[number, 4:5], 0.0)
+    count = weighted.shape[0]
+    high, low = split_two(weighted)
+    product = mm(jnp.concatenate([high, low], axis=0), alt_hot)
+    return product[:count] + product[count:]
+
+
+def row_sea_level(row, chunks, message_ref, alt_ref, alt_bound_ref, sea_ref):
+    count, col_count = sea_ref.shape
+    wanted = jnp.zeros((count, 1), jnp.int32) + row
+    sea_ref[...] = jnp.zeros(sea_ref.shape, F32)
+    for chunk in chunks:
+        number = chunk[0]
+
+        @pl.when((alt_bound_ref[2 * number] <= row) & (row <= alt_bound_ref[2 * number + 1]))
+        def _():
+            sea_ref[...] += alt_product(chunk, message_ref, alt_ref, wanted, col_count)
+
+
+def sea_level(chunks, message_ref, alt_ref, sea_ref):
+    row_count, col_count = sea_ref.shape
+    wanted = lax.broadcasted_iota(jnp.int32, (row_count, 1), 0)
+    sea = jnp.zeros((row_count, col_count), F32)
+    for chunk in chunks:
+        sea = sea + alt_product(chunk, message_ref, alt_ref, wanted, col_count)
     sea_ref[...] = sea
 
 
@@ -278,12 +313,11 @@
 
 
 def outer_forcing(row, is_upper, profile_ref, coast_refs, sea_ref, left_ref, hot_ref, rows_ref, bound_ref, edge_ref):
-    row_count, col_count = sea_ref.shape
-    last = row_count - 1
+    col_count = sea_ref.shape[1]
+    last = coast_refs[0].shape[0] - 1
     profile = jnp.broadcast_to(profile_ref[...], (2 * PAD, LANES))
-    sea = jnp.where(is_upper, sea_ref[last : last + 1, :], sea_ref[0:1, :])
     for start in range(0, col_count, LANES):
-        edge_ref[:, start : start + LANES] = profile * sea[:, start : start + LANES]
+        edge_ref[:, start : start + LANES] = profile * sea_ref[0:1, start : start + LANES]
 
     def step(number, carry):
         @pl.when((bound_ref[2 * number] <= row) & (row <= bound_ref[2 * number + 1]))
@@ -360,28 +394,33 @@
     members = min(32, devices) * 8
     chunks = capacity // 8 * (devices // min(32, devices))
 
-    def kernel(flag_ref, message_ref, profile_ref, wet, north, east, edge_ref, *refs):
-        *outs, row_ref = refs
-        prepare(capacity, alt_capacity, group, col_count, message_ref, *outs)
+    def kernel(flag_ref, message_ref, profile_ref, wet, north, east, edge_ref, left, hot, rows, bound, alt, alt_bound, row_ref, sea_ref):
+        prepare(capacity, group, row_count, col_count, message_ref, left, hot, rows, bound, alt, alt_bound)
         is_upper = flag_ref[NEAR] > 0
         row = jnp.where(is_upper, row_count - 1, 0)
-        outer_forcing(row, is_upper, profile_ref, (wet, north, east), *outs, row_ref)
+        row_sea_level(row, alt_chunks(capacity, alt_capacity, devices), message_ref, alt, alt_bound, sea_ref)
+        outer_forcing(row, is_upper, profile_ref, (wet, north, east), sea_ref, left, hot, rows, bound, row_ref)
         pack_row(row_ref, edge_ref)
 
+    in_vmem = pl.BlockSpec(memory_space=pltpu.VMEM)
+    in_smem = pl.BlockSpec(memory_space=pltpu.SMEM)
     return pl.pallas_call(
         kernel,
         in_specs=in_place(5),
         out_shape=(
             half_shapes(row_count, col_count)[1],
-            jax.ShapeDtypeStruct((row_count, col_count), F32),
             jax.ShapeDtypeStruct((chunks, 2 * PAD, 2 * members), BF),
             jax.ShapeDtypeStruct((chunks, members, col_count), BF),
             jax.ShapeDtypeStruct((chunks, 8, members), jnp.int32),
             jax.ShapeDtypeStruct((2 * chunks,), jnp.int32),
+            jax.ShapeDtypeStruct((chunks, 8, members), F32),
+            jax.ShapeDtypeStruct((2 * chunks,), jnp.int32),
         ),
-        out_specs=[pl.BlockSpec(memory_space=pltpu.VMEM)] * 5
-        + [pl.BlockSpec(memory_space=pltpu.SMEM)],
-        scratch_shapes=[pltpu.VMEM((2 * PAD, col_count), F32)],
+        out_specs=[in_vmem] * 4 + [in_smem, in_vmem, in_smem],
+        scratch_shapes=[
+            pltpu.VMEM((2 * PAD, col_count), F32),
+            pltpu.VMEM((8, col_count), F32),
+        ],
         compiler_params=pltpu.CompilerParams(vmem_limit_bytes=24 * MIB),
         cost_estimate=pl.CostEstimate(
             flops=6_000_000_000, bytes_accessed=8_000_000, transcendentals=0
@@ -390,12 +429,14 @@
     )(flags, message, profile, *coast)
 
 
-def rest_forcing(flags, profile, coast, prepared):
+def rest_forcing(capacity, alt_capacity, flags, message, profile, coast, left, hot, rows, bound, alt):
     row_count, col_count = coast[0].shape
     half = row_count // 2
-
-    def kernel(flag_ref, profile_ref, wet, north, east, sea, left, hot, rows, bound, state, edge_ref, cols_ref):
-        all_forcing(profile_ref, (wet, north, east), sea, left, hot, rows, bound, state)
+    devices = message.shape[0]
+
+    def kernel(flag_ref, message_ref, profile_ref, wet, north, east, left, hot, rows, alt, bound, state, edge_ref, cols_ref, sea_ref):
+        sea_level(alt_chunks(capacity, alt_capacity, devices), message_ref, alt, sea_ref)
+        all_forcing(profile_ref, (wet, north, east), sea_ref, left, hot, rows, bound, state)
         cols = jnp.zeros((PAD, LANES), F32)
         for which in (NEAR, FAR):
             first_row = jnp.where(flag_ref[which] > 0, half, 0)
@@ -407,14 +448,15 @@
     state = jax.ShapeDtypeStruct((row_count, 2 * PAD, col_count), F32)
     return pl.pallas_call(
         kernel,
-        in_specs=in_place(8) + [pl.BlockSpec(memory_space=pltpu.SMEM)],
+        in_specs=in_place(9) + [pl.BlockSpec(memory_space=pltpu.SMEM)],
         out_shape=(state, edge, cols),
+        scratch_shapes=[pltpu.VMEM((row_count, col_count), F32)],
         compiler_params=pltpu.CompilerParams(vmem_limit_bytes=20 * MIB),
         cost_estimate=pl.CostEstimate(
             flops=6_000_000_000, bytes_accessed=8_000_000, transcendentals=0
         ),
         name="forcing_rest",
-    )(flags, profile, *coast, *prepared)
+    )(flags, message, profile, *coast, left, hot, rows, alt, bound)
 
 
 def fold_row(row_ref, mirror_ref, piece, chunk, chunks, rows):
@@ -787,9 +829,11 @@
     devices = count_ja * count_ia
     capacity = round_up(3 * argo_value.shape[0] // devices, 8)
     group = round_up(capacity // 4, 8)
+    alt_capacity = max(2, 3 * alt_value.shape[0] // devices)
     message = send_tables(
         devices,
         capacity,
+        alt_capacity,
         group,
         row_count,
         col_count,
@@ -814,7 +858,6 @@
     matrices = mixing_matrices(vinv)
     profile = jnp.pad(alt_profile.reshape(2, LEVELS, 1), ((0, 0), (0, PAD - LEVELS), (0, 0)))
     profile = profile.reshape(2 * PAD, 1)
-    alt_capacity = max(2, 3 * alt_value.shape[0] // devices)
     coast = (land_mask, coef_north, coef_east)
     rows = row_count // 2
     lower = [matrices[:, :rows], matrices[:, rows:]]
@@ -848,7 +891,9 @@
         capacity, alt_capacity, group, flags, message, profile, coast
     )
     near_edge = swap(NEAR, near_edge)
-    state, far_edge, cols = rest_forcing(flags, profile, coast, prepared)
+    state, far_edge, cols = rest_forcing(
+        capacity, alt_capacity, flags, message, profile, coast, *prepared[:5]
+    )
     near = far = state
     sides = pass_columns(cols)
     far_edge = swap(FAR, far_edge)

time: 126 us -> 126 us (level)
  starting transfers between devices: 33.2 us -> 24.7 us
  Pallas kernels: 44.7 us -> 48.9 us
  waiting for transfers between devices: 43.4 us -> 46.9 us
    ppermute x4, starting transfers between devices: 11 us -> 1.36 us  [pass_columns(): lax.ppermute(cols, 'ia', ring_west)]
    ppermute x6, waiting for transfers between devices: 0.92 us -> 7.51 us  [swap(): return lax.ppermute(edge, ('ja', 'ia'), swaps[which])]
    pallas_call x1, Pallas kernels: 5.7 us -> 9.26 us  [rest_forcing(): pl.pallas_call(kernel, in_specs=in_place(9) + [pl.BlockSpec(memory_space=...]
    ppermute x4, waiting for transfers between devices: 2.61 us -> 0.01 us  [pass_columns(): lax.ppermute(cols, 'ia', ring_west)]
  transfers between devices with their start and end apart: 15 -> 15, of which waited for: 5 -> 4; matrix products, arithmetic and copies ran while one was open for 3% -> 3% of each run, Pallas kernels for 22% -> 25%
where the time goes in v4:
time: 126 us; the launch traced here: 124 us
  Pallas kernels  48.9 us (39%)
  waiting for transfers between devices  46.9 us (37%)
  starting transfers between devices  24.7 us (20%)
  local copies, waits for them, and re-layouts  2.04 us (2%)
  other arithmetic  1.29 us (1%)
    all_to_all x1, waiting for transfers between devices, body(): lax.all_to_all(message, ('ja', 'ia'), split_axis=0, concat_axis=0, tiled=...  39.4 us
    pallas_call x4, Pallas kernels, diffuse(): pl.pallas_call(kernel, in_specs=in_place(8 + len(far_cols)), out_shape=ha...  14.1 us
    ppermute x6, starting transfers between devices, swap(): return lax.ppermute(edge, ('ja', 'ia'), swaps[which])  11.2 us
    pallas_call x1, Pallas kernels, send_tables(): pl.pallas_call(kernel, grid=(devices // per_step,), in_specs=[whole(x) fo...  9.95 us
    pallas_call x1, Pallas kernels, rest_forcing(): pl.pallas_call(kernel, in_specs=in_place(9) + [pl.BlockSpec(memory_space=...  9.26 us
    ppermute x6, waiting for transfers between devices, swap(): return lax.ppermute(edge, ('ja', 'ia'), swaps[which])  7.51 us
    pallas_call x1, Pallas kernels, last_inner(): pl.pallas_call(kernel, in_specs=in_place(13), out_specs=[pl.BlockSpec(mem...  6.47 us
    all_to_all x1, starting transfers between devices, body(): lax.all_to_all(message, ('ja', 'ia'), split_axis=0, concat_axis=0, tiled=...  6.3 us
  transfers between devices with their start and end apart: 15, of which 4 were waited for; matrix products, arithmetic and copies ran while one was open for 3% of the time, Pallas kernels for 25%

profile of v4, /device:TPU:13, one launch (start us, length us, event | category | flops | bytes accessed | tf_op | source)
XLA Modules:
  0.0 124.4 jit_solution(1835011635684417619)
XLA Ops:
  0.0 10.0 %send_tables.1 = f32[32,120,128]{2,1,0:T(8,128)} custom-call(f32[150,1024]{1,0:T(8,128)} %bitcast.11, s32[1,1024]{1,0:T(1,128)} %bitcast.12, s32[1,1024]{1,0:T(1,128)} %bitcast.13, f32[768]{0:T(1024)} %refs_3_.3, s32[768]{0:T(1024)} %refs_4_.1, s32[1,768]{1,0:T(1,128)} %bitcast.14), custom_call_target="tpu_custom_call" | custom-call | tf_op jit(solution)/shard_map/send_tables/pallas_call | solution.py:163
  10.0 0.0 copy-start.4
  10.0 6.3 %all-to-all-start = ((f32[32,120,128]{2,1,0:T(8,128)}), f32[32,120,128]{2,1,0:T(8,128)S(1)}, u32[]{:S(2)}, u32[]{:S(2)}) async-start(f32[32,120,128]{2,1,0:T(8,128)} %send_tables.1), calls=%async_computation | async-start | bytes 3932160 | tf_op jit(solution)/shard_map/all_to_all | solution.py:850
  16.3 0.0 copy-done.4
  16.3 0.1 reshape.19
  16.4 0.1 reshape.22.profile_ref
  16.5 1.7 %copy.17 = f32[16,2,75,75]{2,3,0,1:T(8,128)S(1)} copy(f32[16,2,75,75]{3,1,2,0:T(2,128)} %param.23) | data formatting | bytes 1440000 | tf_op args[11]
  18.3 0.1 pad.13.clone
  18.3 0.1 pad_add_fusion.flag_ref.refs_0_
  18.4 0.2 reduce-precision_convert_fusion
  18.6 0.0 copy-start
  18.6 0.0 copy-start.1
  18.7 0.0 copy-start.2
  18.7 0.9 maximum_maximum_fusion
  19.6 0.1 broadcast_select_fusion
  19.7 39.4 %all-to-all-done.message_ref = f32[32,120,128]{2,1,0:T(8,128)S(1)} async-done(((f32[32,120,128]{2,1,0:T(8,128)}), f32[32,120,128]{2,1,0:T(8,128)S(1)}, u32[]{:S(2)}, u32[]{:S(2)}) %all-to-all-start) | async-done | bytes 1966112 | tf_op jit(solution)/shard_map/all_to_all | solution.py:850
  59.1 0.0 copy-done
  59.1 0.0 copy-done.1
  59.1 0.0 copy-done.2
  59.1 5.1 %forcing_first.1 = (f32[152,512]{1,0:T(8,128)S(1)}, bf16[12,160,512]{2,1,0:T(8,128)(2,1)S(1)}, bf16[12,256,512]{2,1,0:T(8,128)(2,1)S(1)}, s32[12,8,256]{2,1,0:T(...) custom-call(s32[3]{0:T(128)S(1)} %pad_add_fusion.flag_ref.refs_0_, ...), custom_call_target="tpu_custom_call" | custom-call | flops 6000000000 | bytes 8000000 | tf_op jit(solution)/shard_map/forcing_first/pallas_call | solution.py:407
  64.2 1.7 %collective-permute-start.1 = (f32[152,512]{1,0:T(8,128)S(1)}, f32[152,512]{1,0:T(8,128)S(1)}, u32[]{:S(2)}, u32[]{:S(2)}) collective-permute-start(f32[152,512]{1,0:T(8,128)S(1)} %get-tuple-element.39), channel_id=1, source_target_pairs={{0,4},{1,5},{2,6},{3,7},{4,0},{5,1},{6,2},{7,3},{8,12},{9,13},{10,... | collective-permute-start | bytes 933896 | tf_op jit(solution)/shard_map/ppermute | solution.py:885
  66.0 0.0 copy-start.3
  66.0 9.3 %forcing_rest.1 = (f32[16,160,512]{2,1,0:T(8,128)S(1)}, f32[152,512]{1,0:T(8,128)S(1)}, f32[80,128]{1,0:T(8,128)S(1)}) custom-call(s32[3]{0:T(128)S(1)} %pad_add_fusion.flag_ref.refs_0_, f32[32,120,128]{2,1,0:T(8,128)S(1)} %all-to-all-done.message_ref, f32[160,1]{1,0:T(8,128)S(1)} %reshape.22.profile_ref, s32[16,512]{1,0:T(8,128)S(1)} %copy-done, ...), custom_call_target="tpu_custom_call" | custom-call | flops 6000000000 | bytes 8000000 | tf_op jit(solution)/shard_map/forcing_rest/pallas_call | solution.py:449
  75.2 0.1 collective-permute-start.3
  75.3 1.7 %collective-permute-start.2 = (f32[80,128]{1,0:T(8,128)S(1)}, f32[80,128]{1,0:T(8,128)S(1)}, u32[]{:S(2)}, u32[]{:S(2)}) collective-permute-start(f32[80,128]{1,0:T(8,128)S(1)} %get-tuple-element.40.refs_0_), channel_id=1, source_target_pairs={{0,1},{1,2},{2,3},{3,0},{4,5},{5,6},{6,7},{7,4},{8,9},{9,10},{10,1... | collective-permute-start | bytes 122888 | tf_op jit(solution)/shard_map/ppermute | solution.py:888
  77.0 0.0 copy-done.3
  77.0 3.2 %collective-permute-start = (f32[152,512]{1,0:T(8,128)S(1)}, f32[152,512]{1,0:T(8,128)S(1)}, u32[]{:S(2)}, u32[]{:S(2)}) collective-permute-start(f32[152,512]{1,0:T(8,128)S(1)} %get-tuple-element.38), channel_id=1, source_target_pairs={{4,8},{5,9},{6,10},{7,11},{8,4},{9,5},{10,6},{11,7},{12,16},{13,17... | collective-permute-start | bytes 933896 | tf_op jit(solution)/shard_map/ppermute | solution.py:885
  80.2 0.0 collective-permute-done.3.refs_6_.east_in
  80.2 0.0 collective-permute-done.2.refs_5_.west_in
  80.2 0.0 collective-permute-done.1.refs_4_.edge_in
  80.3 0.7 edge_weights.2.coef_ref.near_coef
  81.0 3.5 %diffusion_near.2 = (f32[8,160,512]{2,1,0:T(8,128)S(1)}, f32[152,512]{1,0:T(8,128)S(1)}, f32[80,128]{1,0:T(8,128)S(1)}) custom-call(s32[3]{0:T(128)S(1)} %pad_add_fusion.flag_ref.refs_0_, f32[16,160,512]{2,1,0:T(8,128)S(1)} %get-tuple-element.37.state_ref.other_ref, f32[16,160,512]{2,1,0:T(8,128)S(1)} %get-tuple-element.37.state_ref.other_ref, ...), custom_call_target="tpu_custom_call" | custom-call | flops 3000000000 | bytes 8000000 | tf_op jit(solution)/shard_map/diffusion_near/pallas_call | solution.py:651
  84.4 0.1 collective-permute-start.5
  84.5 1.7 %collective-permute-start.4 = (f32[80,128]{1,0:T(8,128)S(1)}, f32[80,128]{1,0:T(8,128)S(1)}, u32[]{:S(2)}, u32[]{:S(2)}) collective-permute-start(f32[80,128]{1,0:T(8,128)S(1)} %get-tuple-element.41), channel_id=1, source_target_pairs={{0,1},{1,2},{2,3},{3,0},{4,5},{5,6},{6,7},{7,4},{8,9},{9,10},{10,1... | collective-permute-start | bytes 122888 | tf_op jit(solution)/shard_map/ppermute | solution.py:888
  86.2 0.0 collective-permute-start.7
  86.2 2.0 %collective-permute-done.refs_4_.edge_in = f32[152,512]{1,0:T(8,128)S(1)} collective-permute-done((f32[152,512]{1,0:T(8,128)S(1)}, f32[152,512]{1,0:T(8,128)S(1)}, u32[]{:S(2)}, u32[]{:S(2)}) %collective-permute-start) | collective-permute-done | bytes 311328 | tf_op jit(solution)/shard_map/ppermute | solution.py:885
  88.2 0.7 edge_weights.3.coef_ref.far_coef
  88.9 0.0 collective-permute-done.5.east_in
  89.0 0.0 collective-permute-done.4.west_in
  89.0 3.5 %diffusion_far.2 = (f32[8,160,512]{2,1,0:T(8,128)S(1)}, f32[152,512]{1,0:T(8,128)S(1)}, f32[80,128]{1,0:T(8,128)S(1)}) custom-call(s32[3]{0:T(128)S(1)} %pad_add_fusion.flag_ref.refs_0_, f32[16,160,512]{2,1,0:T(8,128)S(1)} %get-tuple-element.37.state_ref.other_ref, f32[16,160,512]{2,1,0:T(8,128)S(1)} %get-tuple-element.37.state_ref.other_ref, ...), custom_call_target="tpu_custom_call" | custom-call | flops 3000000000 | bytes 8000000 | tf_op jit(solution)/shard_map/diffusion_far/pallas_call | solution.py:651
  92.4 3.2 %collective-permute-start.6 = (f32[152,512]{1,0:T(8,128)S(1)}, f32[152,512]{1,0:T(8,128)S(1)}, u32[]{:S(2)}, u32[]{:S(2)}) collective-permute-start(f32[152,512]{1,0:T(8,128)S(1)} %get-tuple-element.44), channel_id=1, source_target_pairs={{4,8},{5,9},{6,10},{7,11},{8,4},{9,5},{10,6},{11,7},{12,16},{13,17... | collective-permute-start | bytes 933896 | tf_op jit(solution)/shard_map/ppermute | solution.py:885
  95.6 0.0 collective-permute-done.7.edge_in
  95.6 3.7 %diffusion_near.3 = (f32[8,160,512]{2,1,0:T(8,128)S(1)}, f32[152,512]{1,0:T(8,128)S(1)}, f32[80,128]{1,0:T(8,128)S(1)}) custom-call(s32[3]{0:T(128)S(1)} %pad_add_fusion.flag_ref.refs_0_, f32[8,160,512]{2,1,0:T(8,128)S(1)} %get-tuple-element.43.state_ref.other_ref, f32[8,160,512]{2,1,0:T(8,128)S(1)} %get-tuple-element.42.other_ref.state_ref, ...), custom_call_target="tpu_custom_call" | custom-call | flops 3000000000 | bytes 8000000 | tf_op jit(solution)/shard_map/diffusion_near/pallas_call | solution.py:651
  99.3 0.3 collective-permute-start.9
  99.7 1.5 %collective-permute-start.8 = (f32[80,128]{1,0:T(8,128)S(1)}, f32[80,128]{1,0:T(8,128)S(1)}, u32[]{:S(2)}, u32[]{:S(2)}) collective-permute-start(f32[80,128]{1,0:T(8,128)S(1)} %get-tuple-element.47), channel_id=1, source_target_pairs={{0,1},{1,2},{2,3},{3,0},{4,5},{5,6},{6,7},{7,4},{8,9},{9,10},{10,1... | collective-permute-start | bytes 122888 | tf_op jit(solution)/shard_map/ppermute | solution.py:888
  101.1 0.0 collective-permute-start.13
  101.1 3.1 %collective-permute-done.6.edge_in = f32[152,512]{1,0:T(8,128)S(1)} collective-permute-done((f32[152,512]{1,0:T(8,128)S(1)}, f32[152,512]{1,0:T(8,128)S(1)}, u32[]{:S(2)}, u32[]{:S(2)}) %collective-permute-start.6) | collective-permute-done | bytes 311328 | tf_op jit(solution)/shard_map/ppermute | solution.py:885
  104.2 0.0 collective-permute-done.9.east_in.near_east
  104.2 0.0 collective-permute-done.8.west_in.near_west
  104.2 3.5 %diffusion_far.3 = (f32[8,160,512]{2,1,0:T(8,128)S(1)}, f32[152,512]{1,0:T(8,128)S(1)}, f32[80,128]{1,0:T(8,128)S(1)}) custom-call(s32[3]{0:T(128)S(1)} %pad_add_fusion.flag_ref.refs_0_, f32[8,160,512]{2,1,0:T(8,128)S(1)} %get-tuple-element.42.other_ref.state_ref, f32[8,160,512]{2,1,0:T(8,128)S(1)} %get-tuple-element.43.state_ref.other_ref, ...), custom_call_target="tpu_custom_call" | custom-call | flops 3000000000 | bytes 8000000 | tf_op jit(solution)/shard_map/diffusion_far/pallas_call | solution.py:651
  107.8 0.9 collective-permute-start.12
  108.7 0.9 collective-permute-start.11
  109.6 3.1 %collective-permute-start.10 = (f32[152,512]{1,0:T(8,128)S(1)}, f32[152,512]{1,0:T(8,128)S(1)}, u32[]{:S(2)}, u32[]{:S(2)}) collective-permute-start(f32[152,512]{1,0:T(8,128)S(1)} %get-tuple-element.49), channel_id=1, source_target_pairs={{4,8},{5,9},{6,10},{7,11},{8,4},{9,5},{10,6},{11,7},{12,16},{13,17... | collective-permute-start | bytes 933896 | tf_op jit(solution)/shard_map/ppermute | solution.py:885
  112.7 0.0 collective-permute-done.12.far_east.east_in
  112.7 0.0 collective-permute-done.11.far_west.west_in
  112.7 0.0 collective-permute-done.13.edge_in
  112.7 6.5 %last_inner.1 = (f32[150,16,512]{2,1,0:T(8,128)}, f32[2,75,8,512]{3,2,1,0:T(8,128)S(1)}) custom-call(s32[3]{0:T(128)S(1)} %pad_add_fusion.flag_ref.refs_0_, f32[8,160,512]{2,1,0:T(8,128)S(1)} %get-tuple-element.51.near_ref, f32[8,160,512]{2,1,0:T(8,128)S(1)} %get-tuple-element.48.far_ref, f32[152,512]{1,0:T(8,128)S(1)} %collective-permute-done.13.edge_in, ...), custom_call_target="tpu_custom_call" | custom-call | flops 6000000000 | bytes 16000000 | tf_op jit(solution)/shard_map/last_inner/pallas_call | solution.py:734
  119.2 2.4 %collective-permute-done.10.edge_in = f32[152,512]{1,0:T(8,128)S(1)} collective-permute-done((f32[152,512]{1,0:T(8,128)S(1)}, f32[152,512]{1,0:T(8,128)S(1)}, u32[]{:S(2)}, u32[]{:S(2)}) %collective-permute-start.10) | collective-permute-done | bytes 311328 | tf_op jit(solution)/shard_map/ppermute | solution.py:885
  121.6 2.6 %last_outer.1 = f32[150,16,512]{2,1,0:T(8,128)} custom-call(s32[3]{0:T(128)S(1)} %pad_add_fusion.flag_ref.refs_0_, f32[8,160,512]{2,1,0:T(8,128)S(1)} %get-tuple-element.48.far_ref, f32[152,512]{1,0:T(8,128)S(1)} %collective-permute-done.10.edge_in, f32[80,128]{1,0:T(8,128)S(1)} %collective-permute-done.11.far_west.west_in, ...), custom_call_target="tpu_custom_call", output_to_operand_aliasing={{}: (10, {})} | custom-call | tf_op jit(solution)/shard_map/last_outer/pallas_call | solution.py:785
  (4 shorter events, 0.0 us)
Async XLA Ops:
  10.0 6.3 %copy-start.4 = (f32[150]{0:T(256)S(1)}, f32[150]{0:T(256)}, u32[]{:S(2)}) copy-start(f32[150]{0:T(256)} %param.18) | copy-start | bytes 1804
  10.0 49.1 %all-to-all-start = ((f32[32,120,128]{2,1,0:T(8,128)}), f32[32,120,128]{2,1,0:T(8,128)S(1)}, u32[]{:S(2)}, u32[]{:S(2)}) async-start(f32[32,120,128]{2,1,0:T(8,128)} %send_tables.1), calls=%async_computation | async-start | bytes 3932160 | tf_op jit(solution)/shard_map/all_to_all | solution.py:850
  18.6 40.4 %copy-start = (s32[16,512]{1,0:T(8,128)S(1)}, s32[16,512]{1,0:T(8,128)}, u32[]{:S(2)}) copy-start(s32[16,512]{1,0:T(8,128)} %mask_ref.3) | copy-start | bytes 98308
  18.6 40.4 %copy-start.1 = (f32[16,512]{1,0:T(8,128)S(1)}, f32[16,512]{1,0:T(8,128)}, u32[]{:S(2)}) copy-start(f32[16,512]{1,0:T(8,128)} %refs_2_.3) | copy-start | bytes 98308
  18.7 40.4 %copy-start.2 = (f32[16,512]{1,0:T(8,128)S(1)}, f32[16,512]{1,0:T(8,128)}, u32[]{:S(2)}) copy-start(f32[16,512]{1,0:T(8,128)} %refs_3_.5) | copy-start | bytes 98308
  64.2 16.0 %collective-permute-start.1 = (f32[152,512]{1,0:T(8,128)S(1)}, f32[152,512]{1,0:T(8,128)S(1)}, u32[]{:S(2)}, u32[]{:S(2)}) collective-permute-start(f32[152,512]{1,0:T(8,128)S(1)} %get-tuple-element.39), channel_id=1, source_target_pairs={{0,4},{1,5},{2,6},{3,7},{4,0},{5,1},{6,2},{7,3},{8,12},{9,13},{10,... | collective-permute-start | bytes 933896 | tf_op jit(solution)/shard_map/ppermute | solution.py:885
  66.0 11.1 %copy-start.3 = (s32[512]{0:T(512)S(1)}, s32[512]{0:T(512)}, u32[]{:S(2)}) copy-start(s32[512]{0:T(512)} %param.22) | copy-start | bytes 6148
  75.2 5.0 %collective-permute-start.3 = (f32[80,128]{1,0:T(8,128)S(1)}, f32[80,128]{1,0:T(8,128)S(1)}, u32[]{:S(2)}, u32[]{:S(2)}) collective-permute-start(f32[80,128]{1,0:T(8,128)S(1)} %get-tuple-element.40.refs_0_), channel_id=1, source_target_pairs={{1,0},{2,1},{3,2},{0,3},{5,4},{6,5},{7,6},{4,7},{9,8},{10,9},{11,1... | collective-permute-start | bytes 122888 | tf_op jit(solution)/shard_map/ppermute | solution.py:888
  75.3 4.9 %collective-permute-start.2 = (f32[80,128]{1,0:T(8,128)S(1)}, f32[80,128]{1,0:T(8,128)S(1)}, u32[]{:S(2)}, u32[]{:S(2)}) collective-permute-start(f32[80,128]{1,0:T(8,128)S(1)} %get-tuple-element.40.refs_0_), channel_id=1, source_target_pairs={{0,1},{1,2},{2,3},{3,0},{4,5},{5,6},{6,7},{7,4},{8,9},{9,10},{10,1... | collective-permute-start | bytes 122888 | tf_op jit(solution)/shard_map/ppermute | solution.py:888
  77.0 11.2 %collective-permute-start = (f32[152,512]{1,0:T(8,128)S(1)}, f32[152,512]{1,0:T(8,128)S(1)}, u32[]{:S(2)}, u32[]{:S(2)}) collective-permute-start(f32[152,512]{1,0:T(8,128)S(1)} %get-tuple-element.38), channel_id=1, source_target_pairs={{4,8},{5,9},{6,10},{7,11},{8,4},{9,5},{10,6},{11,7},{12,16},{13,17... | collective-permute-start | bytes 933896 | tf_op jit(solution)/shard_map/ppermute | solution.py:885
  84.4 4.5 %collective-permute-start.5 = (f32[80,128]{1,0:T(8,128)S(1)}, f32[80,128]{1,0:T(8,128)S(1)}, u32[]{:S(2)}, u32[]{:S(2)}) collective-permute-start(f32[80,128]{1,0:T(8,128)S(1)} %get-tuple-element.41), channel_id=1, source_target_pairs={{1,0},{2,1},{3,2},{0,3},{5,4},{6,5},{7,6},{4,7},{9,8},{10,9},{11,1... | collective-permute-start | bytes 122888 | tf_op jit(solution)/shard_map/ppermute | solution.py:888
  84.5 4.5 %collective-permute-start.4 = (f32[80,128]{1,0:T(8,128)S(1)}, f32[80,128]{1,0:T(8,128)S(1)}, u32[]{:S(2)}, u32[]{:S(2)}) collective-permute-start(f32[80,128]{1,0:T(8,128)S(1)} %get-tuple-element.41), channel_id=1, source_target_pairs={{0,1},{1,2},{2,3},{3,0},{4,5},{5,6},{6,7},{7,4},{8,9},{9,10},{10,1... | collective-permute-start | bytes 122888 | tf_op jit(solution)/shard_map/ppermute | solution.py:888
  86.2 9.4 %collective-permute-start.7 = (f32[152,512]{1,0:T(8,128)S(1)}, f32[152,512]{1,0:T(8,128)S(1)}, u32[]{:S(2)}, u32[]{:S(2)}) collective-permute-start(f32[152,512]{1,0:T(8,128)S(1)} %get-tuple-element.45), channel_id=1, source_target_pairs={{0,4},{1,5},{2,6},{3,7},{4,0},{5,1},{6,2},{7,3},{8,12},{9,13},{10,... | collective-permute-start | bytes 933896 | tf_op jit(solution)/shard_map/ppermute | solution.py:885
  92.4 11.8 %collective-permute-start.6 = (f32[152,512]{1,0:T(8,128)S(1)}, f32[152,512]{1,0:T(8,128)S(1)}, u32[]{:S(2)}, u32[]{:S(2)}) collective-permute-start(f32[152,512]{1,0:T(8,128)S(1)} %get-tuple-element.44), channel_id=1, source_target_pairs={{4,8},{5,9},{6,10},{7,11},{8,4},{9,5},{10,6},{11,7},{12,16},{13,17... | collective-permute-start | bytes 933896 | tf_op jit(solution)/shard_map/ppermute | solution.py:885
  99.3 4.9 %collective-permute-start.9 = (f32[80,128]{1,0:T(8,128)S(1)}, f32[80,128]{1,0:T(8,128)S(1)}, u32[]{:S(2)}, u32[]{:S(2)}) collective-permute-start(f32[80,128]{1,0:T(8,128)S(1)} %get-tuple-element.47), channel_id=1, source_target_pairs={{1,0},{2,1},{3,2},{0,3},{5,4},{6,5},{7,6},{4,7},{9,8},{10,9},{11,1... | collective-permute-start | bytes 122888 | tf_op jit(solution)/shard_map/ppermute | solution.py:888
  99.7 4.6 %collective-permute-start.8 = (f32[80,128]{1,0:T(8,128)S(1)}, f32[80,128]{1,0:T(8,128)S(1)}, u32[]{:S(2)}, u32[]{:S(2)}) collective-permute-start(f32[80,128]{1,0:T(8,128)S(1)} %get-tuple-element.47), channel_id=1, source_target_pairs={{0,1},{1,2},{2,3},{3,0},{4,5},{5,6},{6,7},{7,4},{8,9},{9,10},{10,1... | collective-permute-start | bytes 122888 | tf_op jit(solution)/shard_map/ppermute | solution.py:888
  101.1 11.6 %collective-permute-start.13 = (f32[152,512]{1,0:T(8,128)S(1)}, f32[152,512]{1,0:T(8,128)S(1)}, u32[]{:S(2)}, u32[]{:S(2)}) collective-permute-start(f32[152,512]{1,0:T(8,128)S(1)} %get-tuple-element.52), channel_id=1, source_target_pairs={{0,4},{1,5},{2,6},{3,7},{4,0},{5,1},{6,2},{7,3},{8,12},{9,13},{10,... | collective-permute-start | bytes 933896 | tf_op jit(solution)/shard_map/ppermute | solution.py:885
  107.8 4.9 %collective-permute-start.12 = (f32[80,128]{1,0:T(8,128)S(1)}, f32[80,128]{1,0:T(8,128)S(1)}, u32[]{:S(2)}, u32[]{:S(2)}) collective-permute-start(f32[80,128]{1,0:T(8,128)S(1)} %get-tuple-element.50), channel_id=1, source_target_pairs={{1,0},{2,1},{3,2},{0,3},{5,4},{6,5},{7,6},{4,7},{9,8},{10,9},{11,1... | collective-permute-start | bytes 122888 | tf_op jit(solution)/shard_map/ppermute | solution.py:888
  108.7 4.0 %collective-permute-start.11 = (f32[80,128]{1,0:T(8,128)S(1)}, f32[80,128]{1,0:T(8,128)S(1)}, u32[]{:S(2)}, u32[]{:S(2)}) collective-permute-start(f32[80,128]{1,0:T(8,128)S(1)} %get-tuple-element.50), channel_id=1, source_target_pairs={{0,1},{1,2},{2,3},{3,0},{4,5},{5,6},{6,7},{7,4},{8,9},{9,10},{10,1... | collective-permute-start | bytes 122888 | tf_op jit(solution)/shard_map/ppermute | solution.py:888
  109.6 12.1 %collective-permute-start.10 = (f32[152,512]{1,0:T(8,128)S(1)}, f32[152,512]{1,0:T(8,128)S(1)}, u32[]{:S(2)}, u32[]{:S(2)}) collective-permute-start(f32[152,512]{1,0:T(8,128)S(1)} %get-tuple-element.49), channel_id=1, source_target_pairs={{4,8},{5,9},{6,10},{7,11},{8,4},{9,5},{10,6},{11,7},{12,16},{13,17... | collective-permute-start | bytes 933896 | tf_op jit(solution)/shard_map/ppermute | solution.py:885

commit v5 on v3

--- a/solution.py
+++ b/solution.py
@@ -238,6 +238,7 @@
         return lax.shift_right_arithmetic(cell - 1, shift)
 
     sea = jnp.zeros((row_count, col_count), F32)
+    all_rows = []
     count = 0
     for index in range(devices // block):
         tails = [chunk(index, capacity + 8 * part).T for part in range(per_group)]
@@ -254,8 +255,7 @@
             hot_ref[count] = hot
             rows = rows_of(turned[75:76].astype(jnp.int32))
             rows_ref[count] = jnp.broadcast_to(rows, (8, members))
-            bound_ref[2 * count] = jnp.min(jnp.where(rows >= 0, rows, row_count))
-            bound_ref[2 * count + 1] = jnp.max(rows)
+            all_rows.append(rows.astype(F32))
             count += 1
             if octet >= alt_octets:
                 continue
@@ -266,6 +266,13 @@
             product = mm(jnp.concatenate([high, low], axis=0), alt_hot)
             sea = sea + product[:row_count] + product[row_count:]
     sea_ref[...] = sea
+    all_rows = jnp.concatenate(all_rows, axis=0)
+    least = jnp.where(all_rows >= 0.0, all_rows, float(row_count))
+    least = jnp.min(least, axis=1, keepdims=True).astype(jnp.int32)
+    most = jnp.max(all_rows, axis=1, keepdims=True).astype(jnp.int32)
+    for number in range(count):
+        bound_ref[2 * number] = least[number, 0]
+        bound_ref[2 * number + 1] = most[number, 0]
 
 
 def chosen_rows(number, here, row, span, left_ref, hot_ref):

time: 126 us -> 123 us (0.976)
  starting transfers between devices: 33.2 us -> 31 us
    ppermute x4, starting transfers between devices: 11 us -> 7.14 us  [pass_columns(): lax.ppermute(cols, 'ia', ring_west)]
    ppermute x6, waiting for transfers between devices: 0.92 us -> 3.86 us  [swap(): return lax.ppermute(edge, ('ja', 'ia'), swaps[which])]
    ppermute x4, waiting for transfers between devices: 2.61 us -> 0.34 us  [pass_columns(): lax.ppermute(cols, 'ia', ring_west)]
    ppermute x6, starting transfers between devices: 11.3 us -> 12.9 us  [swap(): return lax.ppermute(edge, ('ja', 'ia'), swaps[which])]
  transfers between devices with their start and end apart: 15 -> 15, of which waited for: 5 -> 5; matrix products, arithmetic and copies ran while one was open for 3% -> 3% of each run, Pallas kernels for 22% -> 23%
where the time goes in v5:
time: 123 us
  waiting for transfers between devices  44.3 us (36%)
  Pallas kernels  43.6 us (35%)
  starting transfers between devices  31 us (25%)
  local copies, waits for them, and re-layouts  2.04 us (2%)
  other arithmetic  1.29 us (1%)
    all_to_all x1, waiting for transfers between devices, body(): lax.all_to_all(message, ('ja', 'ia'), split_axis=0, concat_axis=0, tiled=...  39.4 us
    pallas_call x4, Pallas kernels, diffuse(): pl.pallas_call(kernel, in_specs=in_place(8 + len(far_cols)), out_shape=ha...  14.2 us
    ppermute x6, starting transfers between devices, swap(): return lax.ppermute(edge, ('ja', 'ia'), swaps[which])  12.9 us
    pallas_call x1, Pallas kernels, send_tables(): pl.pallas_call(kernel, grid=(devices // per_step,), in_specs=[whole(x) fo...  9.45 us
    ppermute x4, starting transfers between devices, pass_columns(): lax.ppermute(cols, 'ia', ring_west)  7.14 us
    pallas_call x1, Pallas kernels, last_inner(): pl.pallas_call(kernel, in_specs=in_place(13), out_specs=[pl.BlockSpec(mem...  6.73 us
    all_to_all x1, starting transfers between devices, body(): lax.all_to_all(message, ('ja', 'ia'), split_axis=0, concat_axis=0, tiled=...  6.31 us
    pallas_call x1, Pallas kernels, rest_forcing(): pl.pallas_call(kernel, in_specs=in_place(8) + [pl.BlockSpec(memory_space=...  5.7 us
  transfers between devices with their start and end apart: 15, of which 5 were waited for; matrix products, arithmetic and copies ran while one was open for 3% of the time, Pallas kernels for 23%

profile of v5, /device:TPU:13, one launch (start us, length us, event | category | flops | bytes accessed | tf_op | source)
XLA Modules:
  0.0 122.7 jit_solution(9992609205757982377)
XLA Ops:
  0.0 9.5 %send_tables.1 = f32[32,120,128]{2,1,0:T(8,128)} custom-call(f32[150,1024]{1,0:T(8,128)} %bitcast.11, s32[1,1024]{1,0:T(1,128)} %bitcast.12, s32[1,1024]{1,0:T(1,128)} %bitcast.13, f32[768]{0:T(1024)} %refs_3_.3, s32[768]{0:T(1024)} %refs_4_.1, s32[1,768]{1,0:T(1,128)} %bitcast.14), custom_call_target="tpu_custom_call" | custom-call | tf_op jit(solution)/shard_map/send_tables/pallas_call | solution.py:163
  9.5 0.0 copy-start.4
  9.5 6.3 %all-to-all-start = ((f32[32,120,128]{2,1,0:T(8,128)}), f32[32,120,128]{2,1,0:T(8,128)S(1)}, u32[]{:S(2)}, u32[]{:S(2)}) async-start(f32[32,120,128]{2,1,0:T(8,128)} %send_tables.1), calls=%async_computation | async-start | bytes 3932160 | tf_op jit(solution)/shard_map/all_to_all | solution.py:813
  15.8 0.0 copy-done.4
  15.8 0.1 reshape.19
  15.9 0.1 reshape.22.profile_ref
  16.0 1.7 %copy.17 = f32[16,2,75,75]{2,3,0,1:T(8,128)S(1)} copy(f32[16,2,75,75]{3,1,2,0:T(2,128)} %param.23) | data formatting | bytes 1440000 | tf_op args[11]
  17.8 0.1 pad.13.clone
  17.8 0.1 pad_add_fusion.flag_ref.refs_0_
  17.9 0.2 reduce-precision_convert_fusion
  18.1 0.0 copy-start
  18.2 0.0 copy-start.1
  18.2 0.0 copy-start.2
  18.2 0.9 maximum_maximum_fusion
  19.1 0.1 broadcast_select_fusion
  19.2 39.4 %all-to-all-done.message_ref = f32[32,120,128]{2,1,0:T(8,128)S(1)} async-done(((f32[32,120,128]{2,1,0:T(8,128)}), f32[32,120,128]{2,1,0:T(8,128)S(1)}, u32[]{:S(2)}, u32[]{:S(2)}) %all-to-all-start) | async-done | bytes 1966112 | tf_op jit(solution)/shard_map/all_to_all | solution.py:813
  58.6 0.0 copy-done
  58.6 0.0 copy-done.1
  58.6 0.0 copy-done.2
  58.6 3.5 %forcing_first.1 = (f32[152,512]{1,0:T(8,128)S(1)}, f32[16,512]{1,0:T(8,128)S(1)}, bf16[12,160,512]{2,1,0:T(8,128)(2,1)S(1)}, bf16[12,256,512]{2,1,0:T(8,128)(2,...) custom-call(s32[3]{0:T(128)S(1)} %pad_add_fusion.flag_ref.refs_0_, f32[32,120,128]{2,1,0:T(8,128)S(1)} %all-to-all-done.message_ref, ...), custom_call_target="tpu_custom_call" | custom-call | flops 6000000000 | bytes 8000000 | tf_op jit(solution)/shard_map/forcing_first/pallas_call | solution.py:378
  62.1 2.0 %collective-permute-start.1 = (f32[152,512]{1,0:T(8,128)S(1)}, f32[152,512]{1,0:T(8,128)S(1)}, u32[]{:S(2)}, u32[]{:S(2)}) collective-permute-start(f32[152,512]{1,0:T(8,128)S(1)} %get-tuple-element.39), channel_id=1, source_target_pairs={{0,4},{1,5},{2,6},{3,7},{4,0},{5,1},{6,2},{7,3},{8,12},{9,13},{10,... | collective-permute-start | bytes 933896 | tf_op jit(solution)/shard_map/ppermute | solution.py:849
  64.0 0.0 copy-start.3
  64.0 5.7 %forcing_rest.1 = (f32[16,160,512]{2,1,0:T(8,128)S(1)}, f32[152,512]{1,0:T(8,128)S(1)}, f32[80,128]{1,0:T(8,128)S(1)}) custom-call(s32[3]{0:T(128)S(1)} %pad_add_fusion.flag_ref.refs_0_, f32[160,1]{1,0:T(8,128)S(1)} %reshape.22.profile_ref, s32[16,512]{1,0:T(8,128)S(1)} %copy-done, f32[16,512]{1,0:T(8,128)S(1)} %copy-done.1, f32[16,512]{1,0:T(8,128)S(1)} %copy-done.2, ...), custom_call_target="tpu_custom_call" | custom-call | flops 6000000000 | bytes 8000000 | tf_op jit(solution)/shard_map/forcing_rest/pallas_call | solution.py:415
  69.8 0.1 collective-permute-start.3
  69.9 1.7 %collective-permute-start.2 = (f32[80,128]{1,0:T(8,128)S(1)}, f32[80,128]{1,0:T(8,128)S(1)}, u32[]{:S(2)}, u32[]{:S(2)}) collective-permute-start(f32[80,128]{1,0:T(8,128)S(1)} %get-tuple-element.40.refs_0_), channel_id=1, source_target_pairs={{0,1},{1,2},{2,3},{3,0},{4,5},{5,6},{6,7},{7,4},{8,9},{9,10},{10,1... | collective-permute-start | bytes 122888 | tf_op jit(solution)/shard_map/ppermute | solution.py:852
  71.6 0.0 copy-done.3
  71.6 2.9 %collective-permute-start = (f32[152,512]{1,0:T(8,128)S(1)}, f32[152,512]{1,0:T(8,128)S(1)}, u32[]{:S(2)}, u32[]{:S(2)}) collective-permute-start(f32[152,512]{1,0:T(8,128)S(1)} %get-tuple-element.38), channel_id=1, source_target_pairs={{4,8},{5,9},{6,10},{7,11},{8,4},{9,5},{10,6},{11,7},{12,16},{13,17... | collective-permute-start | bytes 933896 | tf_op jit(solution)/shard_map/ppermute | solution.py:849
  74.5 0.0 collective-permute-done.3.refs_6_.east_in
  74.5 0.7 collective-permute-done.2.refs_5_.west_in
  75.2 0.0 collective-permute-done.1.refs_4_.edge_in
  75.2 0.7 edge_weights.2.coef_ref.near_coef
  75.9 3.5 %diffusion_near.2 = (f32[8,160,512]{2,1,0:T(8,128)S(1)}, f32[152,512]{1,0:T(8,128)S(1)}, f32[80,128]{1,0:T(8,128)S(1)}) custom-call(s32[3]{0:T(128)S(1)} %pad_add_fusion.flag_ref.refs_0_, f32[16,160,512]{2,1,0:T(8,128)S(1)} %get-tuple-element.37.state_ref.other_ref, f32[16,160,512]{2,1,0:T(8,128)S(1)} %get-tuple-element.37.state_ref.other_ref, ...), custom_call_target="tpu_custom_call" | custom-call | flops 3000000000 | bytes 8000000 | tf_op jit(solution)/shard_map/diffusion_near/pallas_call | solution.py:616
  79.4 2.8 %collective-permute-start.5 = (f32[80,128]{1,0:T(8,128)S(1)}, f32[80,128]{1,0:T(8,128)S(1)}, u32[]{:S(2)}, u32[]{:S(2)}) collective-permute-start(f32[80,128]{1,0:T(8,128)S(1)} %get-tuple-element.41), channel_id=1, source_target_pairs={{1,0},{2,1},{3,2},{0,3},{5,4},{6,5},{7,6},{4,7},{9,8},{10,9},{11,1... | collective-permute-start | bytes 122888 | tf_op jit(solution)/shard_map/ppermute | solution.py:852
  82.2 0.0 collective-permute-start.4
  82.2 1.9 %collective-permute-start.7 = (f32[152,512]{1,0:T(8,128)S(1)}, f32[152,512]{1,0:T(8,128)S(1)}, u32[]{:S(2)}, u32[]{:S(2)}) collective-permute-start(f32[152,512]{1,0:T(8,128)S(1)} %get-tuple-element.45), channel_id=1, source_target_pairs={{0,4},{1,5},{2,6},{3,7},{4,0},{5,1},{6,2},{7,3},{8,12},{9,13},{10,... | collective-permute-start | bytes 933896 | tf_op jit(solution)/shard_map/ppermute | solution.py:849
  84.1 0.0 collective-permute-done.refs_4_.edge_in
  84.2 0.7 edge_weights.3.coef_ref.far_coef
  84.9 0.0 collective-permute-done.5.east_in
  84.9 0.0 collective-permute-done.4.west_in
  84.9 3.7 %diffusion_far.2 = (f32[8,160,512]{2,1,0:T(8,128)S(1)}, f32[152,512]{1,0:T(8,128)S(1)}, f32[80,128]{1,0:T(8,128)S(1)}) custom-call(s32[3]{0:T(128)S(1)} %pad_add_fusion.flag_ref.refs_0_, f32[16,160,512]{2,1,0:T(8,128)S(1)} %get-tuple-element.37.state_ref.other_ref, f32[16,160,512]{2,1,0:T(8,128)S(1)} %get-tuple-element.37.state_ref.other_ref, ...), custom_call_target="tpu_custom_call" | custom-call | flops 3000000000 | bytes 8000000 | tf_op jit(solution)/shard_map/diffusion_far/pallas_call | solution.py:616
  88.6 2.6 %collective-permute-start.6 = (f32[152,512]{1,0:T(8,128)S(1)}, f32[152,512]{1,0:T(8,128)S(1)}, u32[]{:S(2)}, u32[]{:S(2)}) collective-permute-start(f32[152,512]{1,0:T(8,128)S(1)} %get-tuple-element.44), channel_id=1, source_target_pairs={{4,8},{5,9},{6,10},{7,11},{8,4},{9,5},{10,6},{11,7},{12,16},{13,17... | collective-permute-start | bytes 933896 | tf_op jit(solution)/shard_map/ppermute | solution.py:849
  91.2 0.4 collective-permute-done.7.edge_in
  91.6 3.5 %diffusion_near.3 = (f32[8,160,512]{2,1,0:T(8,128)S(1)}, f32[152,512]{1,0:T(8,128)S(1)}, f32[80,128]{1,0:T(8,128)S(1)}) custom-call(s32[3]{0:T(128)S(1)} %pad_add_fusion.flag_ref.refs_0_, f32[8,160,512]{2,1,0:T(8,128)S(1)} %get-tuple-element.43.state_ref.other_ref, f32[8,160,512]{2,1,0:T(8,128)S(1)} %get-tuple-element.42.other_ref.state_ref, ...), custom_call_target="tpu_custom_call" | custom-call | flops 3000000000 | bytes 8000000 | tf_op jit(solution)/shard_map/diffusion_near/pallas_call | solution.py:616
  95.2 2.6 %collective-permute-start.9 = (f32[80,128]{1,0:T(8,128)S(1)}, f32[80,128]{1,0:T(8,128)S(1)}, u32[]{:S(2)}, u32[]{:S(2)}) collective-permute-start(f32[80,128]{1,0:T(8,128)S(1)} %get-tuple-element.47), channel_id=1, source_target_pairs={{1,0},{2,1},{3,2},{0,3},{5,4},{6,5},{7,6},{4,7},{9,8},{10,9},{11,1... | collective-permute-start | bytes 122888 | tf_op jit(solution)/shard_map/ppermute | solution.py:852
  97.8 0.1 collective-permute-start.8
  97.9 1.6 %collective-permute-start.13 = (f32[152,512]{1,0:T(8,128)S(1)}, f32[152,512]{1,0:T(8,128)S(1)}, u32[]{:S(2)}, u32[]{:S(2)}) collective-permute-start(f32[152,512]{1,0:T(8,128)S(1)} %get-tuple-element.52), channel_id=1, source_target_pairs={{0,4},{1,5},{2,6},{3,7},{4,0},{5,1},{6,2},{7,3},{8,12},{9,13},{10,... | collective-permute-start | bytes 933896 | tf_op jit(solution)/shard_map/ppermute | solution.py:849
  99.5 0.0 collective-permute-done.6.edge_in
  99.5 0.3 collective-permute-done.9.east_in.near_east
  99.8 0.0 collective-permute-done.8.west_in.near_west
  99.8 3.5 %diffusion_far.3 = (f32[8,160,512]{2,1,0:T(8,128)S(1)}, f32[152,512]{1,0:T(8,128)S(1)}, f32[80,128]{1,0:T(8,128)S(1)}) custom-call(s32[3]{0:T(128)S(1)} %pad_add_fusion.flag_ref.refs_0_, f32[8,160,512]{2,1,0:T(8,128)S(1)} %get-tuple-element.42.other_ref.state_ref, f32[8,160,512]{2,1,0:T(8,128)S(1)} %get-tuple-element.43.state_ref.other_ref, ...), custom_call_target="tpu_custom_call" | custom-call | flops 3000000000 | bytes 8000000 | tf_op jit(solution)/shard_map/diffusion_far/pallas_call | solution.py:616
  103.3 1.6 %collective-permute-start.12 = (f32[80,128]{1,0:T(8,128)S(1)}, f32[80,128]{1,0:T(8,128)S(1)}, u32[]{:S(2)}, u32[]{:S(2)}) collective-permute-start(f32[80,128]{1,0:T(8,128)S(1)} %get-tuple-element.50), channel_id=1, source_target_pairs={{1,0},{2,1},{3,2},{0,3},{5,4},{6,5},{7,6},{4,7},{9,8},{10,9},{11,1... | collective-permute-start | bytes 122888 | tf_op jit(solution)/shard_map/ppermute | solution.py:852
  104.9 2.9 %collective-permute-start.11 = (f32[80,128]{1,0:T(8,128)S(1)}, f32[80,128]{1,0:T(8,128)S(1)}, u32[]{:S(2)}, u32[]{:S(2)}) collective-permute-start(f32[80,128]{1,0:T(8,128)S(1)} %get-tuple-element.50), channel_id=1, source_target_pairs={{0,1},{1,2},{2,3},{3,0},{4,5},{5,6},{6,7},{7,4},{8,9},{9,10},{10,1... | collective-permute-start | bytes 122888 | tf_op jit(solution)/shard_map/ppermute | solution.py:852
  107.8 1.9 %collective-permute-start.10 = (f32[152,512]{1,0:T(8,128)S(1)}, f32[152,512]{1,0:T(8,128)S(1)}, u32[]{:S(2)}, u32[]{:S(2)}) collective-permute-start(f32[152,512]{1,0:T(8,128)S(1)} %get-tuple-element.49), channel_id=1, source_target_pairs={{4,8},{5,9},{6,10},{7,11},{8,4},{9,5},{10,6},{11,7},{12,16},{13,17... | collective-permute-start | bytes 933896 | tf_op jit(solution)/shard_map/ppermute | solution.py:849
  109.7 0.0 collective-permute-done.12.far_east.east_in
  109.7 0.0 collective-permute-done.11.far_west.west_in
  109.8 0.0 collective-permute-done.13.edge_in
  109.8 6.7 %last_inner.1 = (f32[150,16,512]{2,1,0:T(8,128)}, f32[2,75,8,512]{3,2,1,0:T(8,128)S(1)}) custom-call(s32[3]{0:T(128)S(1)} %pad_add_fusion.flag_ref.refs_0_, f32[8,160,512]{2,1,0:T(8,128)S(1)} %get-tuple-element.51.near_ref, f32[8,160,512]{2,1,0:T(8,128)S(1)} %get-tuple-element.48.far_ref, f32[152,512]{1,0:T(8,128)S(1)} %collective-permute-done.13.edge_in, ...), custom_call_target="tpu_custom_call" | custom-call | flops 6000000000 | bytes 16000000 | tf_op jit(solution)/shard_map/last_inner/pallas_call | solution.py:699
  116.5 3.4 %collective-permute-done.10.edge_in = f32[152,512]{1,0:T(8,128)S(1)} collective-permute-done((f32[152,512]{1,0:T(8,128)S(1)}, f32[152,512]{1,0:T(8,128)S(1)}, u32[]{:S(2)}, u32[]{:S(2)}) %collective-permute-start.10) | collective-permute-done | bytes 311328 | tf_op jit(solution)/shard_map/ppermute | solution.py:849
  119.9 2.6 %last_outer.1 = f32[150,16,512]{2,1,0:T(8,128)} custom-call(s32[3]{0:T(128)S(1)} %pad_add_fusion.flag_ref.refs_0_, f32[8,160,512]{2,1,0:T(8,128)S(1)} %get-tuple-element.48.far_ref, f32[152,512]{1,0:T(8,128)S(1)} %collective-permute-done.10.edge_in, f32[80,128]{1,0:T(8,128)S(1)} %collective-permute-done.11.far_west.west_in, ...), custom_call_target="tpu_custom_call", output_to_operand_aliasing={{}: (10, {})} | custom-call | tf_op jit(solution)/shard_map/last_outer/pallas_call | solution.py:750
  (4 shorter events, 0.0 us)
Async XLA Ops:
  9.5 6.3 %copy-start.4 = (f32[150]{0:T(256)S(1)}, f32[150]{0:T(256)}, u32[]{:S(2)}) copy-start(f32[150]{0:T(256)} %param.18) | copy-start | bytes 1804
  9.5 49.1 %all-to-all-start = ((f32[32,120,128]{2,1,0:T(8,128)}), f32[32,120,128]{2,1,0:T(8,128)S(1)}, u32[]{:S(2)}, u32[]{:S(2)}) async-start(f32[32,120,128]{2,1,0:T(8,128)} %send_tables.1), calls=%async_computation | async-start | bytes 3932160 | tf_op jit(solution)/shard_map/all_to_all | solution.py:813
  18.1 40.4 %copy-start = (s32[16,512]{1,0:T(8,128)S(1)}, s32[16,512]{1,0:T(8,128)}, u32[]{:S(2)}) copy-start(s32[16,512]{1,0:T(8,128)} %mask_ref.3) | copy-start | bytes 98308
  18.2 40.4 %copy-start.1 = (f32[16,512]{1,0:T(8,128)S(1)}, f32[16,512]{1,0:T(8,128)}, u32[]{:S(2)}) copy-start(f32[16,512]{1,0:T(8,128)} %refs_2_.3) | copy-start | bytes 98308
  18.2 40.4 %copy-start.2 = (f32[16,512]{1,0:T(8,128)S(1)}, f32[16,512]{1,0:T(8,128)}, u32[]{:S(2)}) copy-start(f32[16,512]{1,0:T(8,128)} %refs_3_.5) | copy-start | bytes 98308
  62.1 13.2 %collective-permute-start.1 = (f32[152,512]{1,0:T(8,128)S(1)}, f32[152,512]{1,0:T(8,128)S(1)}, u32[]{:S(2)}, u32[]{:S(2)}) collective-permute-start(f32[152,512]{1,0:T(8,128)S(1)} %get-tuple-element.39), channel_id=1, source_target_pairs={{0,4},{1,5},{2,6},{3,7},{4,0},{5,1},{6,2},{7,3},{8,12},{9,13},{10,... | collective-permute-start | bytes 933896 | tf_op jit(solution)/shard_map/ppermute | solution.py:849
  64.0 7.5 %copy-start.3 = (s32[512]{0:T(512)S(1)}, s32[512]{0:T(512)}, u32[]{:S(2)}) copy-start(s32[512]{0:T(512)} %param.22) | copy-start | bytes 6148
  69.8 4.7 %collective-permute-start.3 = (f32[80,128]{1,0:T(8,128)S(1)}, f32[80,128]{1,0:T(8,128)S(1)}, u32[]{:S(2)}, u32[]{:S(2)}) collective-permute-start(f32[80,128]{1,0:T(8,128)S(1)} %get-tuple-element.40.refs_0_), channel_id=1, source_target_pairs={{1,0},{2,1},{3,2},{0,3},{5,4},{6,5},{7,6},{4,7},{9,8},{10,9},{11,1... | collective-permute-start | bytes 122888 | tf_op jit(solution)/shard_map/ppermute | solution.py:852
  69.9 5.3 %collective-permute-start.2 = (f32[80,128]{1,0:T(8,128)S(1)}, f32[80,128]{1,0:T(8,128)S(1)}, u32[]{:S(2)}, u32[]{:S(2)}) collective-permute-start(f32[80,128]{1,0:T(8,128)S(1)} %get-tuple-element.40.refs_0_), channel_id=1, source_target_pairs={{0,1},{1,2},{2,3},{3,0},{4,5},{5,6},{6,7},{7,4},{8,9},{9,10},{10,1... | collective-permute-start | bytes 122888 | tf_op jit(solution)/shard_map/ppermute | solution.py:852
  71.6 12.6 %collective-permute-start = (f32[152,512]{1,0:T(8,128)S(1)}, f32[152,512]{1,0:T(8,128)S(1)}, u32[]{:S(2)}, u32[]{:S(2)}) collective-permute-start(f32[152,512]{1,0:T(8,128)S(1)} %get-tuple-element.38), channel_id=1, source_target_pairs={{4,8},{5,9},{6,10},{7,11},{8,4},{9,5},{10,6},{11,7},{12,16},{13,17... | collective-permute-start | bytes 933896 | tf_op jit(solution)/shard_map/ppermute | solution.py:849
  79.4 5.4 %collective-permute-start.5 = (f32[80,128]{1,0:T(8,128)S(1)}, f32[80,128]{1,0:T(8,128)S(1)}, u32[]{:S(2)}, u32[]{:S(2)}) collective-permute-start(f32[80,128]{1,0:T(8,128)S(1)} %get-tuple-element.41), channel_id=1, source_target_pairs={{1,0},{2,1},{3,2},{0,3},{5,4},{6,5},{7,6},{4,7},{9,8},{10,9},{11,1... | collective-permute-start | bytes 122888 | tf_op jit(solution)/shard_map/ppermute | solution.py:852
  82.2 2.7 %collective-permute-start.4 = (f32[80,128]{1,0:T(8,128)S(1)}, f32[80,128]{1,0:T(8,128)S(1)}, u32[]{:S(2)}, u32[]{:S(2)}) collective-permute-start(f32[80,128]{1,0:T(8,128)S(1)} %get-tuple-element.41), channel_id=1, source_target_pairs={{0,1},{1,2},{2,3},{3,0},{4,5},{5,6},{6,7},{7,4},{8,9},{9,10},{10,1... | collective-permute-start | bytes 122888 | tf_op jit(solution)/shard_map/ppermute | solution.py:852
  82.2 9.4 %collective-permute-start.7 = (f32[152,512]{1,0:T(8,128)S(1)}, f32[152,512]{1,0:T(8,128)S(1)}, u32[]{:S(2)}, u32[]{:S(2)}) collective-permute-start(f32[152,512]{1,0:T(8,128)S(1)} %get-tuple-element.45), channel_id=1, source_target_pairs={{0,4},{1,5},{2,6},{3,7},{4,0},{5,1},{6,2},{7,3},{8,12},{9,13},{10,... | collective-permute-start | bytes 933896 | tf_op jit(solution)/shard_map/ppermute | solution.py:849
  88.6 10.9 %collective-permute-start.6 = (f32[152,512]{1,0:T(8,128)S(1)}, f32[152,512]{1,0:T(8,128)S(1)}, u32[]{:S(2)}, u32[]{:S(2)}) collective-permute-start(f32[152,512]{1,0:T(8,128)S(1)} %get-tuple-element.44), channel_id=1, source_target_pairs={{4,8},{5,9},{6,10},{7,11},{8,4},{9,5},{10,6},{11,7},{12,16},{13,17... | collective-permute-start | bytes 933896 | tf_op jit(solution)/shard_map/ppermute | solution.py:849
  95.2 4.6 %collective-permute-start.9 = (f32[80,128]{1,0:T(8,128)S(1)}, f32[80,128]{1,0:T(8,128)S(1)}, u32[]{:S(2)}, u32[]{:S(2)}) collective-permute-start(f32[80,128]{1,0:T(8,128)S(1)} %get-tuple-element.47), channel_id=1, source_target_pairs={{1,0},{2,1},{3,2},{0,3},{5,4},{6,5},{7,6},{4,7},{9,8},{10,9},{11,1... | collective-permute-start | bytes 122888 | tf_op jit(solution)/shard_map/ppermute | solution.py:852
  97.8 2.0 %collective-permute-start.8 = (f32[80,128]{1,0:T(8,128)S(1)}, f32[80,128]{1,0:T(8,128)S(1)}, u32[]{:S(2)}, u32[]{:S(2)}) collective-permute-start(f32[80,128]{1,0:T(8,128)S(1)} %get-tuple-element.47), channel_id=1, source_target_pairs={{0,1},{1,2},{2,3},{3,0},{4,5},{5,6},{6,7},{7,4},{8,9},{9,10},{10,1... | collective-permute-start | bytes 122888 | tf_op jit(solution)/shard_map/ppermute | solution.py:852
  97.9 11.9 %collective-permute-start.13 = (f32[152,512]{1,0:T(8,128)S(1)}, f32[152,512]{1,0:T(8,128)S(1)}, u32[]{:S(2)}, u32[]{:S(2)}) collective-permute-start(f32[152,512]{1,0:T(8,128)S(1)} %get-tuple-element.52), channel_id=1, source_target_pairs={{0,4},{1,5},{2,6},{3,7},{4,0},{5,1},{6,2},{7,3},{8,12},{9,13},{10,... | collective-permute-start | bytes 933896 | tf_op jit(solution)/shard_map/ppermute | solution.py:849
  103.3 6.4 %collective-permute-start.12 = (f32[80,128]{1,0:T(8,128)S(1)}, f32[80,128]{1,0:T(8,128)S(1)}, u32[]{:S(2)}, u32[]{:S(2)}) collective-permute-start(f32[80,128]{1,0:T(8,128)S(1)} %get-tuple-element.50), channel_id=1, source_target_pairs={{1,0},{2,1},{3,2},{0,3},{5,4},{6,5},{7,6},{4,7},{9,8},{10,9},{11,1... | collective-permute-start | bytes 122888 | tf_op jit(solution)/shard_map/ppermute | solution.py:852
  104.9 4.8 %collective-permute-start.11 = (f32[80,128]{1,0:T(8,128)S(1)}, f32[80,128]{1,0:T(8,128)S(1)}, u32[]{:S(2)}, u32[]{:S(2)}) collective-permute-start(f32[80,128]{1,0:T(8,128)S(1)} %get-tuple-element.50), channel_id=1, source_target_pairs={{0,1},{1,2},{2,3},{3,0},{4,5},{5,6},{6,7},{7,4},{8,9},{9,10},{10,1... | collective-permute-start | bytes 122888 | tf_op jit(solution)/shard_map/ppermute | solution.py:852
  107.8 12.1 %collective-permute-start.10 = (f32[152,512]{1,0:T(8,128)S(1)}, f32[152,512]{1,0:T(8,128)S(1)}, u32[]{:S(2)}, u32[]{:S(2)}) collective-permute-start(f32[152,512]{1,0:T(8,128)S(1)} %get-tuple-element.49), channel_id=1, source_target_pairs={{4,8},{5,9},{6,10},{7,11},{8,4},{9,5},{10,6},{11,7},{12,16},{13,17... | collective-permute-start | bytes 933896 | tf_op jit(solution)/shard_map/ppermute | solution.py:849
